TPU v7x, 32 devices: a whole 2x2x4 slice. The times are simulated.
32 devices in a mesh: band: 8 (over z, y), lev: 4 (over x, core).
Axes of the slice: x: 2, y: 2, z: 4, core: 2. Of those that a mesh axis runs over, the one named last changes fastest.
Arguments:
- spectra: bfloat16 [1280, 2, 120, 1280], P('band', None, 'lev'), may hold values from -6 to 6
- legendre: bfloat16 [1280, 1280, 16], P('band'), may hold values from -0.15625 to 0.15625
- slot_wave: int32 [1280], replicated, may hold values from -1 to 1279, as said below
- row_points: int32 [16], replicated, may hold values from 20 to 5136, as said below
- gauss_weight: float32 [16], replicated, may hold values from 0.5 to 2
- layer_depth: float32 [24], replicated, may hold values from 0.1 to 1
- mode_speed: float32 [120], P('lev'), may hold values from 0.5 to 8
Outputs:
- advanced: float32 [1280, 2, 120, 1280], P('band', None, 'lev')
Inputs may be any that keep to these rules, and one draw needn't show every extreme that they name: `slot_wave`: every wavenumber 0 to 1279 stands in exactly one slot. Slots 2k and 2k + 1 of one index of band hold a pair m and 1279 - m, or are both empty. `row_points`: rows 2k and 2k + 1 have 20 + 4 i and 20 + 4 (1279 - i) points for some i in 0 to 1279, in either order, so that together they have 4 * 1279 + 40 points.
All inputs are finite; a program needn't handle non-finite values.
Results may differ from a plain program's by a relative error of at most 0.0043.
Values may be sent and summed in bfloat16 or wider, within the bound.
No kernel may reach another device: no remote copies, remote signals or barrier semaphores. Data moves between devices by JAX's collectives and lax.ppermute only.
A program may use at most 192 MiB of HBM per device.

v0:
```python
import math

import jax
import jax.numpy as jnp
from jax import lax
from jax.sharding import PartitionSpec as P

TRUNC = 1279
FIELDS = 5
LEVELS = 24
NDEG = 1280
PAIR_PTS = 5248


precise = lax.Precision.HIGHEST
time_step = 1.0


def make_basis(wave_table, row_len, column, inside):
    wave_num = jnp.maximum(wave_table, 0)[:, None]
    residue = wave_num * column[None, :] % row_len[None, :]
    row_float = row_len.astype(jnp.float32)[None, :]
    phase_angle = residue.astype(jnp.float32) * (2.0 * math.pi / row_float)
    active = (
        (wave_table[:, None] >= 0)
        & (2 * wave_table[:, None] <= row_len[None, :] - 1)
        & inside[None, :]
    )
    norm_scale = jnp.where(active, 1.0 / jnp.sqrt(row_float), jnp.zeros((), jnp.float32))
    return jnp.stack(
        [jnp.cos(phase_angle) * norm_scale, -jnp.sin(phase_angle) * norm_scale]
    ).astype(jnp.bfloat16)


def grid_terms(grid_vals, layer_depth):
    width = grid_vals.shape[1]
    stacked = grid_vals.reshape(FIELDS, LEVELS, width)
    wind_u = stacked[0]
    wind_v = stacked[1]
    temper = stacked[2]
    humid = stacked[3]
    ozone_mix = stacked[4]
    level_ids = jnp.arange(LEVELS, dtype=jnp.int32)
    tri_ones = (level_ids[None, :] >= level_ids[:, None]).astype(jnp.float32) * layer_depth[None, :]
    geopotential = jnp.dot(tri_ones, temper, precision=precise)
    energy = 0.5 * (wind_u * wind_u + wind_v * wind_v) + geopotential
    outputs = jnp.stack(
        [wind_u * temper, wind_v * temper, wind_u * humid, wind_v * ozone_mix, energy]
    )
    return outputs.reshape(FIELDS * LEVELS, width).astype(jnp.bfloat16)


def shards(spectra, legendre, slot_wave, row_points, gauss_weight, layer_depth, mode_speed):
    slot_count = spectra.shape[0]
    field_local = spectra.shape[2]
    band_count = lax.axis_size("band")
    group_count = lax.axis_size("lev")
    band_index = lax.axis_index("band")
    lev_index = lax.axis_index("lev")
    lat_count = legendre.shape[2]
    lat_local = lat_count // band_count
    all_slots = slot_wave.shape[0]
    local_wave = lax.dynamic_slice_in_dim(slot_wave, band_index * slot_count, slot_count)
    degree = jnp.arange(NDEG, dtype=jnp.int32)
    live_mask = (local_wave[:, None] >= 0) & (degree[None, :] >= local_wave[:, None])
    masked = jnp.where(live_mask[:, None, None, :], spectra, jnp.zeros((), spectra.dtype))
    received = []
    for component in range(2):
        product = jnp.einsum(
            "sfn,snr->rsf", masked[:, component], legendre, preferred_element_type=jnp.float32
        ).astype(jnp.bfloat16)
        sent = product.reshape(lat_count, 1, slot_count * field_local)
        arrived = lax.all_to_all(sent, "band", split_axis=0, concat_axis=1, tiled=True)
        received.append(arrived.reshape(lat_local, all_slots, field_local))
    by_rows = jnp.stack(received, axis=2)
    own_points = lax.dynamic_slice_in_dim(row_points, band_index * lat_local, lat_local)
    own_weight = lax.dynamic_slice_in_dim(gauss_weight, band_index * lat_local, lat_local)
    tile_len = PAIR_PTS // group_count
    weight_mult = (jnp.where(slot_wave == 0, 1.0, 2.0) * (slot_wave >= 0)).astype(jnp.bfloat16)
    position = lev_index * tile_len + jnp.arange(tile_len, dtype=jnp.int32)
    geometry_second_row = position >= own_points[0]
    column = position - jnp.where(geometry_second_row, own_points[0], 0)
    row_len = jnp.where(geometry_second_row, own_points[1], own_points[0])
    inside = column < row_len
    basis_table = make_basis(slot_wave, row_len, column, inside)
    coeffs = lax.all_gather(by_rows, "lev", axis=3, tiled=True) * weight_mult[None, :, None, None]
    first_part = jnp.einsum(
        "scf,csp->fp", coeffs[0], basis_table, preferred_element_type=jnp.float32
    )
    second_part = jnp.einsum(
        "scf,csp->fp", coeffs[1], basis_table, preferred_element_type=jnp.float32
    )
    grid_vals = jnp.where(geometry_second_row[None, :], second_part, first_part)
    tendency = grid_terms(grid_vals, layer_depth)
    zeros_like = jnp.zeros((), jnp.bfloat16)
    first_part = jnp.einsum(
        "fp,csp->fsc",
        jnp.where(geometry_second_row[None, :], zeros_like, tendency),
        basis_table,
        preferred_element_type=jnp.float32,
    )
    second_part = jnp.einsum(
        "fp,csp->fsc",
        jnp.where(geometry_second_row[None, :], tendency, zeros_like),
        basis_table,
        preferred_element_type=jnp.float32,
    )
    summed = lax.psum_scatter(
        jnp.stack([first_part, second_part], axis=1), "lev", scatter_dimension=0, tiled=True
    )
    weighted = (summed * own_weight[None, :, None, None]).astype(jnp.bfloat16)
    sent_back = weighted.reshape(field_local, lat_local, band_count, slot_count * 2)
    arrived_back = lax.all_to_all(sent_back, "band", split_axis=2, concat_axis=1, tiled=True)
    by_waves = arrived_back.reshape(field_local, lat_count, slot_count, 2)
    tendency_spec = jnp.einsum(
        "frsc,snr->scfn", by_waves, legendre, preferred_element_type=jnp.float32
    )
    helm_factor = (degree * (degree + 1)).astype(jnp.float32) / float(TRUNC * (TRUNC + 1))
    denominator = (
        1.0
        + time_step * time_step * helm_factor[None, None, None, :] * mode_speed[None, None, :, None]
    )
    advanced = (masked.astype(jnp.float32) + time_step * tendency_spec) / denominator
    return jnp.where(live_mask[:, None, None, :], advanced, jnp.zeros((), jnp.float32))


def solution(mesh):
    return jax.shard_map(
        shards,
        mesh=mesh,
        in_specs=(
            P("band", None, "lev", None),
            P("band", None, None),
            P(),
            P(),
            P(),
            P(),
            P("lev"),
        ),
        out_specs=P("band", None, "lev", None),
        check_vma=False,
    )
```

profile of v0, /device:TPU:0, one launch (start us, length us, event | category | flops | bytes accessed | tf_op | source)
XLA Modules:
  0.0 405.7 jit_solution(11083833899849859011)
XLA Ops:
  6.5 0.8 broadcast_compare_fusion.2
  7.3 0.2 fusion.22
  7.6 18.1 %copy_select_fusion = bf16[160,2,30,1280]{3,2,0,1:T(8,128)(2,1)} fusion(bf16[160,2,30,1280]{3,1,2,0:T(2,128)(2,1)} %param.7, pred[160,1280]{1,0:T(8,128)(4,1)S(1)} %fusion.22), kind=kLoop, calls=%fused_computation.3 | loop fusion | flops 12288000 | bytes 49356800 | tf_op jit(solution)/shard_map/jit(_where)/select_n | solution.py:66
  25.7 0.0 copy-start.5
  25.7 8.8 %fusion.20 = bf16[16,160,30]{2,0,1:T(8,128)(2,1)S(1)} fusion(bf16[160,1280,16]{1,2,0:T(8,128)(2,1)} %param.8, bf16[160,2,30,1280]{3,2,0,1:T(8,128)(2,1)} %copy_select_fusion), kind=kOutput, calls=%fused_computation.37 | convolution fusion | flops 196684800 | bytes 19814400 | tf_op jit(solution)/shard_map/sfn,snr->rsf/dot_general | solution.py:69
  34.5 0.2 copy.123
  34.7 1.4 reshape.646
  36.1 0.5 broadcast.668
  36.6 1.5 reduce.2
  38.2 0.7 reshape.650
  38.9 7.3 %all-to-all-start.1 = ((bf16[8,2,4800]{2,1,0:T(2,128)(2,1)}), bf16[8,2,4800]{2,1,0:T(2,128)(2,1)S(1)}, u32[]{:S(2)}, u32[]{:S(2)}) async-start(bf16[8,2,4800]{2,1,0:T(2,128)(2,1)} %reshape.650), calls=%async_computation.1 | async-start | bytes 311296 | tf_op jit(solution)/shard_map/all_to_all | solution.py:73
  46.2 0.1 dynamic_slice.10
  46.3 0.6 fusion.46
  46.9 0.7 select_subtract_fusion
  47.6 1.3 compare_select_fusion
  48.8 1.3 fusion.38
  50.1 8.9 %fusion.21 = bf16[16,160,30]{2,0,1:T(8,128)(2,1)S(1)} fusion(bf16[160,1280,16]{1,2,0:T(8,128)(2,1)} %param.8, bf16[160,2,30,1280]{3,2,0,1:T(8,128)(2,1)} %copy_select_fusion), kind=kOutput, calls=%fused_computation.38 | convolution fusion | flops 196684800 | bytes 19814400 | tf_op jit(solution)/shard_map/sfn,snr->rsf/dot_general | solution.py:69
  59.0 1.3 select_compare_fusion
  60.3 0.2 copy.120
  60.4 1.4 reshape.645
  61.8 1.5 reduce.3
  63.4 0.7 reshape.652
  64.1 6.0 %all-to-all-start = ((bf16[8,2,4800]{2,1,0:T(2,128)(2,1)}), bf16[8,2,4800]{2,1,0:T(2,128)(2,1)S(1)}, u32[]{:S(2)}, u32[]{:S(2)}) async-start(bf16[8,2,4800]{2,1,0:T(2,128)(2,1)} %reshape.652), calls=%async_computation | async-start | bytes 311296 | tf_op jit(solution)/shard_map/all_to_all | solution.py:73
  70.1 0.4 all-gather.2.cloned.1.call-start
  70.5 0.7 fusion.42
  71.2 0.1 reshape.651
  71.4 0.9 reduce.1
  72.3 0.1 all_to_all.37
  72.4 5.2 %all-to-all-done = bf16[8,2,4800]{2,1,0:T(2,128)(2,1)S(1)} async-done(((bf16[8,2,4800]{2,1,0:T(2,128)(2,1)}), bf16[8,2,4800]{2,1,0:T(2,128)(2,1)S(1)}, u32[]{:S(2)}, u32[]{:S(2)}) %all-to-all-start) | async-done | bytes 153632 | tf_op jit(solution)/shard_map/all_to_all | solution.py:73
  77.6 0.1 reshape.653
  77.7 0.9 reduce
  78.7 0.1 all_to_all.34
  78.8 1.5 stack_reshape.6
  80.3 1.5 stack_reshape.7
  81.8 0.3 pad_maximum_fusion.2
  82.1 1.3 copy.126
  83.5 0.0 all-gather.2.cloned.1.call-update
  83.5 0.0 all-reduce.3.cloned.1.call-start
  83.6 110.1 %fusion.4 = (bf16[1,1280,1312]{1,2,0:T(8,128)(2,1)S(1)}, bf16[1,1280,1312]{1,2,0:T(8,128)(2,1)}) fusion(f32[1312]{0:T(1024)S(1)} %get-tuple-element.19, s32[1280]{0:T(1024)S(1)} %get-tuple-element.12, f32[1312]{0:T(1024)S(1)} %get-tuple-element.20, s32[1312]{0:T(1024)S(1)} %get-tuple-element.15, s32[1312]{0:T(1024)S(1)} %select_subtract_fusion, ...), kind=kLoop, calls=%fused_computation.11 | loop fusion | flops 31907840 | bytes 6757824 | tf_op jit(solution)/shard_map/convert.10
  193.7 0.0 all-gather.2.cloned.1.call-done
  193.7 1.5 copy_multiply_fusion
  195.2 4.5 %convolution_bitcast_fusion.3 = f32[120,1312]{1,0:T(8,128)S(1)} fusion(bf16[2,1280,2,120]{1,3,2,0:T(8,128)(2,1)S(1)} %copy_multiply_fusion, bf16[1,1280,1312]{1,2,0:T(8,128)(2,1)} %get-tuple-element.10, bf16[1,1280,1312]{1,2,0:T(8,128)(2,1)S(1)} %get-tuple-element.9), kind=kOutput, calls=%fused_computation.28 | convolution fusion | flops 809451520 | bytes 7961600 | tf_op jit(solution)/shard_map/scf,csp->fp/dot_general | solution.py:90
  199.7 0.0 copy-start.6
  199.7 2.4 fusion.13
  202.2 0.3 fusion.16
  202.5 0.1 bitcast_select_fusion.1
  202.6 1.9 convolution_bitcast_fusion.1
  204.6 1.9 convolution_bitcast_fusion
  206.5 0.0 copy-start.8
  206.5 0.2 pad_maximum_fusion.1
  206.7 2.7 copy.132
  209.4 0.0 all-reduce.3.cloned.1.call-update
  209.5 0.1 dynamic_slice.11
  209.6 0.6 dynamic-slice
  210.8 53.9 %all-reduce.3.cloned.1.call-done = f32[120,2,1280,2]{2,3,1,0:T(2,128)} async-done(((f32[120,2,1280,2]{2,3,1,0:T(2,128)}), f32[120,2,1280,2]{2,3,1,0:T(2,128)}) %all-reduce.3.cloned.1.call-update) | async-done | bytes 2457616
  264.7 1.3 fusion.23
  266.1 1.2 copy.133
  267.3 1.4 copy.134
  268.7 5.7 %all-to-all-start.2 = ((bf16[30,2,8,320]{3,1,0,2:T(2,128)(2,1)}), bf16[30,2,8,320]{3,1,0,2:T(2,128)(2,1)S(1)}, u32[]{:S(2)}, u32[]{:S(2)}) async-start(bf16[30,2,8,320]{3,1,0,2:T(2,128)(2,1)} %copy.134), calls=%async_computation.2 | async-start | bytes 737280 | tf_op jit(solution)/shard_map/all_to_all | solution.py:113
  274.5 0.1 multiply_add_fusion
  274.6 10.9 %all-to-all-done.2 = bf16[30,2,8,320]{3,1,0,2:T(2,128)(2,1)S(1)} async-done(((bf16[30,2,8,320]{3,1,0,2:T(2,128)(2,1)}), bf16[30,2,8,320]{3,1,0,2:T(2,128)(2,1)S(1)}, u32[]{:S(2)}, u32[]{:S(2)}) %all-to-all-start.2) | async-done | bytes 307232 | tf_op jit(solution)/shard_map/all_to_all | solution.py:113
  285.5 0.9 copy.135
  286.5 31.5 %fusion.1 = f32[160,2,30,1280]{3,2,0,1:T(8,128)} fusion(f32[30,1280]{1,0:T(8,128)S(1)} %multiply_add_fusion, pred[160,1280]{1,0:T(8,128)(4,1)S(1)} %copy-done.2, bf16[160,1280,16]{1,2,0:T(8,128)(2,1)} %param.8, bf16[30,16,160,2]{0,3,2,1:T(2,128)(2,1)S(1)} %bitcast.98, bf16[160,2,30,1280]{3,1,2,0:T(2,128)(2,1)} %param.7), kind=kOutput, calls=%fused_computation.2 | convolution fusion | flops 454656000 | bytes 80947200 | tf_op jit(solution)/shard_map/frsc,snr->scfn/dot_general | solution.py:115
  317.9 80.7 %copy.137 = f32[160,2,30,1280]{3,1,2,0:T(2,128)} copy(f32[160,2,30,1280]{3,2,0,1:T(8,128)} %fusion.1) | data formatting | bytes 98304000 | tf_op jit(solution)/shard_map/jit(_where)/select_n | solution.py:124
  (26 shorter events, 0.2 us)
Async XLA Ops:
  7.6 18.1 %copy-start.1 = (pred[160,1280]{1,0:T(8,128)(4,1)}, pred[160,1280]{1,0:T(8,128)(4,1)S(1)}, u32[]{:S(2)}) copy-start(pred[160,1280]{1,0:T(8,128)(4,1)S(1)} %fusion.22) | copy-start | bytes 614404
  25.7 20.5 %copy-start.3 = (s32[1280]{0:T(1024)S(1)}, s32[1280]{0:T(1024)}, u32[]{:S(2)}) copy-start(s32[1280]{0:T(1024)} %param.9) | copy-start | bytes 15364
  25.7 20.5 %copy-start.5 = (s32[16]{0:T(128)S(1)}, s32[16]{0:T(128)}, u32[]{:S(2)}) copy-start(s32[16]{0:T(128)} %param.10) | copy-start | bytes 196
  38.9 25.2 %all-to-all-start.1 = ((bf16[8,2,4800]{2,1,0:T(2,128)(2,1)}), bf16[8,2,4800]{2,1,0:T(2,128)(2,1)S(1)}, u32[]{:S(2)}, u32[]{:S(2)}) async-start(bf16[8,2,4800]{2,1,0:T(2,128)(2,1)} %reshape.650), calls=%async_computation.1 | async-start | bytes 311296 | tf_op jit(solution)/shard_map/all_to_all | solution.py:73
  64.1 13.5 %all-to-all-start = ((bf16[8,2,4800]{2,1,0:T(2,128)(2,1)}), bf16[8,2,4800]{2,1,0:T(2,128)(2,1)S(1)}, u32[]{:S(2)}, u32[]{:S(2)}) async-start(bf16[8,2,4800]{2,1,0:T(2,128)(2,1)} %reshape.652), calls=%async_computation | async-start | bytes 311296 | tf_op jit(solution)/shard_map/all_to_all | solution.py:73
  70.1 123.6 %all-gather.2.cloned.1.call-start = ((), (), s32[]{:S(2)}) async-start(), calls=%async_computation.3 | async-start | bytes 1536000 | tf_op jit(solution)/shard_map/all_gather | solution.py:86
  83.5 181.2 %all-reduce.3.cloned.1.call-start = ((), (), s32[]{:S(2)}) async-start(), calls=%async_computation.4 | async-start | bytes 4915200
  195.2 4.5 %copy-start = (bf16[1,1280,1312]{1,2,0:T(8,128)(2,1)S(1)}, bf16[1,1280,1312]{1,2,0:T(8,128)(2,1)}, u32[]{:S(2)}) copy-start(bf16[1,1280,1312]{1,2,0:T(8,128)(2,1)} %get-tuple-element.10) | copy-start | bytes 10076164
  199.7 2.5 copy-start.6
  206.5 3.0 copy-start.7
  206.5 3.1 copy-start.8
  206.7 67.8 %copy-start.4 = (f32[30]{0:T(128)S(1)}, f32[30]{0:T(128)}, u32[]{:S(2)}) copy-start(f32[30]{0:T(128)} %param.13) | copy-start | bytes 364
  206.7 79.7 %copy-start.2 = (pred[160,1280]{1,0:T(8,128)(4,1)S(1)}, pred[160,1280]{1,0:T(8,128)(4,1)}, u32[]{:S(2)}) copy-start(pred[160,1280]{1,0:T(8,128)(4,1)} %copy-done.1) | copy-start | bytes 614404
  268.7 16.8 %all-to-all-start.2 = ((bf16[30,2,8,320]{3,1,0,2:T(2,128)(2,1)}), bf16[30,2,8,320]{3,1,0,2:T(2,128)(2,1)S(1)}, u32[]{:S(2)}, u32[]{:S(2)}) async-start(bf16[30,2,8,320]{3,1,0,2:T(2,128)(2,1)} %copy.134), calls=%async_computation.2 | async-start | bytes 737280 | tf_op jit(solution)/shard_map/all_to_all | solution.py:113
Sparse Core Ops, SparseCore 0:
  83.6 15.5 all-gather.1
  209.6 55.1 all-reduce.2
where the time goes:
time: 413 us; the launch traced here: 406 us
  other arithmetic  143 us (35%)
  local copies, waits for them, and re-layouts  98.3 us (24%)
  waiting for transfers between devices  70.1 us (17%)
  matrix products  60.2 us (15%)
  starting transfers between devices  19.4 us (5%)
  between operations  14.7 us (4%)
    another operation x1, other arithmetic  110 us
    select_n x1, local copies, waits for them, and re-layouts, shards(): jnp.where(live_mask[:, None, None, :], advanced, jnp.zeros((), jnp.float32))  80.7 us
    unnamed x3, waiting for transfers between devices  53.9 us
    dot_general x1, matrix products, shards(): jnp.einsum('frsc,snr->scfn', by_waves, legendre, preferred_element_type=j...  31.5 us
    select_n x1, other arithmetic, shards(): jnp.where(live_mask[:, None, None, :], spectra, jnp.zeros((), spectra.dty...  18.1 us
    dot_general x2, matrix products, shards(): jnp.einsum('sfn,snr->rsf', masked[:, component], legendre, preferred_elem...  17.7 us
    all_to_all x2, starting transfers between devices, shards(): lax.all_to_all(sent, 'band', split_axis=0, concat_axis=1, tiled=True)  13.3 us
    all_to_all x1, waiting for transfers between devices, shards(): lax.all_to_all(sent_back, 'band', split_axis=2, concat_axis=1, tiled=True)  10.9 us
  transfers between devices with their start and end apart: 5, of which 3 were waited for; matrix products, arithmetic and copies ran while one was open for 32% of the time, Pallas kernels for 0%

commit v1 on v0

v1 whole, which is shorter than its diff:
```python
import functools
import math

import jax
import jax.numpy as jnp
from jax import lax
from jax.experimental import pallas as pl
from jax.experimental.layout import Layout, with_layout_constraint
from jax.experimental.pallas import tpu as pltpu
from jax.sharding import PartitionSpec as P

FIELDS = 5
LEVELS = 24
TEMPER = 2
ENERGY = 4
LVL_ROWS = 8
SLAB = 128
MIB = 1024 * 1024

time_step = 1.0

COS_POLY = (
    0.9999999890590235, -19.739204499453994, 64.93911745989843, -85.45013953092186,
    60.167630951185615, -25.967599249120923, 6.528658161956132,
)
SIN_POLY = (
    6.283185302511506, -41.3417004053176, 81.60513138579954, -76.70301535389986,
    42.02592698629647, -14.89984666973851, 3.2381375126489513,
)


def up_to(value, unit):
    return -(-value // unit) * unit


class Sizes:
    def __init__(self, bands, groups, slots, fields, degrees, rows):
        self.bands, self.groups = bands, groups
        self.slots, self.fields, self.degrees, self.rows = slots, fields, degrees, rows
        self.tiles = degrees // SLAB
        self.slot_rows = fields * self.tiles * 2
        self.field_pad = up_to(fields, 8)
        self.share = -(-fields // groups)
        self.lanes = 4 * self.share
        self.quarters = 2
        if 4 * self.lanes <= SLAB and slots % 4 == 0:
            self.quarters = 4
        self.halves = self.quarters // 2
        self.chunk_live = slots // self.quarters
        self.chunk = up_to(self.chunk_live, 8)
        self.spots = self.quarters * self.chunk
        self.block = slots
        for size in (8, 4):
            if slots % size == 0 and (size * self.slot_rows) % 16 == 0:
                self.block = size
                break
        self.steps = slots // self.block
        self.pairs = self.halves * bands * self.chunk
        self.trunc = degrees - 1
        self.orbits = up_to((4 * self.trunc + 40) // 4 + 2, SLAB)
        self.levels = LEVELS // groups
        self.row_fields = FIELDS * LVL_ROWS


def owners(sizes, field):
    first, last = field * LEVELS, (field + 1) * LEVELS
    return [
        g for g in range(sizes.groups)
        if g * sizes.fields < last and (g + 1) * sizes.fields > first
    ]


def geo_rounds(sizes):
    sources, targets = owners(sizes, TEMPER), owners(sizes, ENERGY)
    wide = max(len(sources), len(targets))
    rounds = []
    for turn in range(wide):
        pairs = []
        for k in range(wide):
            s, t = k, (k + turn) % wide
            if s < len(sources) and t < len(targets):
                pairs.append((sources[s], targets[t]))
        if pairs:
            rounds.append(pairs)
    return rounds


def iota(shape, dim):
    return lax.broadcasted_iota(jnp.int32, shape, dim)


def one_hot(cond):
    return jnp.where(cond, 1.0, 0.0).astype(jnp.bfloat16)


def dot(a, b, dims=((1,), (0,))):
    return lax.dot_general(a, b, (dims, ((), ())), preferred_element_type=jnp.float32)


def chunk_position(sizes, lane):
    quarter = lane // sizes.lanes
    rest = lane % sizes.lanes
    row = rest // (2 * sizes.share)
    comp = rest // sizes.share % 2
    item = rest % sizes.share
    return quarter, row, comp, item


def spread_matrix(sizes, lev, transposed):
    tall = sizes.quarters * 4 * sizes.field_pad
    wide = sizes.groups * SLAB
    shape = (wide, tall) if transposed else (tall, wide)
    src = iota(shape, 1 if transposed else 0)
    dst = iota(shape, 0 if transposed else 1)
    group = dst // SLAB
    quarter, row, comp, item = chunk_position(sizes, dst % SLAB)
    start = lev * sizes.fields
    field = lax.rem(group - start % sizes.groups + sizes.groups, sizes.groups) + sizes.groups * item
    want = ((quarter * 2 + row) * 2 + comp) * sizes.field_pad + field
    return one_hot((src == want) & (field < sizes.fields) & (quarter < sizes.quarters))


def inverse_kernel(
    sizes, wave, lev_ref, geo_at, x_ref, leg_ref, depth_ref, active_ref,
    send_ref, geo_ref, wide, spots,
):
    step = pl.program_id(0)
    sz = sizes
    height = 2 * sz.slot_rows

    @pl.when(step == 0)
    def _():
        spots[...] = jnp.zeros_like(spots)
        wide[:, pl.ds(height, wide.shape[1] - height), :] = jnp.zeros(
            (wide.shape[0], wide.shape[1] - height, SLAB), jnp.float32
        )

    degree = iota((1, sz.degrees), 1)
    for pair in range(sz.block // 2):
        buf = wide.at[pair % wide.shape[0]]
        buf[pl.ds(0, height), :] = x_ref[pl.ds(pair * height, height), :].astype(jnp.float32)
        place = step * (sz.block // 2) + pair
        first_odd = wave[2 * place] & 1
        for side in range(2):
            number = wave[2 * place + side]
            table = jnp.where(degree >= number, leg_ref[2 * pair + side].astype(jnp.float32), 0.0)
            table = table.astype(jnp.bfloat16)
            total = jnp.zeros((sz.rows, 2 * sz.field_pad), jnp.float32)
            for t in range(0, sz.tiles, 2):
                parts = []
                for tt in range(t, min(t + 2, sz.tiles)):
                    parts.append(jnp.concatenate([
                        buf[pl.ds(side * sz.slot_rows + 2 * tt + c, sz.field_pad, stride=2 * sz.tiles), :]
                        for c in range(2)
                    ], axis=0).astype(jnp.bfloat16))
                values = jnp.concatenate(parts, axis=1)
                piece = table[:, t * SLAB:t * SLAB + values.shape[1]]
                total += dot(piece, values, ((1,), (1,)))
            odd = first_odd if side == 0 else 1 - first_odd
            half = place // sz.chunk_live
            spot = (odd * sz.halves + half) * sz.chunk + (place - half * sz.chunk_live)
            at = pl.multiple_of(spot * sz.rows, sz.rows)
            spots[pl.ds(at, sz.rows), 0:2 * sz.field_pad] = total

    @pl.when(step == sz.steps - 1)
    def _():
        lev = lev_ref[0]
        spread = spread_matrix(sz, lev, False)
        pad = 2 * sz.field_pad
        shape = (2 * pad, SLAB)
        src, dst = iota(shape, 0), iota(shape, 1)
        weights = []
        for turn in range(geo_ref.shape[0]):
            field = lev * sz.fields + src % sz.field_pad
            under = field - TEMPER * LEVELS
            above = geo_at[turn] + dst % sz.field_pad
            hit = (
                (src // sz.field_pad == dst // sz.field_pad) & (src % sz.field_pad < sz.fields)
                & (under >= 0) & (under < LEVELS) & (above >= 0) & (above <= under)
                & (dst % sz.field_pad < sz.fields)
            )
            weight = jnp.where(hit, depth_ref[...], 0.0)
            high = weight.astype(jnp.bfloat16)
            low = (weight - high.astype(jnp.float32)).astype(jnp.bfloat16)
            weights.append(jnp.concatenate([high, low], axis=0))
        number = active_ref[:, 0:1]
        mult = jnp.where(number > 0, 2.0, jnp.where(number == 0, 1.0, 0.0))
        geo_lane = iota((sz.spots, SLAB), 1)
        for rp in range(sz.rows // 2):
            both = jnp.concatenate([
                spots[pl.ds(2 * rp + r, sz.spots, stride=sz.rows), :][:, 0:pad] for r in range(2)
            ], axis=1)
            exact = both.astype(jnp.bfloat16)
            scaled = (exact.astype(jnp.float32) * mult)
            cut = jnp.concatenate([
                scaled[q * sz.chunk:(q + 1) * sz.chunk] for q in range(sz.quarters)
            ], axis=1).astype(jnp.bfloat16)
            chunk = dot(cut, spread).astype(jnp.bfloat16)
            for g in range(sz.groups):
                send_ref[rp, g] = chunk[:, g * SLAB:(g + 1) * SLAB]
            points = jnp.where(
                geo_lane // pad == 0, active_ref[:, 1 + 2 * rp:2 + 2 * rp],
                active_ref[:, 2 + 2 * rp:3 + 2 * rp],
            )
            sine_zero = (number == 0) & (geo_lane // sz.field_pad % 2 == 1)
            points = jnp.where(sine_zero, 0.0, points)
            double = jnp.concatenate([exact, exact], axis=1)
            for turn in range(geo_ref.shape[0]):
                geo_ref[turn, rp] = (dot(double, weights[turn]) * points).astype(jnp.bfloat16)


def basis_kernel(sizes, points_ref, even_ref, out_ref, rows):
    sz = sizes
    width = sz.orbits

    def turn_of(mj, length, inverse):
        whole = jnp.floor(mj * inverse + 0.5)
        return (mj - whole * length) * inverse

    def cos_sin(z):
        y = z * z
        c = jnp.full_like(y, COS_POLY[-1])
        for a in COS_POLY[-2::-1]:
            c = c * y + a
        s = jnp.full_like(y, SIN_POLY[-1])
        for a in SIN_POLY[-2::-1]:
            s = s * y + a
        return c, s * z

    @pl.when(pl.program_id(0) == 0)
    def _():
        length_a = points_ref[0].astype(jnp.float32)
        length_b = points_ref[1].astype(jnp.float32)
        count_a = points_ref[0] // 4 + 1
        at = iota((8, width), 1)
        second = at >= count_a
        column = (at - jnp.where(second, count_a, 0)).astype(jnp.float32)
        length = jnp.where(second, length_b, length_a)
        inverse = 1.0 / length
        c, s = cos_sin(turn_of(sz.trunc * column, length, inverse))
        rows[0] = column
        rows[1] = length
        rows[2] = inverse
        rows[3] = 1.0 / jnp.sqrt(length)
        rows[4] = c
        rows[5] = s

    high = out_ref.shape[1]
    tall = 32
    for at in range(0, width, SLAB):
        cols = pl.ds(at, SLAB)
        column, length, inverse, scale, top_c, top_s = (
            jnp.concatenate([rows[k, :, cols]] * (tall // 8), axis=0) for k in range(6)
        )
        bound = 0.5 * (length - 1.0)

        def body(i, carry):
            start = pl.multiple_of(i * tall, tall)
            even = even_ref[pl.ds(start, tall), :]
            c, s = cos_sin(turn_of(even * column, length, inverse))
            c = c * scale
            s = s * scale
            oc = top_c * c + top_s * s
            os = top_s * c - top_c * s
            live = even <= bound
            odd_live = (sz.trunc - even) <= bound
            dest = pl.ds(start, tall)
            out_ref[0, dest, cols] = jnp.where(live, c, 0.0).astype(jnp.bfloat16)
            out_ref[1, dest, cols] = jnp.where(live, -s, 0.0).astype(jnp.bfloat16)
            out_ref[2, dest, cols] = jnp.where(odd_live, oc, 0.0).astype(jnp.bfloat16)
            out_ref[3, dest, cols] = jnp.where(odd_live, -os, 0.0).astype(jnp.bfloat16)
            return carry

        lax.fori_loop(0, high // tall, body, 0)


def take_matrix(sizes, lev, transposed):
    sz = sizes
    tall = sz.groups * SLAB
    wide = sz.quarters * 2 * SLAB
    shape = (wide, tall) if transposed else (tall, wide)
    src = iota(shape, 1 if transposed else 0)
    dst = iota(shape, 0 if transposed else 1)
    piece = dst // SLAB
    lane = dst % SLAB
    row = lane // sz.row_fields
    field = lane % sz.row_fields // LVL_ROWS
    level = lane % LVL_ROWS
    whole = field * LEVELS + level * sz.groups + lev
    owner = whole // sz.fields
    start = owner * sz.fields
    first = lax.rem(lev - start % sz.groups + sz.groups, sz.groups)
    item = (whole - start - first) // sz.groups
    want = owner * SLAB + (piece // 2) * sz.lanes + (row * 2 + piece % 2) * sz.share + item
    return one_hot((src == want) & (row < 2) & (level < sz.levels))


def grid_kernel(sizes, points_ref, gauss_ref, lev_ref, recv_ref, basis_ref, send_ref, terms):
    sz = sizes
    lev = lev_ref[0]
    width = sz.bands * sz.chunk
    joined = jnp.concatenate([
        recv_ref[:, g].astype(jnp.float32).reshape(width, SLAB) for g in range(sz.groups)
    ], axis=1).astype(jnp.bfloat16)
    taken = dot(joined, take_matrix(sz, lev, False))
    coeffs = []
    for parity in range(2):
        for comp in range(2):
            parts = []
            for half in range(sz.halves):
                piece = (parity * sz.halves + half) * 2 + comp
                parts.append(taken[:, piece * SLAB:(piece + 1) * SLAB])
            coeffs.append(jnp.concatenate(parts, axis=0).T.astype(jnp.bfloat16)[0:2 * sz.row_fields])
    count_a = points_ref[0] // 4 + 1
    count_b = points_ref[1] // 4 + 1
    high = sz.row_fields
    for at in range(0, sz.orbits, SLAB):
        cols = pl.ds(at, SLAB)
        place = iota((1, SLAB), 1) + at
        second = place >= count_a
        grids = []
        for k in range(4):
            both = dot(coeffs[k], basis_ref[k, :, cols])
            grids.append(jnp.where(second, both[high:], both[:high]))
        ce, se, co, so = grids
        plus, minus = ce + co, ce - co
        splus, sminus = se + so, se - so
        values = (plus + splus, minus - sminus, minus + sminus, plus - splus)
        outs = []
        for v in values:
            u, w, tem, hum, ozo = (v[i * LVL_ROWS:(i + 1) * LVL_ROWS] for i in range(FIELDS))
            outs.append(jnp.concatenate(
                [u * tem, w * tem, u * hum, w * ozo, 0.5 * (u * u + w * w)], axis=0
            ))
        offset = place - jnp.where(second, count_a, 0)
        count = jnp.where(second, count_b, count_a)
        weight = jnp.where((offset == 0) | (offset == count - 1), 0.5, 1.0)
        weight = jnp.where(offset < count, weight, 0.0)
        t0, t1, t2, t3 = (o * weight for o in outs)
        a, b, c, d = t0 + t3, t1 + t2, t0 - t3, t2 - t1
        folds = (a + b, c + d, a - b, c - d)
        for k in range(4):
            first = jnp.where(second, 0.0, folds[k])
            last = jnp.where(second, folds[k], 0.0)
            empty = jnp.zeros((SLAB - 2 * high, SLAB), jnp.float32)
            terms[k, :, cols] = jnp.concatenate([first, last, empty], axis=0).astype(jnp.bfloat16)
    gauss = jnp.where(iota((1, SLAB), 1) < high, gauss_ref[0], gauss_ref[1])
    back = []
    for k in range(4):
        back.append((dot(basis_ref[k], terms[k], ((1,), (1,))) * gauss).astype(jnp.bfloat16))
    columns = []
    for parity in range(2):
        for half in range(sz.halves):
            for comp in range(2):
                columns.append(back[parity * 2 + comp][half * width:(half + 1) * width])
    sent = dot(jnp.concatenate(columns, axis=1), take_matrix(sz, lev, True))
    for g in range(sz.groups):
        part = sent[:, g * SLAB:(g + 1) * SLAB].reshape(sz.bands, sz.chunk, SLAB)
        send_ref[:, g] = part.astype(jnp.bfloat16)


def forward_kernel(
    sizes, wave, lev_ref, back_ref, geo_ref, x_ref, leg_ref, speed_ref, out_ref,
    wide, spots, inverse,
):
    sz = sizes
    step = pl.program_id(0)
    pad = 2 * sz.field_pad
    height = 2 * sz.slot_rows

    @pl.when(step == 0)
    def _():
        wide[:, pl.ds(height, wide.shape[1] - height), :] = jnp.zeros(
            (wide.shape[0], wide.shape[1] - height, SLAB), jnp.float32
        )
        gather = spread_matrix(sz, lev_ref[0], True)
        for rp in range(sz.rows // 2):
            cut = jnp.concatenate([back_ref[rp, g] for g in range(sz.groups)], axis=1)
            whole = dot(cut, gather)
            rows = jnp.concatenate([
                whole[:, q * 2 * pad:(q + 1) * 2 * pad] for q in range(sz.quarters)
            ], axis=0)
            for turn in range(geo_ref.shape[0]):
                rows = rows + geo_ref[turn, rp].astype(jnp.float32)[:, 0:2 * pad]
            for r in range(2):
                part = rows[:, r * pad:(r + 1) * pad]
                part = jnp.concatenate([part, jnp.zeros((sz.spots, SLAB - pad), jnp.float32)], axis=1)
                spots[pl.ds(2 * rp + r, sz.spots, stride=sz.rows), :] = part
        for t in range(sz.tiles):
            degree = iota((sz.field_pad, SLAB), 1) + t * SLAB
            helm = (degree * (degree + 1)).astype(jnp.float32) / float(sz.trunc * (sz.trunc + 1))
            inverse[t] = 1.0 / (1.0 + time_step * time_step * helm * speed_ref[...])

    for pair in range(sz.block // 2):
        buf = wide.at[pair % wide.shape[0]]
        buf[pl.ds(0, height), :] = x_ref[pl.ds(pair * height, height), :].astype(jnp.float32)
        place = step * (sz.block // 2) + pair
        first_odd = wave[2 * place] & 1
        for side in range(2):
            number = wave[2 * place + side]
            floor = jnp.where(number < 0, sz.degrees, number)
            odd = first_odd if side == 0 else 1 - first_odd
            half = place // sz.chunk_live
            spot = (odd * sz.halves + half) * sz.chunk + (place - half * sz.chunk_live)
            at = pl.multiple_of(spot * sz.rows, sz.rows)
            left = spots[pl.ds(at, sz.rows), :].T.astype(jnp.bfloat16)[0:pad]
            base = (2 * pair + side) * sz.slot_rows
            for t in range(sz.tiles):
                tend = dot(left, leg_ref[2 * pair + side, :, t * SLAB:(t + 1) * SLAB])
                live = iota((1, SLAB), 1) + t * SLAB >= floor
                for c in range(2):
                    old = buf[pl.ds(side * sz.slot_rows + 2 * t + c, sz.field_pad, stride=2 * sz.tiles), :]
                    new = (old + time_step * tend[c * sz.field_pad:(c + 1) * sz.field_pad]) * inverse[t]
                    new = jnp.where(live, new, 0.0)
                    out_ref[pl.ds(base + 2 * t + c, sz.fields, stride=2 * sz.tiles), :] = new[0:sz.fields]


def params(mib):
    return pltpu.CompilerParams(vmem_limit_bytes=mib * MIB)


def smem():
    return pl.BlockSpec(memory_space=pltpu.SMEM)


def whole_block(shape):
    return pl.BlockSpec(shape, lambda *_: (0,) * len(shape))


def shards(spectra, legendre, slot_wave, row_points, gauss_weight, layer_depth, mode_speed):
    slots, _, fields, degrees = spectra.shape
    rows = legendre.shape[2]
    sz = Sizes(lax.axis_size("band"), lax.axis_size("lev"), slots, fields, degrees, rows)
    band_index = lax.axis_index("band")
    lev_index = lax.axis_index("lev")
    lev = lev_index.astype(jnp.int32).reshape(1)
    wave = lax.dynamic_slice_in_dim(slot_wave, band_index * slots, slots)
    own_points = lax.dynamic_slice_in_dim(row_points, band_index * 2, 2)
    own_weight = lax.dynamic_slice_in_dim(gauss_weight, band_index * 2, 2)

    lines = spectra.reshape(slots, 2, fields, sz.tiles, SLAB)
    lines = with_layout_constraint(lines, Layout((0, 2, 3, 1, 4)))
    lines = lines.transpose(0, 2, 3, 1, 4).reshape(slots * sz.slot_rows, SLAB)
    tables = legendre.transpose(0, 2, 1)

    pair_wave = slot_wave.reshape(-1, 2)
    even_wave = jnp.where(pair_wave[:, 0] % 2 == 0, pair_wave[:, 0], pair_wave[:, 1])
    even_wave = even_wave.reshape(sz.bands, sz.halves, sz.chunk_live)
    even_wave = jnp.pad(even_wave, ((0, 0), (0, 0), (0, sz.chunk - sz.chunk_live)), constant_values=0)
    even_wave = even_wave.transpose(1, 0, 2).reshape(sz.pairs, 1).astype(jnp.float32)

    own_pair = wave.reshape(-1, 2)
    swap = own_pair[:, :1] % 2 != 0
    own_pair = jnp.where(swap, own_pair[:, ::-1], own_pair)
    spot_wave = own_pair.reshape(sz.halves, sz.chunk_live, 2).transpose(2, 0, 1)
    spot_wave = jnp.pad(
        spot_wave, ((0, 0), (0, 0), (0, sz.chunk - sz.chunk_live)), constant_values=-1
    ).reshape(sz.spots, 1)
    reach = (spot_wave >= 0) & (2 * spot_wave <= row_points[None, :] - 1)
    active = jnp.concatenate(
        [spot_wave.astype(jnp.float32), jnp.where(reach, gauss_weight[None, :], 0.0)], axis=1
    )

    rounds = geo_rounds(sz)
    places = []
    for pairs in rounds:
        table = [2 * LEVELS + sz.fields] * sz.groups
        for source, target in pairs:
            table[source] = target * sz.fields - ENERGY * LEVELS
        places.append(table)
    geo_at = jnp.array(places, jnp.int32)[:, lev_index]
    held = lev_index * sz.fields + jnp.arange(sz.field_pad, dtype=jnp.int32) - TEMPER * LEVELS
    depth = layer_depth[jnp.clip(held, 0, LEVELS - 1)]
    depth = jnp.tile(depth, 4).reshape(4 * sz.field_pad, 1)

    tail = up_to((sz.field_pad - sz.fields) * 2 * sz.tiles, 16)
    wide_shape = pltpu.VMEM((2, 2 * sz.slot_rows + tail, SLAB), jnp.float32)
    spots_shape = pltpu.VMEM((sz.spots * sz.rows, SLAB), jnp.float32)
    lines_block = (sz.block * sz.slot_rows, SLAB)
    table_block = (sz.block, sz.rows, degrees)
    send_shape = (sz.bands, sz.groups, sz.chunk, SLAB)
    geo_shape = (len(rounds), sz.rows // 2, sz.spots, SLAB)

    sent, geo = pl.pallas_call(
        functools.partial(inverse_kernel, sz),
        grid=(sz.steps,),
        in_specs=[
            smem(), smem(), smem(),
            pl.BlockSpec(lines_block, lambda i: (i, 0)),
            pl.BlockSpec(table_block, lambda i: (i, 0, 0)),
            whole_block(depth.shape),
            whole_block(active.shape),
        ],
        out_specs=[whole_block(send_shape), whole_block(geo_shape)],
        out_shape=[
            jax.ShapeDtypeStruct(send_shape, jnp.bfloat16),
            jax.ShapeDtypeStruct(geo_shape, jnp.bfloat16),
        ],
        scratch_shapes=[wide_shape, spots_shape],
        compiler_params=params(32),
        name="inverse_legendre",
    )(wave, lev, geo_at, lines, tables, depth, active)

    both = ("band", "lev")
    total = sz.bands * sz.groups
    flat = (total * sz.chunk, SLAB)
    arrived = lax.all_to_all(sent.reshape(flat), both, split_axis=0, concat_axis=0, tiled=True)
    geo_here = jnp.stack([
        lax.ppermute(geo[turn], "lev", pairs) for turn, pairs in enumerate(rounds)
    ])

    basis_shape = (4, sz.pairs, sz.orbits)
    high = SLAB if sz.pairs % SLAB == 0 else sz.pairs
    basis = pl.pallas_call(
        functools.partial(basis_kernel, sz),
        grid=(sz.pairs // high,),
        in_specs=[smem(), pl.BlockSpec((high, 1), lambda i: (i, 0))],
        out_specs=pl.BlockSpec((4, high, sz.orbits), lambda i: (0, i, 0)),
        out_shape=jax.ShapeDtypeStruct(basis_shape, jnp.bfloat16),
        scratch_shapes=[pltpu.VMEM((6, 8, sz.orbits), jnp.float32)],
        compiler_params=params(32),
        cost_estimate=pl.CostEstimate(flops=60 * sz.pairs * sz.orbits, bytes_accessed=8 * sz.pairs * sz.orbits, transcendentals=0),
        name="basis",
    )(own_points, even_wave)

    returned = pl.pallas_call(
        functools.partial(grid_kernel, sz),
        in_specs=[smem(), smem(), smem()] + [pl.BlockSpec(memory_space=pltpu.VMEM)] * 2,
        out_specs=pl.BlockSpec(memory_space=pltpu.VMEM),
        out_shape=jax.ShapeDtypeStruct(send_shape, jnp.bfloat16),
        scratch_shapes=[pltpu.VMEM((4, SLAB, sz.orbits), jnp.bfloat16)],
        compiler_params=params(40),
        name="grid_products",
    )(own_points, own_weight, lev, arrived.reshape(send_shape), basis)

    back = lax.all_to_all(returned.reshape(flat), both, split_axis=0, concat_axis=0, tiled=True)

    speed = jnp.pad(mode_speed, (0, sz.field_pad - fields)).reshape(sz.field_pad, 1)
    out = pl.pallas_call(
        functools.partial(forward_kernel, sz),
        grid=(sz.steps,),
        in_specs=[
            smem(), smem(),
            whole_block(send_shape), whole_block(geo_shape),
            pl.BlockSpec(lines_block, lambda i: (i, 0)),
            pl.BlockSpec(table_block, lambda i: (i, 0, 0)),
            whole_block(speed.shape),
        ],
        out_specs=pl.BlockSpec(lines_block, lambda i: (i, 0)),
        out_shape=jax.ShapeDtypeStruct((slots * sz.slot_rows, SLAB), jnp.float32),
        scratch_shapes=[wide_shape, spots_shape, pltpu.VMEM((sz.tiles, sz.field_pad, SLAB), jnp.float32)],
        compiler_params=params(40),
        name="forward_legendre",
    )(wave, lev, back.reshape(send_shape), geo_here, lines, tables, speed)

    out = out.reshape(slots, fields, sz.tiles, 2, SLAB).transpose(0, 1, 3, 2, 4)
    return out.reshape(slots, fields, 2, degrees).transpose(0, 2, 1, 3)


def solution(mesh):
    return jax.shard_map(
        shards,
        mesh=mesh,
        in_specs=(
            P("band", None, "lev", None),
            P("band", None, None),
            P(),
            P(),
            P(),
            P(),
            P("lev"),
        ),
        out_specs=P("band", None, "lev", None),
        check_vma=False,
    )
```

time: 413 us -> 132 us (0.32); the launches traced: 406 us -> 131 us
  other arithmetic: 143 us -> 1.75 us
  Pallas kernels: 0 us -> 87.5 us
  local copies, waits for them, and re-layouts: 98.3 us -> 16.2 us
  matrix products: 60.2 us -> 0 us
  waiting for transfers between devices: 70.1 us -> 10.4 us
  between operations: 14.7 us -> 0.2 us
  starting transfers between devices: 19.4 us -> 14.5 us
    another operation x3 -> x1, other arithmetic: 111 us -> 0.06 us  [shards(): jnp.stack([lax.ppermute(geo[turn], 'lev', pairs) for turn, pairs in enume...]
    pallas_call x0 -> x4, Pallas kernels: none -> 87.5 us  [the longest x1 33.5 us: shards(): pl.pallas_call(functools.partial(forward_kernel, sz), grid=(sz.steps,), i...]
    select_n x1 -> x0, local copies, waits for them, and re-layouts: 80.7 us -> none  [shards(): jnp.where(live_mask[:, None, None, :], advanced, jnp.zeros((), jnp.float32))]
    dot_general x8 -> x0, matrix products: 60.2 us -> none  [the longest x1 31.5 us: shards(): jnp.einsum('frsc,snr->scfn', by_waves, legendre, preferred_element_type=j...]
    unnamed x3 -> x0, waiting for transfers between devices: 53.9 us -> none
    select_n x3 -> x2, other arithmetic: 19.5 us -> 0.76 us  [the longest x1 0.75 us: shards(): jnp.where(reach, gauss_weight[None, :], 0.0)]
    unnamed x23 -> x18, local copies, waits for them, and re-layouts: 2.4 us -> 11.8 us
    another operation x4 -> x2, local copies, waits for them, and re-layouts: 7.12 us -> 0.12 us  [shards(): depth = jnp.tile(depth, 4).reshape(4 * sz.field_pad, 1)]
  transfers between devices with their start and end apart: 5 -> 4, of which waited for: 3 -> 1; matrix products, arithmetic and copies ran while one was open for 32% -> 1% of each run, Pallas kernels for 0% -> 19%
where the time goes in v1:
time: 132 us; the launch traced here: 131 us
  Pallas kernels  87.5 us (66%)
  local copies, waits for them, and re-layouts  16.2 us (12%)
  starting transfers between devices  14.5 us (11%)
  waiting for transfers between devices  10.4 us (8%)
  other arithmetic  1.75 us (1%)
    pallas_call x1, Pallas kernels, shards(): pl.pallas_call(functools.partial(forward_kernel, sz), grid=(sz.steps,), i...  33.5 us
    pallas_call x1, Pallas kernels, shards(): pl.pallas_call(functools.partial(basis_kernel, sz), grid=(sz.pairs // hig...  24.5 us
    pallas_call x1, Pallas kernels, shards(): pl.pallas_call(functools.partial(inverse_kernel, sz), grid=(sz.steps,), i...  21.7 us
    unnamed x18, local copies, waits for them, and re-layouts  11.8 us
    all_to_all x1, waiting for transfers between devices, shards(): lax.all_to_all(returned.reshape(flat), both, split_axis=0, concat_axis=0,...  10.4 us
    pallas_call x1, Pallas kernels, shards(): pl.pallas_call(functools.partial(grid_kernel, sz), in_specs=[smem(), smem...  7.86 us
    all_to_all x1, starting transfers between devices, shards(): lax.all_to_all(sent.reshape(flat), both, split_axis=0, concat_axis=0, til...  7.29 us
    all_to_all x1, starting transfers between devices, shards(): lax.all_to_all(returned.reshape(flat), both, split_axis=0, concat_axis=0,...  5.83 us
  transfers between devices with their start and end apart: 4, of which 1 were waited for; matrix products, arithmetic and copies ran while one was open for 1% of the time, Pallas kernels for 19%

profile of v1, /device:TPU:0, one launch (start us, length us, event | category | flops | bytes accessed | tf_op | source)
XLA Modules:
  0.0 130.6 jit_solution(2537057230757986048)
XLA Ops:
  0.0 0.0 copy-start
  0.0 0.0 copy-start.5
  0.0 0.0 copy-start.7
  0.0 0.0 copy-start.6
  0.0 0.8 dynamic_slice.12.wave
  0.8 0.1 reshape.124
  1.0 0.1 fusion.2
  1.1 0.1 rev.3
  1.2 0.1 fusion.5
  1.3 0.7 broadcast_add_fusion
  2.0 0.1 copy.25
  2.1 0.1 convert_element_type.32
  2.2 0.1 copy.27
  2.2 0.1 mul.37
  2.3 0.1 copy.26
  2.4 0.1 ge.24
  2.5 0.8 and_select_fusion.1
  3.3 0.1 copy.29.active_ref
  3.4 0.0 copy-done
  3.4 0.7 gather_fusion
  4.1 0.1 reshape_tile.4.depth_ref
  4.2 0.7 dynamic-slice_bitcast_fusion.geo_at
  4.9 0.0 copy-start.3
  4.9 2.9 %copy-done.3 = bf16[160,1280,16]{1,2,0:T(8,128)(2,1)S(1)} copy-done((bf16[160,1280,16]{1,2,0:T(8,128)(2,1)S(1)}, bf16[160,1280,16]{1,2,0:T(8,128)(2,1)}, u32[]{:S(2)}) %copy-start.3) | copy-done | bytes 6553624
  7.8 0.0 copy-start.8
  7.8 21.7 %inverse_legendre.1 = (bf16[8,4,40,128]{3,2,1,0:T(8,128)(2,1)}, bf16[2,8,160,128]{3,2,1,0:T(8,128)(2,1)S(1)}) custom-call(s32[160]{0:T(256)S(1)} %dynamic_slice.12.wave, s32[1]{0:T(128)} %bitcast.lev_ref, s32[2]{0:T(128)S(1)} %dynamic-slice_bitcast_fusion.geo_at, bf16[96000,128]{1,0:T(8,128)(2,1)} %bitcast.42, bf16[160,16,1280]{2,1,0:T(8,128)(2,1)S(1)} %bitcast.38, ...), custom_call_target="tpu_custom_call" | custom-call | tf_op jit(solution)/shard_map/inverse_legendre/pallas_call | solution.py:484
  29.5 7.3 %all-to-all-start = ((bf16[32,40,128]{2,1,0:T(8,128)(2,1)}), bf16[32,40,128]{2,1,0:T(8,128)(2,1)S(1)}, u32[]{:S(2)}, u32[]{:S(2)}) async-start(bf16[32,40,128]{2,1,0:T(8,128)(2,1)} %bitcast.13), calls=%async_computation | async-start | bytes 655360 | tf_op jit(solution)/shard_map/all_to_all | solution.py:507
  36.8 0.0 copy-done.7
  36.8 0.1 dynamic_slice.13.points_ref
  36.9 0.0 copy-done.6
  36.9 0.1 dynamic_slice.14.gauss_ref
  37.0 0.0 copy-done.5
  37.0 0.3 reshape.126
  37.3 0.3 slice_reduce_fusion
  37.6 0.1 squeeze.18
  37.7 0.1 squeeze.17
  37.8 0.1 convert_element_type.36.even_ref
  38.0 24.5 %basis.1.basis_ref = bf16[4,640,1408]{2,1,0:T(8,128)(2,1)S(1)} custom-call(s32[2]{0:T(128)S(1)} %dynamic_slice.13.points_ref, f32[640,1]{1,0:T(8,128)S(1)} %convert_element_type.36.even_ref), custom_call_target="tpu_custom_call" | custom-call | flops 54067200 | bytes 7208960 | tf_op jit(solution)/shard_map/basis/pallas_call | solution.py:514
  62.5 0.0 copy-start.1
  62.5 3.0 %copy-done.1 = bf16[4,640,1408]{2,1,0:T(8,128)(2,1)} copy-done((bf16[4,640,1408]{2,1,0:T(8,128)(2,1)}, bf16[4,640,1408]{2,1,0:T(8,128)(2,1)S(1)}, u32[]{:S(2)}) %copy-start.1) | copy-done | bytes 7208984
  65.5 0.0 all-to-all-done
  65.5 0.0 copy-start.2
  65.5 3.0 %copy-done.2 = bf16[4,640,1408]{2,1,0:T(8,128)(2,1)S(1)} copy-done((bf16[4,640,1408]{2,1,0:T(8,128)(2,1)S(1)}, bf16[4,640,1408]{2,1,0:T(8,128)(2,1)}, u32[]{:S(2)}) %copy-start.2) | copy-done | bytes 7208984
  68.5 7.9 %grid_products.1 = bf16[8,4,40,128]{3,2,1,0:T(8,128)(2,1)} custom-call(s32[2]{0:T(128)S(1)} %dynamic_slice.13.points_ref, f32[2]{0:T(128)S(1)} %dynamic_slice.14.gauss_ref, s32[1]{0:T(128)} %bitcast.lev_ref, bf16[8,4,40,128]{3,2,1,0:T(8,128)(2,1)S(1)} %bitcast.40, bf16[4,640,1408]{2,1,0:T(8,128)(2,1)S(1)} %copy-done.2), custom_call_target="tpu_custom_call" | custom-call | tf_op jit(solution)/shard_map/grid_products/pallas_call | solution.py:526
  76.4 5.8 %all-to-all-start.1 = ((bf16[32,40,128]{2,1,0:T(8,128)(2,1)}), bf16[32,40,128]{2,1,0:T(8,128)(2,1)S(1)}, u32[]{:S(2)}, u32[]{:S(2)}) async-start(bf16[32,40,128]{2,1,0:T(8,128)(2,1)} %bitcast.16), calls=%async_computation.1 | async-start | bytes 655360 | tf_op jit(solution)/shard_map/all_to_all | solution.py:536
  82.3 0.7 collective-permute-start
  83.0 0.7 collective-permute-start.1
  83.7 0.0 copy-done.8
  83.7 0.1 copy.32.speed_ref
  83.8 0.0 collective-permute-done
  83.8 0.0 collective-permute-done.1
  83.8 0.1 pad_maximum_fusion.geo_ref
  83.8 10.4 %all-to-all-done.1 = bf16[32,40,128]{2,1,0:T(8,128)(2,1)S(1)} async-done(((bf16[32,40,128]{2,1,0:T(8,128)(2,1)}), bf16[32,40,128]{2,1,0:T(8,128)(2,1)S(1)}, u32[]{:S(2)}, u32[]{:S(2)}) %all-to-all-start.1) | async-done | bytes 327712 | tf_op jit(solution)/shard_map/all_to_all | solution.py:536
  94.2 0.0 copy-start.4
  94.2 2.9 %copy-done.4 = bf16[160,1280,16]{1,2,0:T(8,128)(2,1)S(1)} copy-done((bf16[160,1280,16]{1,2,0:T(8,128)(2,1)S(1)}, bf16[160,1280,16]{1,2,0:T(8,128)(2,1)}, u32[]{:S(2)}) %copy-start.4) | copy-done | bytes 6553624
  97.1 33.5 %forward_legendre.1 = f32[96000,128]{1,0:T(8,128)} custom-call(s32[160]{0:T(256)S(1)} %dynamic_slice.12.wave, s32[1]{0:T(128)} %bitcast.lev_ref, bf16[8,4,40,128]{3,2,1,0:T(8,128)(2,1)S(1)} %bitcast.41, bf16[2,8,160,128]{3,2,1,0:T(8,128)(2,1)S(1)} %pad_maximum_fusion.geo_ref, bf16[96000,128]{1,0:T(8,128)(2,1)} %bitcast.43, ...), custom_call_target="tpu_custom_call" | custom-call | tf_op jit(solution)/shard_map/forward_legendre/pallas_call | solution.py:539
  (10 shorter events, 0.1 us)
Async XLA Ops:
  0.0 3.4 %copy-start = (f32[24]{0:T(128)S(1)}, f32[24]{0:T(128)}, u32[]{:S(2)}) copy-start(f32[24]{0:T(128)} %param.13) | copy-start | bytes 292
  0.0 37.0 %copy-start.5 = (s32[1280]{0:T(1024)S(1)}, s32[1280]{0:T(1024)}, u32[]{:S(2)}) copy-start(s32[1280]{0:T(1024)} %param.10) | copy-start | bytes 15364
  0.0 36.8 %copy-start.7 = (s32[16]{0:T(128)S(1)}, s32[16]{0:T(128)}, u32[]{:S(2)}) copy-start(s32[16]{0:T(128)} %param.11) | copy-start | bytes 196
  0.0 36.9 %copy-start.6 = (f32[16]{0:T(128)S(1)}, f32[16]{0:T(128)}, u32[]{:S(2)}) copy-start(f32[16]{0:T(128)} %param.12) | copy-start | bytes 196
  4.9 2.9 %copy-start.3 = (bf16[160,1280,16]{1,2,0:T(8,128)(2,1)S(1)}, bf16[160,1280,16]{1,2,0:T(8,128)(2,1)}, u32[]{:S(2)}) copy-start(bf16[160,1280,16]{1,2,0:T(8,128)(2,1)} %param.9) | copy-start | bytes 19660804
  7.8 75.9 %copy-start.8 = (f32[30]{0:T(128)S(1)}, f32[30]{0:T(128)}, u32[]{:S(2)}) copy-start(f32[30]{0:T(128)} %param.14) | copy-start | bytes 364
  29.5 36.0 %all-to-all-start = ((bf16[32,40,128]{2,1,0:T(8,128)(2,1)}), bf16[32,40,128]{2,1,0:T(8,128)(2,1)S(1)}, u32[]{:S(2)}, u32[]{:S(2)}) async-start(bf16[32,40,128]{2,1,0:T(8,128)(2,1)} %bitcast.13), calls=%async_computation | async-start | bytes 655360 | tf_op jit(solution)/shard_map/all_to_all | solution.py:507
  62.5 3.0 %copy-start.1 = (bf16[4,640,1408]{2,1,0:T(8,128)(2,1)}, bf16[4,640,1408]{2,1,0:T(8,128)(2,1)S(1)}, u32[]{:S(2)}) copy-start(bf16[4,640,1408]{2,1,0:T(8,128)(2,1)S(1)} %basis.1.basis_ref) | copy-start | bytes 21626884
  65.5 3.0 %copy-start.2 = (bf16[4,640,1408]{2,1,0:T(8,128)(2,1)S(1)}, bf16[4,640,1408]{2,1,0:T(8,128)(2,1)}, u32[]{:S(2)}) copy-start(bf16[4,640,1408]{2,1,0:T(8,128)(2,1)} %copy-done.1) | copy-start | bytes 21626884
  76.4 17.8 %all-to-all-start.1 = ((bf16[32,40,128]{2,1,0:T(8,128)(2,1)}), bf16[32,40,128]{2,1,0:T(8,128)(2,1)S(1)}, u32[]{:S(2)}, u32[]{:S(2)}) async-start(bf16[32,40,128]{2,1,0:T(8,128)(2,1)} %bitcast.16), calls=%async_computation.1 | async-start | bytes 655360 | tf_op jit(solution)/shard_map/all_to_all | solution.py:536
  82.3 1.5 %collective-permute-start = (bf16[8,160,128]{2,1,0:T(8,128)(2,1)S(1)}, bf16[8,160,128]{2,1,0:T(8,128)(2,1)S(1)}, u32[]{:S(2)}, u32[]{:S(2)}) collective-permute-start(bf16[8,160,128]{2,1,0:T(8,128)(2,1)S(1)} %get-tuple-element.13), channel_id=1, source_target_pairs={{1,3},{5,7},{9,11},{13,15},{17,19},{21,23},{25,27},{29,31}} | collective-permute-start | bytes 983048 | tf_op jit(solution)/shard_map/ppermute | solution.py:509
  83.0 0.8 collective-permute-start.1
  94.2 2.9 %copy-start.4 = (bf16[160,1280,16]{1,2,0:T(8,128)(2,1)S(1)}, bf16[160,1280,16]{1,2,0:T(8,128)(2,1)}, u32[]{:S(2)}) copy-start(bf16[160,1280,16]{1,2,0:T(8,128)(2,1)} %param.9) | copy-start | bytes 19660804

commit v2 on v1

v2 whole, which is shorter than its diff:
```python
import functools
import math

import jax
import jax.numpy as jnp
from jax import lax
from jax.experimental import pallas as pl
from jax.experimental.layout import Layout, with_layout_constraint
from jax.experimental.pallas import tpu as pltpu
from jax.sharding import PartitionSpec as P

FIELDS = 5
LEVELS = 24
TEMPER = 2
ENERGY = 4
LVL_ROWS = 8
SLAB = 128
MIB = 1024 * 1024

time_step = 1.0

COS_POLY = (
    0.9999999890590235, -19.739204499453994, 64.93911745989843, -85.45013953092186,
    60.167630951185615, -25.967599249120923, 6.528658161956132,
)
SIN_POLY = (
    6.283185302511506, -41.3417004053176, 81.60513138579954, -76.70301535389986,
    42.02592698629647, -14.89984666973851, 3.2381375126489513,
)


def up_to(value, unit):
    return -(-value // unit) * unit


class Sizes:
    def __init__(self, bands, groups, slots, fields, degrees, rows):
        self.bands, self.groups = bands, groups
        self.slots, self.fields, self.degrees, self.rows = slots, fields, degrees, rows
        self.tiles = degrees // SLAB
        self.slot_rows = fields * self.tiles * 2
        self.field_pad = up_to(fields, 8)
        self.share = -(-fields // groups)
        self.lanes = 4 * self.share
        self.quarters = 2
        if 4 * self.lanes <= SLAB and slots % 4 == 0:
            self.quarters = 4
        self.halves = self.quarters // 2
        self.chunk_live = slots // self.quarters
        self.chunk = up_to(self.chunk_live, 8)
        self.spots = self.quarters * self.chunk
        self.block = slots
        for size in (8, 4):
            if slots % size == 0 and (size * self.slot_rows) % 16 == 0:
                self.block = size
                break
        self.steps = slots // self.block
        self.pairs = self.halves * bands * self.chunk
        self.trunc = degrees - 1
        self.sorted = degrees // 2
        self.orbits = up_to((4 * self.trunc + 40) // 4 + 2, SLAB)
        self.levels = LEVELS // groups


def owners(sizes, field):
    first, last = field * LEVELS, (field + 1) * LEVELS
    return [
        g for g in range(sizes.groups)
        if g * sizes.fields < last and (g + 1) * sizes.fields > first
    ]


def geo_rounds(sizes):
    sources, targets = owners(sizes, TEMPER), owners(sizes, ENERGY)
    wide = max(len(sources), len(targets))
    rounds = []
    for turn in range(wide):
        pairs = []
        for k in range(wide):
            s, t = k, (k + turn) % wide
            if s < len(sources) and t < len(targets):
                pairs.append((sources[s], targets[t]))
        if pairs:
            rounds.append(pairs)
    return rounds


def iota(shape, dim):
    return lax.broadcasted_iota(jnp.int32, shape, dim)


def one_hot(cond):
    return jnp.where(cond, 1.0, 0.0).astype(jnp.bfloat16)


def dot(a, b, dims=((1,), (0,))):
    return lax.dot_general(a, b, (dims, ((), ())), preferred_element_type=jnp.float32)


def halving(value):
    return value.bit_length() - 1 if value & (value - 1) == 0 else None


def quotient(x, by):
    bits = halving(by)
    return x >> bits if bits is not None else lax.div(x, jnp.int32(by))


def remainder(x, by):
    return x & (by - 1) if halving(by) is not None else lax.rem(x, jnp.int32(by))


def spread_matrix(sizes, lev):
    sz = sizes
    tall = sz.quarters * 4 * sz.field_pad
    wide = sz.groups * SLAB
    dst = iota((1, wide), 1)
    group = quotient(dst, SLAB)
    lane = remainder(dst, SLAB)
    quarter = quotient(lane, sz.lanes)
    rest = remainder(lane, sz.lanes)
    row = quotient(rest, 2 * sz.share)
    rest = remainder(rest, 2 * sz.share)
    comp = quotient(rest, sz.share)
    item = remainder(rest, sz.share)
    start = remainder(lev * sz.fields, sz.groups)
    field = remainder(group - start + sz.groups, sz.groups) + sz.groups * item
    want = ((quarter * 2 + row) * sz.field_pad + field) * 2 + comp
    want = jnp.where((field < sz.fields) & (quarter < sz.quarters), want, -1)
    return one_hot(iota((tall, wide), 0) == want)


def inverse_kernel(sizes, rounds, wave, points, gauss, layer_depth, *refs):
    sz = sizes
    x_refs = refs[:sz.tiles]
    leg_ref, send_ref, geo_ref, spots, numbers = refs[sz.tiles:]
    step = pl.program_id(0)
    band = lax.axis_index("band")
    lev = lax.axis_index("lev")
    pad = 2 * sz.field_pad
    live_rows = 2 * sz.fields

    @pl.when(step == 0)
    def _():
        spots[...] = jnp.zeros_like(spots)
        numbers[...] = jnp.full_like(numbers, -1)

    views = [ref.reshape(sz.block, live_rows, SLAB) for ref in x_refs]
    degree = iota((1, sz.degrees), 1)
    for pair in range(sz.block // 2):
        place = step * (sz.block // 2) + pair
        slot = band * sz.slots + 2 * place
        first_odd = wave[slot] & 1
        for side in range(2):
            number = wave[slot + side]
            table = jnp.where(degree >= number, leg_ref[2 * pair + side].astype(jnp.float32), 0.0)
            table = table.astype(jnp.bfloat16)
            total = jnp.zeros((sz.rows, live_rows), jnp.float32)
            for t in range(0, sz.tiles, 2):
                values = jnp.concatenate(
                    [views[tt][2 * pair + side] for tt in range(t, min(t + 2, sz.tiles))], axis=1
                )
                piece = table[:, t * SLAB:t * SLAB + values.shape[1]]
                total += dot(piece, values, ((1,), (1,)))
            odd = first_odd if side == 0 else 1 - first_odd
            half = place // sz.chunk_live
            spot = (odd * sz.halves + half) * sz.chunk + (place - half * sz.chunk_live)
            at = pl.multiple_of(spot * sz.rows, sz.rows)
            spots[pl.ds(at, sz.rows), 0:live_rows] = total
            numbers[pl.ds(spot, 1), :] = jnp.full((1, SLAB), number, jnp.int32)

    @pl.when(step == sz.steps - 1)
    def _():
        spread = spread_matrix(sz, lev)
        shape = (2 * pad, SLAB)
        src, dst = iota(shape, 0), iota(shape, 1)
        from_row, from_field, from_comp = src // pad, (src % pad) >> 1, src & 1
        to_row, to_field, to_comp = dst // pad, (dst % pad) >> 1, dst & 1
        weights = []
        for pairs in rounds:
            first = jnp.int32(2 * LEVELS + sz.fields)
            for source, target in pairs:
                first = jnp.where(lev == source, target * sz.fields - ENERGY * LEVELS, first)
            under = lev * sz.fields + from_field - TEMPER * LEVELS
            above = first + to_field
            hit = (
                (from_row == to_row) & (from_comp == to_comp)
                & (from_field < sz.fields) & (to_field < sz.fields)
                & (above >= 0) & (above <= under)
            )
            weight = jnp.zeros(shape, jnp.float32)
            for level in range(LEVELS):
                weight = jnp.where(hit & (under == level), layer_depth[level], weight)
            high = weight.astype(jnp.bfloat16)
            low = (weight - high.astype(jnp.float32)).astype(jnp.bfloat16)
            weights.append(jnp.concatenate([high, low], axis=0))
        number = numbers[...]
        lane = iota((sz.spots, SLAB), 1)
        known = (number >= 0) & ~((number == 0) & (lane & 1 == 1))
        for rp in range(sz.rows // 2):
            exact = jnp.concatenate([
                spots[pl.ds(2 * rp + r, sz.spots, stride=sz.rows), :][:, 0:pad] for r in range(2)
            ], axis=1)
            cut = jnp.concatenate([
                exact[q * sz.chunk:(q + 1) * sz.chunk] for q in range(sz.quarters)
            ], axis=1).astype(jnp.bfloat16)
            chunk = dot(cut, spread).astype(jnp.bfloat16)
            for g in range(sz.groups):
                send_ref[rp, g] = chunk[:, g * SLAB:(g + 1) * SLAB]
            count = jnp.where(lane < pad, points[2 * rp], points[2 * rp + 1])
            scale = jnp.where(lane < pad, gauss[2 * rp], gauss[2 * rp + 1])
            scale = jnp.where(known & (2 * number <= count - 1), scale, 0.0)
            exact = exact.astype(jnp.bfloat16)
            double = jnp.concatenate([exact, exact], axis=1)
            for turn in range(len(rounds)):
                geo_ref[turn, rp] = (dot(double, weights[turn]) * scale).astype(jnp.bfloat16)


def cos_sin(z):
    y = z * z
    c = jnp.full_like(y, COS_POLY[-1])
    for a in COS_POLY[-2::-1]:
        c = c * y + a
    s = jnp.full_like(y, SIN_POLY[-1])
    for a in SIN_POLY[-2::-1]:
        s = s * y + a
    return c, s * z


def basis_kernel(sizes, points, out_ref, cosines, sines):
    sz = sizes
    step = pl.program_id(0)
    turns = sz.sorted // 16
    bands_row = 16 + up_to(turns, 8)

    @pl.when(step == 0)
    def _():
        first = lax.axis_index("band") * 2
        length_a, length_b = points[first], points[first + 1]
        count_a = length_a // 4 + 1
        high = cosines.shape[0]
        row = iota((high, SLAB), 0)
        number = jnp.where(row < 16, 2 * row, jnp.where(row < bands_row, 32 * (row - 16), sz.trunc))
        number = number.astype(jnp.float32)
        for at in range(0, sz.orbits, SLAB):
            place = iota((1, SLAB), 1) + at
            second = place >= count_a
            column = (place - jnp.where(second, count_a, 0)).astype(jnp.float32)
            length = jnp.where(second, length_b, length_a).astype(jnp.float32)
            inverse = 1.0 / length
            scale = jnp.where(row < 16, 1.0 / jnp.sqrt(length), 1.0)
            product = number * column
            whole = jnp.floor(product * inverse + 0.5)
            c, s = cos_sin((product - whole * length) * inverse)
            cosines[:, pl.ds(at, SLAB)] = c * scale
            sines[:, pl.ds(at, SLAB)] = s * scale

    groups = out_ref.shape[1] // 16
    for at in range(0, sz.orbits, SLAB):
        cols = pl.ds(at, SLAB)
        base_c, base_n = cosines[0:16, cols], -sines[0:16, cols]
        top_c, top_n = cosines[pl.ds(bands_row, 1), cols], -sines[pl.ds(bands_row, 1), cols]
        turn_rows = pl.ds(pl.multiple_of(16 + step * groups, 8), groups)
        all_c, all_s = cosines[turn_rows, cols], sines[turn_rows, cols]
        for k in range(groups):
            turn_c, turn_s = all_c[k:k + 1], all_s[k:k + 1]
            c = turn_c * base_c + turn_s * base_n
            n = turn_c * base_n - turn_s * base_c
            rows = pl.ds(16 * k, 16)
            out_ref[0, rows, cols] = c.astype(jnp.bfloat16)
            out_ref[1, rows, cols] = n.astype(jnp.bfloat16)
            out_ref[2, rows, cols] = (top_c * c + top_n * n).astype(jnp.bfloat16)
            out_ref[3, rows, cols] = (top_n * c - top_c * n).astype(jnp.bfloat16)


def take_matrix(sizes, lev):
    sz = sizes
    tall = sz.groups * SLAB
    wide = sz.quarters * 2 * SLAB
    dst = iota((1, wide), 1)
    piece = quotient(dst, SLAB)
    lane = remainder(dst, SLAB)
    row = quotient(lane, SLAB // 2)
    field = quotient(remainder(lane, SLAB // 2), LVL_ROWS)
    level = remainder(lane, LVL_ROWS)
    whole = field * LEVELS + level * sz.groups + lev
    owner = quotient(whole, sz.fields)
    start = owner * sz.fields
    first = remainder(lev - remainder(start, sz.groups) + sz.groups, sz.groups)
    item = quotient(whole - start - first, sz.groups)
    want = owner * SLAB + (piece >> 1) * sz.lanes + (row * 2 + (piece & 1)) * sz.share + item
    want = jnp.where((field < FIELDS) & (level < sz.levels), want, -1)
    return one_hot(iota((tall, wide), 0) == want)


def grid_kernel(
    sizes, points, gauss, recv_ref, even_row, even_col, basis_hbm, send_ref, basis, terms, arrivals,
):
    sz = sizes
    parts = sz.orbits // SLAB
    copies = []
    for part in range(parts):
        cols = pl.ds(part * SLAB, SLAB)
        copies.append(pltpu.make_async_copy(basis_hbm.at[:, :, cols], basis.at[:, :, cols], arrivals.at[part]))
        copies[-1].start()
    lev = lax.axis_index("lev")
    first_row = lax.axis_index("band") * 2
    length_a, length_b = points[first_row], points[first_row + 1]
    count_a, count_b = length_a // 4 + 1, length_b // 4 + 1
    high = FIELDS * LVL_ROWS
    half_slab = SLAB // 2
    width = sz.bands * sz.chunk
    take = take_matrix(sz, lev)
    order = one_hot(iota((sz.sorted, sz.pairs), 0) * 2 == even_row[...])
    joined = jnp.concatenate([
        recv_ref[:, g].astype(jnp.float32).reshape(width, SLAB) for g in range(sz.groups)
    ], axis=1).astype(jnp.bfloat16)
    taken = dot(joined, take)
    coeffs = []
    number = iota((2 * SLAB, sz.sorted), 1) * 2
    bound = jnp.where(iota((2 * SLAB, sz.sorted), 0) & half_slab == 0, length_a, length_b) - 1
    for parity in range(2):
        rows = []
        for half in range(sz.halves):
            piece = (parity * sz.halves + half) * 2
            rows.append(taken[:, piece * SLAB:(piece + 2) * SLAB])
        values = jnp.concatenate(rows, axis=0).T.astype(jnp.bfloat16)
        placed = dot(values, order, ((1,), (1,)))
        mine = number if parity == 0 else sz.trunc - number
        mult = jnp.where(mine == 0, 1.0, 2.0)
        placed = jnp.where(2 * mine <= bound, placed * mult, 0.0).astype(jnp.bfloat16)
        coeffs += [placed[:SLAB], placed[SLAB:]]
    for part in range(parts):
        copies[part].wait()
        at = part * SLAB
        cols = pl.ds(at, SLAB)
        place = iota((1, SLAB), 1) + at
        second = place >= count_a
        grids = []
        for k in range(4):
            both = dot(coeffs[k], basis[k, :, cols])
            grids.append(jnp.where(second, both[half_slab:half_slab + high], both[:high]))
        ce, se, co, so = grids
        plus, minus = ce + co, ce - co
        splus, sminus = se + so, se - so
        values = (plus + splus, minus - sminus, minus + sminus, plus - splus)
        outs = []
        for v in values:
            u, w, tem, hum, ozo = (v[i * LVL_ROWS:(i + 1) * LVL_ROWS] for i in range(FIELDS))
            outs.append(jnp.concatenate(
                [u * tem, w * tem, u * hum, w * ozo, 0.5 * (u * u + w * w)], axis=0
            ))
        offset = place - jnp.where(second, count_a, 0)
        count = jnp.where(second, count_b, count_a)
        weight = jnp.where((offset == 0) | (offset == count - 1), 0.5, 1.0)
        weight = jnp.where(offset < count, weight, 0.0)
        t0, t1, t2, t3 = (o * weight for o in outs)
        a, b, c, d = t0 + t3, t1 + t2, t0 - t3, t2 - t1
        folds = (a + b, c + d, a - b, c - d)
        empty = jnp.zeros((half_slab - high, SLAB), jnp.float32)
        for k in range(4):
            first = jnp.where(second, 0.0, folds[k])
            last = jnp.where(second, folds[k], 0.0)
            terms[k, :, cols] = jnp.concatenate([first, empty, last, empty], axis=0).astype(jnp.bfloat16)
    lane = iota((1, SLAB), 1)
    scale = jnp.where(lane < half_slab, gauss[first_row], gauss[first_row + 1])
    bound = jnp.where(lane < half_slab, length_a, length_b) - 1
    number = iota((sz.sorted, SLAB), 0) * 2
    back_order = one_hot(iota((sz.pairs, sz.sorted), 1) * 2 == even_col[...])
    pieces = []
    for parity in range(2):
        mine = number if parity == 0 else sz.trunc - number
        sums = jnp.concatenate([
            jnp.where(
                2 * mine <= bound,
                dot(basis[parity * 2 + comp], terms[parity * 2 + comp], ((1,), (1,))) * scale, 0.0,
            ).astype(jnp.bfloat16)
            for comp in range(2)
        ], axis=1)
        slots = dot(back_order, sums).astype(jnp.bfloat16)
        pieces += [slots[half * width:(half + 1) * width] for half in range(sz.halves)]
    sent = dot(jnp.concatenate(pieces, axis=1), take, ((1,), (1,)))
    for g in range(sz.groups):
        part = sent[:, g * SLAB:(g + 1) * SLAB].reshape(sz.bands, sz.chunk, SLAB)
        send_ref[:, g] = part.astype(jnp.bfloat16)


def forward_kernel(
    sizes, wave, speed, back_ref, geo_ref, x_ref, leg_ref, out_ref, wide, spots, inverse, speeds,
):
    sz = sizes
    step = pl.program_id(0)
    band = lax.axis_index("band")
    pad = 2 * sz.field_pad
    height = 2 * sz.slot_rows

    @pl.when(step == 0)
    def _():
        wide[:, pl.ds(height, wide.shape[1] - height), :] = jnp.zeros(
            (wide.shape[0], wide.shape[1] - height, SLAB), jnp.float32
        )
        gather = spread_matrix(sz, lax.axis_index("lev"))
        src, dst = iota((2 * pad, 1), 0), iota((1, 2 * pad), 1)
        place = src & (2 * pad - pad) | ((src & 1) * sz.field_pad) | ((src & (pad - 1)) >> 1)
        sort = one_hot(place == dst)
        for rp in range(sz.rows // 2):
            cut = jnp.concatenate([back_ref[rp, g] for g in range(sz.groups)], axis=1)
            whole = dot(cut, gather, ((1,), (1,)))
            rows = jnp.concatenate([
                whole[:, q * 2 * pad:(q + 1) * 2 * pad] for q in range(sz.quarters)
            ], axis=0)
            for turn in range(geo_ref.shape[0]):
                rows = rows + geo_ref[turn, rp].astype(jnp.float32)[:, 0:2 * pad]
            rows = dot(rows.astype(jnp.bfloat16), sort)
            for r in range(2):
                part = rows[:, r * pad:(r + 1) * pad]
                part = jnp.concatenate([part, jnp.zeros((sz.spots, SLAB - pad), jnp.float32)], axis=1)
                spots[pl.ds(2 * rp + r, sz.spots, stride=sz.rows), :] = part
        speeds[...] = jnp.ones_like(speeds)
        for f in range(sz.fields):
            speeds[pl.ds(f, 1), :] = jnp.full((1, SLAB), speed[f], jnp.float32)
        for t in range(sz.tiles):
            degree = iota((1, SLAB), 1) + t * SLAB
            helm = (degree * (degree + 1)).astype(jnp.float32) / float(sz.trunc * (sz.trunc + 1))
            inverse[t] = 1.0 / (1.0 + time_step * time_step * helm * speeds[...])

    for pair in range(sz.block // 2):
        buf = wide.at[pair % wide.shape[0]]
        buf[pl.ds(0, height), :] = x_ref[pl.ds(pair * height, height), :].astype(jnp.float32)
        place = step * (sz.block // 2) + pair
        slot = band * sz.slots + 2 * place
        first_odd = wave[slot] & 1
        for side in range(2):
            number = wave[slot + side]
            floor = jnp.where(number < 0, sz.degrees, number)
            odd = first_odd if side == 0 else 1 - first_odd
            half = place // sz.chunk_live
            spot = (odd * sz.halves + half) * sz.chunk + (place - half * sz.chunk_live)
            at = pl.multiple_of(spot * sz.rows, sz.rows)
            left = spots[pl.ds(at, sz.rows), :].T.astype(jnp.bfloat16)[0:pad]
            base = (2 * pair + side) * sz.slot_rows
            for t in range(sz.tiles):
                tend = dot(left, leg_ref[2 * pair + side, :, t * SLAB:(t + 1) * SLAB])
                live = iota((1, SLAB), 1) + t * SLAB >= floor
                for c in range(2):
                    old = buf[pl.ds(side * sz.slot_rows + 2 * t + c, sz.field_pad, stride=2 * sz.tiles), :]
                    new = (old + time_step * tend[c * sz.field_pad:(c + 1) * sz.field_pad]) * inverse[t]
                    new = jnp.where(live, new, 0.0)
                    out_ref[pl.ds(base + 2 * t + c, sz.fields, stride=2 * sz.tiles), :] = new[0:sz.fields]


def params(mib):
    return pltpu.CompilerParams(vmem_limit_bytes=mib * MIB)


def smem():
    return pl.BlockSpec(memory_space=pltpu.SMEM)


def whole_block(shape):
    return pl.BlockSpec(shape, lambda *_: (0,) * len(shape))


def shards(spectra, legendre, slot_wave, row_points, gauss_weight, layer_depth, mode_speed):
    slots, _, fields, degrees = spectra.shape
    rows = legendre.shape[2]
    sz = Sizes(lax.axis_size("band"), lax.axis_size("lev"), slots, fields, degrees, rows)

    tiled = spectra.reshape(slots, 2, fields, sz.tiles, SLAB)
    tiled = with_layout_constraint(tiled, Layout((0, 2, 3, 1, 4)))
    tiled = tiled.transpose(0, 2, 3, 1, 4)
    lines = tiled.reshape(slots * sz.slot_rows, SLAB)
    tables = legendre.transpose(0, 2, 1)

    rounds = geo_rounds(sz)
    tail = up_to((sz.field_pad - sz.fields) * 2 * sz.tiles, 16)
    wide_shape = pltpu.VMEM((2, 2 * sz.slot_rows + tail, SLAB), jnp.float32)
    spots_shape = pltpu.VMEM((sz.spots * sz.rows, SLAB), jnp.float32)
    lines_block = (sz.block * sz.slot_rows, SLAB)
    table_block = (sz.block, sz.rows, degrees)
    send_shape = (sz.bands, sz.groups, sz.chunk, SLAB)
    geo_shape = (len(rounds), sz.rows // 2, sz.spots, SLAB)

    def tile_spec(t):
        return pl.BlockSpec((sz.block, fields, 1, 2, SLAB), lambda i: (i, 0, t, 0, 0))

    sent, geo = pl.pallas_call(
        functools.partial(inverse_kernel, sz, rounds),
        grid=(sz.steps,),
        in_specs=[smem(), smem(), smem(), smem()]
        + [tile_spec(t) for t in range(sz.tiles)]
        + [pl.BlockSpec(table_block, lambda i: (i, 0, 0))],
        out_specs=[whole_block(send_shape), whole_block(geo_shape)],
        out_shape=[
            jax.ShapeDtypeStruct(send_shape, jnp.bfloat16),
            jax.ShapeDtypeStruct(geo_shape, jnp.bfloat16),
        ],
        scratch_shapes=[spots_shape, pltpu.VMEM((sz.spots, SLAB), jnp.int32)],
        compiler_params=params(56),
        name="inverse_legendre",
    )(slot_wave, row_points, gauss_weight, layer_depth, *([tiled] * sz.tiles), tables)

    both = ("band", "lev")
    total = sz.bands * sz.groups
    flat = (total * sz.chunk, SLAB)
    arrived = lax.all_to_all(sent.reshape(flat), both, split_axis=0, concat_axis=0, tiled=True)

    pair_wave = slot_wave.reshape(-1, 2)
    even_wave = jnp.where(pair_wave[:, 0] % 2 == 0, pair_wave[:, 0], pair_wave[:, 1])
    even_wave = even_wave.reshape(sz.bands, sz.halves, sz.chunk_live)
    even_wave = jnp.pad(even_wave, ((0, 0), (0, 0), (0, sz.chunk - sz.chunk_live)), constant_values=-1)
    even_wave = even_wave.transpose(1, 0, 2).reshape(sz.pairs)

    high = SLAB if sz.sorted % SLAB == 0 else sz.sorted
    table_rows = 16 + up_to(sz.sorted // 16, 8) + 8
    basis = pl.pallas_call(
        functools.partial(basis_kernel, sz),
        grid=(sz.sorted // high,),
        in_specs=[smem()],
        out_specs=pl.BlockSpec((4, high, sz.orbits), lambda i: (0, i, 0)),
        out_shape=jax.ShapeDtypeStruct((4, sz.sorted, sz.orbits), jnp.bfloat16),
        scratch_shapes=[pltpu.VMEM((table_rows, sz.orbits), jnp.float32)] * 2,
        compiler_params=params(56),
        cost_estimate=pl.CostEstimate(
            flops=20 * sz.sorted * sz.orbits, bytes_accessed=8 * sz.sorted * sz.orbits, transcendentals=0,
        ),
        name="basis",
    )(row_points)

    geo, arrived = lax.optimization_barrier((geo, arrived))
    moved = [lax.ppermute(geo[turn], "lev", pairs) for turn, pairs in enumerate(rounds)]
    vmem = pl.BlockSpec(memory_space=pltpu.VMEM)
    returned = pl.pallas_call(
        functools.partial(grid_kernel, sz),
        in_specs=[smem(), smem(), vmem, vmem, vmem, pl.BlockSpec(memory_space=pl.ANY)],
        out_specs=vmem,
        out_shape=jax.ShapeDtypeStruct(send_shape, jnp.bfloat16),
        scratch_shapes=[
            pltpu.VMEM((4, sz.sorted, sz.orbits), jnp.bfloat16),
            pltpu.VMEM((4, SLAB, sz.orbits), jnp.bfloat16),
            pltpu.SemaphoreType.DMA((sz.orbits // SLAB,)),
        ],
        compiler_params=params(56),
        cost_estimate=pl.CostEstimate(
            flops=4 * 4 * SLAB * sz.sorted * sz.orbits, bytes_accessed=8 * sz.sorted * sz.orbits, transcendentals=0,
        ),
        name="grid_products",
    )(
        row_points, gauss_weight, arrived.reshape(send_shape),
        even_wave.reshape(1, sz.pairs), even_wave.reshape(sz.pairs, 1), basis,
    )
    *moved, returned = lax.optimization_barrier((*moved, returned))

    back = lax.all_to_all(returned.reshape(flat), both, split_axis=0, concat_axis=0, tiled=True)

    out = pl.pallas_call(
        functools.partial(forward_kernel, sz),
        grid=(sz.steps,),
        in_specs=[
            smem(), smem(),
            whole_block(send_shape), whole_block(geo_shape),
            pl.BlockSpec(lines_block, lambda i: (i, 0)),
            pl.BlockSpec(table_block, lambda i: (i, 0, 0)),
        ],
        out_specs=pl.BlockSpec(lines_block, lambda i: (i, 0)),
        out_shape=jax.ShapeDtypeStruct((slots * sz.slot_rows, SLAB), jnp.float32),
        scratch_shapes=[
            wide_shape, spots_shape,
            pltpu.VMEM((sz.tiles, sz.field_pad, SLAB), jnp.float32),
            pltpu.VMEM((sz.field_pad, SLAB), jnp.float32),
        ],
        compiler_params=params(56),
        name="forward_legendre",
    )(slot_wave, mode_speed, back.reshape(send_shape), jnp.stack(moved), lines, tables)

    out = out.reshape(slots, fields, sz.tiles, 2, SLAB).transpose(0, 1, 3, 2, 4)
    return out.reshape(slots, fields, 2, degrees).transpose(0, 2, 1, 3)


def solution(mesh):
    return jax.shard_map(
        shards,
        mesh=mesh,
        in_specs=(
            P("band", None, "lev", None),
            P("band", None, None),
            P(),
            P(),
            P(),
            P(),
            P("lev"),
        ),
        out_specs=P("band", None, "lev", None),
        check_vma=False,
    )
```

time: 132 us -> 120 us (0.909)
  waiting for transfers between devices: 10.4 us -> 22.3 us
  local copies, waits for them, and re-layouts: 16.2 us -> 4.3 us
  Pallas kernels: 87.5 us -> 78.1 us
  starting transfers between devices: 14.5 us -> 12.5 us
    pallas_call x2, Pallas kernels: 46.2 us -> 30.4 us  [the longest x1 24.8 us: shards(): pl.pallas_call(functools.partial(inverse_kernel, sz, rounds), grid=(sz.st...]
    all_to_all x1, waiting for transfers between devices: 0.01 us -> 11.2 us  [shards(): lax.all_to_all(sent.reshape(flat), both, split_axis=0, concat_axis=0, til...]
    unnamed x18 -> x6, local copies, waits for them, and re-layouts: 11.8 us -> 0.73 us
    pallas_call x1, Pallas kernels: 33.5 us -> 37.2 us  [shards(): pl.pallas_call(functools.partial(forward_kernel, sz), grid=(sz.steps,), i...]
    pallas_call x1, Pallas kernels: 7.86 us -> 10.5 us  [shards(): pl.pallas_call(functools.partial(grid_kernel, sz), in_specs=[smem(), smem...]
    all_to_all x1, starting transfers between devices: 5.83 us -> 3.87 us  [shards(): lax.all_to_all(returned.reshape(flat), both, split_axis=0, concat_axis=0,...]
    another operation x2, local copies, waits for them, and re-layouts: 0.12 us -> 1.55 us  [the longest x1 0.88 us: shards(): even_wave.reshape(sz.pairs, 1)]
  transfers between devices with their start and end apart: 4 -> 4, of which waited for: 1 -> 2; matrix products, arithmetic and copies ran while one was open for 1% -> 3% of each run, Pallas kernels for 19% -> 14%
where the time goes in v2:
time: 120 us; the launch traced here: 118 us
  Pallas kernels  78.1 us (65%)
  waiting for transfers between devices  22.3 us (19%)
  starting transfers between devices  12.5 us (10%)
  local copies, waits for them, and re-layouts  4.3 us (4%)
    pallas_call x1, Pallas kernels, shards(): pl.pallas_call(functools.partial(forward_kernel, sz), grid=(sz.steps,), i...  37.2 us
    pallas_call x1, Pallas kernels, shards(): pl.pallas_call(functools.partial(inverse_kernel, sz, rounds), grid=(sz.st...  24.8 us
    all_to_all x1, waiting for transfers between devices, shards(): lax.all_to_all(sent.reshape(flat), both, split_axis=0, concat_axis=0, til...  11.2 us
    all_to_all x1, waiting for transfers between devices, shards(): lax.all_to_all(returned.reshape(flat), both, split_axis=0, concat_axis=0,...  11.1 us
    pallas_call x1, Pallas kernels, shards(): pl.pallas_call(functools.partial(grid_kernel, sz), in_specs=[smem(), smem...  10.5 us
    all_to_all x1, starting transfers between devices, shards(): lax.all_to_all(sent.reshape(flat), both, split_axis=0, concat_axis=0, til...  7.3 us
    pallas_call x1, Pallas kernels, shards(): pl.pallas_call(functools.partial(basis_kernel, sz), grid=(sz.sorted // hi...  5.64 us
    all_to_all x1, starting transfers between devices, shards(): lax.all_to_all(returned.reshape(flat), both, split_axis=0, concat_axis=0,...  3.87 us
  transfers between devices with their start and end apart: 4, of which 2 were waited for; matrix products, arithmetic and copies ran while one was open for 3% of the time, Pallas kernels for 14%

profile of v2, /device:TPU:0, one launch (start us, length us, event | category | flops | bytes accessed | tf_op | source)
XLA Modules:
  0.0 118.2 jit_solution(7440160126230590181)
XLA Ops:
  0.0 0.0 copy-start.2
  0.0 24.8 %inverse_legendre.1 = (bf16[8,4,40,128]{3,2,1,0:T(8,128)(2,1)}, bf16[2,8,160,128]{3,2,1,0:T(8,128)(2,1)}) custom-call(s32[1280]{0:T(1024)} %wave.3, s32[16]{0:T(128)} %points.5, f32[16]{0:T(128)} %gauss.3, f32[24]{0:T(128)} %layer_depth.1, bf16[160,30,10,2,128]{4,3,2,1,0:T(2,128)(2,1)} %bitcast.26, bf16[160,30,10,2,128]{4,3,2,1,0:T(2,128)(2,1)} %bitcast.27, ...), custom_call_target="tpu_custom_call" | custom-call | tf_op jit(solution)/shard_map/inverse_legendre/pallas_call | solution.py:487
  24.8 7.3 %all-to-all-start = ((bf16[32,40,128]{2,1,0:T(8,128)(2,1)}), bf16[32,40,128]{2,1,0:T(8,128)(2,1)S(1)}, u32[]{:S(2)}, u32[]{:S(2)}) async-start(bf16[32,40,128]{2,1,0:T(8,128)(2,1)} %bitcast.44), calls=%async_computation | async-start | bytes 655360 | tf_op jit(solution)/shard_map/all_to_all | solution.py:506
  32.1 0.0 copy-done.2
  32.1 0.3 reshape.35
  32.4 0.3 slice_reduce_fusion
  32.7 0.1 squeeze.16
  32.8 0.1 squeeze.15
  32.9 11.2 %all-to-all-done = bf16[32,40,128]{2,1,0:T(8,128)(2,1)S(1)} async-done(((bf16[32,40,128]{2,1,0:T(8,128)(2,1)}), bf16[32,40,128]{2,1,0:T(8,128)(2,1)S(1)}, u32[]{:S(2)}, u32[]{:S(2)}) %all-to-all-start) | async-done | bytes 327712 | tf_op jit(solution)/shard_map/all_to_all | solution.py:506
  44.1 0.0 copy-start.1
  44.1 1.2 %slice_bitcast_fusion = (bf16[8,160,128]{2,1,0:T(8,128)(2,1)S(1)}, bf16[8,160,128]{2,1,0:T(8,128)(2,1)S(1)}) fusion(bf16[2,8,160,128]{3,2,1,0:T(8,128)(2,1)} %get-tuple-element.14), kind=kLoop, calls=%fused_computation.3 | loop fusion | bytes 1310720 | tf_op jit(solution)/shard_map/squeeze | solution.py:531
  45.3 0.7 collective-permute-start.1
  46.0 0.7 collective-permute-start
  46.8 0.7 reshape_reshape.6.even_row
  47.4 0.9 reshape_reshape.8.even_col
  48.3 5.6 %basis.1.basis_hbm = bf16[4,640,1408]{2,1,0:T(8,128)(2,1)} custom-call(s32[16]{0:T(128)} %points.5), custom_call_target="tpu_custom_call" | custom-call | flops 18022400 | bytes 7208960 | tf_op jit(solution)/shard_map/basis/pallas_call | solution.py:516
  53.9 0.0 copy-done.1
  53.9 10.5 %grid_products.1 = bf16[8,4,40,128]{3,2,1,0:T(8,128)(2,1)} custom-call(s32[16]{0:T(128)} %points.5, f32[16]{0:T(128)} %gauss.3, bf16[8,4,40,128]{3,2,1,0:T(8,128)(2,1)} %bitcast.40, s32[1,640]{1,0:T(1,128)} %reshape_reshape.6.even_row, s32[640,1]{1,0:T(8,128)} %reshape_reshape.8.even_col, bf16[4,640,1408]{2,1,0:T(8,128)(2,1)} %basis.1.basis_hbm), custom_call_target="tpu_custom_call" | custom-call | flops 1845493760 | bytes 7208960 | tf_op jit(solution)/shard_map/grid_products/pallas_call | solution.py:533
  64.4 0.0 collective-permute-done.1
  64.5 0.0 collective-permute-done
  64.5 3.9 %all-to-all-start.1 = ((bf16[32,40,128]{2,1,0:T(8,128)(2,1)}), bf16[32,40,128]{2,1,0:T(8,128)(2,1)S(1)}, u32[]{:S(2)}, u32[]{:S(2)}) async-start(bf16[32,40,128]{2,1,0:T(8,128)(2,1)} %bitcast.41), calls=%async_computation.1 | async-start | bytes 655360 | tf_op jit(solution)/shard_map/all_to_all | solution.py:554
  68.3 0.9 pad_maximum_fusion.geo_ref
  69.2 11.1 %all-to-all-done.1 = bf16[32,40,128]{2,1,0:T(8,128)(2,1)S(1)} async-done(((bf16[32,40,128]{2,1,0:T(8,128)(2,1)}), bf16[32,40,128]{2,1,0:T(8,128)(2,1)S(1)}, u32[]{:S(2)}, u32[]{:S(2)}) %all-to-all-start.1) | async-done | bytes 327712 | tf_op jit(solution)/shard_map/all_to_all | solution.py:554
  80.3 0.0 copy-start
  80.3 0.7 copy-done
  81.1 37.2 %forward_legendre.1 = f32[96000,128]{1,0:T(8,128)} custom-call(s32[1280]{0:T(1024)} %wave.3, f32[30]{0:T(128)} %speed.1, bf16[8,4,40,128]{3,2,1,0:T(8,128)(2,1)} %bitcast.39, bf16[2,8,160,128]{3,2,1,0:T(8,128)(2,1)} %pad_maximum_fusion.geo_ref, bf16[96000,128]{1,0:T(8,128)(2,1)} %bitcast.36, bf16[160,16,1280]{2,1,0:T(8,128)(2,1)} %bitcast.38), custom_call_target="tpu_custom_call" | custom-call | tf_op jit(solution)/shard_map/forward_legendre/pallas_call | solution.py:556
  (2 shorter events, 0.0 us)
Async XLA Ops:
  0.0 32.1 %copy-start.2 = (s32[1280]{0:T(1024)S(1)}, s32[1280]{0:T(1024)}, u32[]{:S(2)}) copy-start(s32[1280]{0:T(1024)} %wave.3) | copy-start | bytes 15364
  24.8 19.3 %all-to-all-start = ((bf16[32,40,128]{2,1,0:T(8,128)(2,1)}), bf16[32,40,128]{2,1,0:T(8,128)(2,1)S(1)}, u32[]{:S(2)}, u32[]{:S(2)}) async-start(bf16[32,40,128]{2,1,0:T(8,128)(2,1)} %bitcast.44), calls=%async_computation | async-start | bytes 655360 | tf_op jit(solution)/shard_map/all_to_all | solution.py:506
  44.1 9.8 %copy-start.1 = (bf16[32,40,128]{2,1,0:T(8,128)(2,1)}, bf16[32,40,128]{2,1,0:T(8,128)(2,1)S(1)}, u32[]{:S(2)}) copy-start(bf16[32,40,128]{2,1,0:T(8,128)(2,1)S(1)} %all-to-all-done) | copy-start | bytes 983044
  45.3 19.1 %collective-permute-start.1 = (bf16[8,160,128]{2,1,0:T(8,128)(2,1)S(1)}, bf16[8,160,128]{2,1,0:T(8,128)(2,1)S(1)}, u32[]{:S(2)}, u32[]{:S(2)}) collective-permute-start(bf16[8,160,128]{2,1,0:T(8,128)(2,1)S(1)} %get-tuple-element.21), channel_id=1, source_target_pairs={{2,3},{6,7},{10,11},{14,15},{18,19},{22,23},{26,27},{30,31}} | collective-permute-start | bytes 983048 | tf_op jit(solution)/shard_map/ppermute | solution.py:531
  46.0 18.4 %collective-permute-start = (bf16[8,160,128]{2,1,0:T(8,128)(2,1)S(1)}, bf16[8,160,128]{2,1,0:T(8,128)(2,1)S(1)}, u32[]{:S(2)}, u32[]{:S(2)}) collective-permute-start(bf16[8,160,128]{2,1,0:T(8,128)(2,1)S(1)} %get-tuple-element.22), channel_id=1, source_target_pairs={{1,3},{5,7},{9,11},{13,15},{17,19},{21,23},{25,27},{29,31}} | collective-permute-start | bytes 983048 | tf_op jit(solution)/shard_map/ppermute | solution.py:531
  64.5 15.9 %all-to-all-start.1 = ((bf16[32,40,128]{2,1,0:T(8,128)(2,1)}), bf16[32,40,128]{2,1,0:T(8,128)(2,1)S(1)}, u32[]{:S(2)}, u32[]{:S(2)}) async-start(bf16[32,40,128]{2,1,0:T(8,128)(2,1)} %bitcast.41), calls=%async_computation.1 | async-start | bytes 655360 | tf_op jit(solution)/shard_map/all_to_all | solution.py:554
  80.3 0.7 copy-start

commit v3 on v2

--- a/solution.py
+++ b/solution.py
@@ -125,29 +125,39 @@
     item = remainder(rest, sz.share)
     start = remainder(lev * sz.fields, sz.groups)
     field = remainder(group - start + sz.groups, sz.groups) + sz.groups * item
-    want = ((quarter * 2 + row) * sz.field_pad + field) * 2 + comp
+    want = ((quarter * 2 + row) * 2 + comp) * sz.field_pad + field
     want = jnp.where((field < sz.fields) & (quarter < sz.quarters), want, -1)
     return one_hot(iota((tall, wide), 0) == want)
 
 
-def inverse_kernel(sizes, rounds, wave, points, gauss, layer_depth, *refs):
+def spot_of(sizes, place, odd):
+    half = place // sizes.chunk_live
+    return (odd * sizes.halves + half) * sizes.chunk + (place - half * sizes.chunk_live)
+
+
+def inverse_kernel(sizes, rounds, wave, points, gauss, layer_depth, x_ref, leg_ref, send_ref, *refs):
     sz = sizes
-    x_refs = refs[:sz.tiles]
-    leg_ref, send_ref, geo_ref, spots, numbers = refs[sz.tiles:]
+    geo_refs = refs[:len(rounds)]
+    wide, spots, numbers = refs[len(rounds):]
     step = pl.program_id(0)
     band = lax.axis_index("band")
     lev = lax.axis_index("lev")
     pad = 2 * sz.field_pad
-    live_rows = 2 * sz.fields
+    height = 2 * sz.slot_rows
 
     @pl.when(step == 0)
     def _():
         spots[...] = jnp.zeros_like(spots)
         numbers[...] = jnp.full_like(numbers, -1)
-
-    views = [ref.reshape(sz.block, live_rows, SLAB) for ref in x_refs]
+        wide[:, pl.ds(height, wide.shape[1] - height), :] = jnp.zeros(
+            (wide.shape[0], wide.shape[1] - height, SLAB), jnp.float32
+        )
+
     degree = iota((1, sz.degrees), 1)
+    found = []
     for pair in range(sz.block // 2):
+        buf = wide.at[pair % wide.shape[0]]
+        buf[pl.ds(0, height), :] = x_ref[pl.ds(pair * height, height), :].astype(jnp.float32)
         place = step * (sz.block // 2) + pair
         slot = band * sz.slots + 2 * place
         first_odd = wave[slot] & 1
@@ -155,27 +165,32 @@
             number = wave[slot + side]
             table = jnp.where(degree >= number, leg_ref[2 * pair + side].astype(jnp.float32), 0.0)
             table = table.astype(jnp.bfloat16)
-            total = jnp.zeros((sz.rows, live_rows), jnp.float32)
+            total = jnp.zeros((sz.rows, pad), jnp.float32)
             for t in range(0, sz.tiles, 2):
-                values = jnp.concatenate(
-                    [views[tt][2 * pair + side] for tt in range(t, min(t + 2, sz.tiles))], axis=1
-                )
+                parts = []
+                for tt in range(t, min(t + 2, sz.tiles)):
+                    first = side * sz.slot_rows + 2 * tt
+                    parts.append(jnp.concatenate([
+                        buf[pl.ds(first + c, sz.field_pad, stride=2 * sz.tiles), :] for c in range(2)
+                    ], axis=0).astype(jnp.bfloat16))
+                values = jnp.concatenate(parts, axis=1)
                 piece = table[:, t * SLAB:t * SLAB + values.shape[1]]
                 total += dot(piece, values, ((1,), (1,)))
             odd = first_odd if side == 0 else 1 - first_odd
-            half = place // sz.chunk_live
-            spot = (odd * sz.halves + half) * sz.chunk + (place - half * sz.chunk_live)
-            at = pl.multiple_of(spot * sz.rows, sz.rows)
-            spots[pl.ds(at, sz.rows), 0:live_rows] = total
-            numbers[pl.ds(spot, 1), :] = jnp.full((1, SLAB), number, jnp.int32)
+            found.append((spot_of(sz, place, odd), number, total))
+    for spot, number, total in found:
+        at = pl.multiple_of(spot * sz.rows, sz.rows)
+        spots[pl.ds(at, sz.rows), 0:pad] = total
+        numbers[pl.ds(spot, 1), :] = jnp.full((1, SLAB), number, jnp.int32)
 
     @pl.when(step == sz.steps - 1)
     def _():
         spread = spread_matrix(sz, lev)
         shape = (2 * pad, SLAB)
         src, dst = iota(shape, 0), iota(shape, 1)
-        from_row, from_field, from_comp = src // pad, (src % pad) >> 1, src & 1
-        to_row, to_field, to_comp = dst // pad, (dst % pad) >> 1, dst & 1
+        bits = sz.field_pad.bit_length() - 1
+        from_field, from_side = src & (sz.field_pad - 1), src >> bits
+        to_field, to_side = dst & (sz.field_pad - 1), dst >> bits
         weights = []
         for pairs in rounds:
             first = jnp.int32(2 * LEVELS + sz.fields)
@@ -184,7 +199,7 @@
             under = lev * sz.fields + from_field - TEMPER * LEVELS
             above = first + to_field
             hit = (
-                (from_row == to_row) & (from_comp == to_comp)
+                (from_side == to_side)
                 & (from_field < sz.fields) & (to_field < sz.fields)
                 & (above >= 0) & (above <= under)
             )
@@ -196,7 +211,7 @@
             weights.append(jnp.concatenate([high, low], axis=0))
         number = numbers[...]
         lane = iota((sz.spots, SLAB), 1)
-        known = (number >= 0) & ~((number == 0) & (lane & 1 == 1))
+        known = (number >= 0) & ~((number == 0) & (lane & sz.field_pad != 0))
         for rp in range(sz.rows // 2):
             exact = jnp.concatenate([
                 spots[pl.ds(2 * rp + r, sz.spots, stride=sz.rows), :][:, 0:pad] for r in range(2)
@@ -213,7 +228,7 @@
             exact = exact.astype(jnp.bfloat16)
             double = jnp.concatenate([exact, exact], axis=1)
             for turn in range(len(rounds)):
-                geo_ref[turn, rp] = (dot(double, weights[turn]) * scale).astype(jnp.bfloat16)
+                geo_refs[turn][rp] = (dot(double, weights[turn]) * scale).astype(jnp.bfloat16)
 
 
 def cos_sin(z):
@@ -297,10 +312,11 @@
     sizes, points, gauss, recv_ref, even_row, even_col, basis_hbm, send_ref, basis, terms, arrivals,
 ):
     sz = sizes
-    parts = sz.orbits // SLAB
+    step = 2 * SLAB
+    parts = -(-sz.orbits // step)
     copies = []
     for part in range(parts):
-        cols = pl.ds(part * SLAB, SLAB)
+        cols = pl.ds(part * step, min(step, sz.orbits - part * step))
         copies.append(pltpu.make_async_copy(basis_hbm.at[:, :, cols], basis.at[:, :, cols], arrivals.at[part]))
         copies[-1].start()
     lev = lax.axis_index("lev")
@@ -319,6 +335,7 @@
     coeffs = []
     number = iota((2 * SLAB, sz.sorted), 1) * 2
     bound = jnp.where(iota((2 * SLAB, sz.sorted), 0) & half_slab == 0, length_a, length_b) - 1
+    kept = (0, half_slab, SLAB, SLAB + half_slab)
     for parity in range(2):
         rows = []
         for half in range(sz.halves):
@@ -328,18 +345,20 @@
         placed = dot(values, order, ((1,), (1,)))
         mine = number if parity == 0 else sz.trunc - number
         mult = jnp.where(mine == 0, 1.0, 2.0)
-        placed = jnp.where(2 * mine <= bound, placed * mult, 0.0).astype(jnp.bfloat16)
-        coeffs += [placed[:SLAB], placed[SLAB:]]
+        placed = jnp.where(2 * mine <= bound, placed * mult, 0.0)
+        placed = jnp.concatenate([placed[k:k + high] for k in kept], axis=0).astype(jnp.bfloat16)
+        coeffs += [placed[:2 * high], placed[2 * high:]]
     for part in range(parts):
         copies[part].wait()
-        at = part * SLAB
-        cols = pl.ds(at, SLAB)
-        place = iota((1, SLAB), 1) + at
+        at = part * step
+        many = min(step, sz.orbits - at)
+        cols = pl.ds(at, many)
+        place = iota((1, many), 1) + at
         second = place >= count_a
         grids = []
         for k in range(4):
             both = dot(coeffs[k], basis[k, :, cols])
-            grids.append(jnp.where(second, both[half_slab:half_slab + high], both[:high]))
+            grids.append(jnp.where(second, both[high:], both[:high]))
         ce, se, co, so = grids
         plus, minus = ce + co, ce - co
         splus, sminus = se + so, se - so
@@ -357,7 +376,7 @@
         t0, t1, t2, t3 = (o * weight for o in outs)
         a, b, c, d = t0 + t3, t1 + t2, t0 - t3, t2 - t1
         folds = (a + b, c + d, a - b, c - d)
-        empty = jnp.zeros((half_slab - high, SLAB), jnp.float32)
+        empty = jnp.zeros((half_slab - high, many), jnp.float32)
         for k in range(4):
             first = jnp.where(second, 0.0, folds[k])
             last = jnp.where(second, folds[k], 0.0)
@@ -386,9 +405,10 @@
 
 
 def forward_kernel(
-    sizes, wave, speed, back_ref, geo_ref, x_ref, leg_ref, out_ref, wide, spots, inverse, speeds,
+    sizes, wave, speed, back_ref, *refs,
 ):
     sz = sizes
+    *geo_refs, x_ref, leg_ref, out_ref, wide, spots, inverse, speeds = refs
     step = pl.program_id(0)
     band = lax.axis_index("band")
     pad = 2 * sz.field_pad
@@ -400,18 +420,14 @@
             (wide.shape[0], wide.shape[1] - height, SLAB), jnp.float32
         )
         gather = spread_matrix(sz, lax.axis_index("lev"))
-        src, dst = iota((2 * pad, 1), 0), iota((1, 2 * pad), 1)
-        place = src & (2 * pad - pad) | ((src & 1) * sz.field_pad) | ((src & (pad - 1)) >> 1)
-        sort = one_hot(place == dst)
         for rp in range(sz.rows // 2):
             cut = jnp.concatenate([back_ref[rp, g] for g in range(sz.groups)], axis=1)
             whole = dot(cut, gather, ((1,), (1,)))
             rows = jnp.concatenate([
                 whole[:, q * 2 * pad:(q + 1) * 2 * pad] for q in range(sz.quarters)
             ], axis=0)
-            for turn in range(geo_ref.shape[0]):
-                rows = rows + geo_ref[turn, rp].astype(jnp.float32)[:, 0:2 * pad]
-            rows = dot(rows.astype(jnp.bfloat16), sort)
+            for geo_ref in geo_refs:
+                rows = rows + geo_ref[rp].astype(jnp.float32)[:, 0:2 * pad]
             for r in range(2):
                 part = rows[:, r * pad:(r + 1) * pad]
                 part = jnp.concatenate([part, jnp.zeros((sz.spots, SLAB - pad), jnp.float32)], axis=1)
@@ -424,9 +440,8 @@
             helm = (degree * (degree + 1)).astype(jnp.float32) / float(sz.trunc * (sz.trunc + 1))
             inverse[t] = 1.0 / (1.0 + time_step * time_step * helm * speeds[...])
 
+    work = []
     for pair in range(sz.block // 2):
-        buf = wide.at[pair % wide.shape[0]]
-        buf[pl.ds(0, height), :] = x_ref[pl.ds(pair * height, height), :].astype(jnp.float32)
         place = step * (sz.block // 2) + pair
         slot = band * sz.slots + 2 * place
         first_odd = wave[slot] & 1
@@ -434,19 +449,27 @@
             number = wave[slot + side]
             floor = jnp.where(number < 0, sz.degrees, number)
             odd = first_odd if side == 0 else 1 - first_odd
-            half = place // sz.chunk_live
-            spot = (odd * sz.halves + half) * sz.chunk + (place - half * sz.chunk_live)
-            at = pl.multiple_of(spot * sz.rows, sz.rows)
-            left = spots[pl.ds(at, sz.rows), :].T.astype(jnp.bfloat16)[0:pad]
+            at = pl.multiple_of(spot_of(sz, place, odd) * sz.rows, sz.rows)
+            work.append((floor, spots[pl.ds(at, sz.rows), :].T.astype(jnp.bfloat16)[0:pad]))
+
+    for pair in range(sz.block // 2):
+        buf = wide.at[pair % wide.shape[0]]
+        buf[pl.ds(0, height), :] = x_ref[pl.ds(pair * height, height), :].astype(jnp.float32)
+        for side in range(2):
+            floor, left = work[2 * pair + side]
             base = (2 * pair + side) * sz.slot_rows
-            for t in range(sz.tiles):
-                tend = dot(left, leg_ref[2 * pair + side, :, t * SLAB:(t + 1) * SLAB])
-                live = iota((1, SLAB), 1) + t * SLAB >= floor
-                for c in range(2):
-                    old = buf[pl.ds(side * sz.slot_rows + 2 * t + c, sz.field_pad, stride=2 * sz.tiles), :]
-                    new = (old + time_step * tend[c * sz.field_pad:(c + 1) * sz.field_pad]) * inverse[t]
-                    new = jnp.where(live, new, 0.0)
-                    out_ref[pl.ds(base + 2 * t + c, sz.fields, stride=2 * sz.tiles), :] = new[0:sz.fields]
+            for first in range(0, sz.tiles, 2):
+                count = min(2, sz.tiles - first)
+                tends = dot(left, leg_ref[2 * pair + side, :, first * SLAB:(first + count) * SLAB])
+                for t in range(first, first + count):
+                    tend = tends[:, (t - first) * SLAB:(t - first + 1) * SLAB]
+                    live = iota((1, SLAB), 1) + t * SLAB >= floor
+                    for c in range(2):
+                        rows = pl.ds(side * sz.slot_rows + 2 * t + c, sz.field_pad, stride=2 * sz.tiles)
+                        new = buf[rows, :] + time_step * tend[c * sz.field_pad:(c + 1) * sz.field_pad]
+                        new = jnp.where(live, new * inverse[t], 0.0)
+                        rows = pl.ds(base + 2 * t + c, sz.fields, stride=2 * sz.tiles)
+                        out_ref[rows, :] = new[0:sz.fields]
 
 
 def params(mib):
@@ -468,44 +491,41 @@
 
     tiled = spectra.reshape(slots, 2, fields, sz.tiles, SLAB)
     tiled = with_layout_constraint(tiled, Layout((0, 2, 3, 1, 4)))
-    tiled = tiled.transpose(0, 2, 3, 1, 4)
-    lines = tiled.reshape(slots * sz.slot_rows, SLAB)
+    lines = tiled.transpose(0, 2, 3, 1, 4).reshape(slots * sz.slot_rows, SLAB)
     tables = legendre.transpose(0, 2, 1)
 
     rounds = geo_rounds(sz)
     tail = up_to((sz.field_pad - sz.fields) * 2 * sz.tiles, 16)
-    wide_shape = pltpu.VMEM((2, 2 * sz.slot_rows + tail, SLAB), jnp.float32)
+    wide_shape = pltpu.VMEM((4, 2 * sz.slot_rows + tail, SLAB), jnp.float32)
     spots_shape = pltpu.VMEM((sz.spots * sz.rows, SLAB), jnp.float32)
     lines_block = (sz.block * sz.slot_rows, SLAB)
     table_block = (sz.block, sz.rows, degrees)
     send_shape = (sz.bands, sz.groups, sz.chunk, SLAB)
-    geo_shape = (len(rounds), sz.rows // 2, sz.spots, SLAB)
-
-    def tile_spec(t):
-        return pl.BlockSpec((sz.block, fields, 1, 2, SLAB), lambda i: (i, 0, t, 0, 0))
-
-    sent, geo = pl.pallas_call(
+    geo_shape = (sz.rows // 2, sz.spots, SLAB)
+
+    sent, *geo = pl.pallas_call(
         functools.partial(inverse_kernel, sz, rounds),
         grid=(sz.steps,),
-        in_specs=[smem(), smem(), smem(), smem()]
-        + [tile_spec(t) for t in range(sz.tiles)]
-        + [pl.BlockSpec(table_block, lambda i: (i, 0, 0))],
-        out_specs=[whole_block(send_shape), whole_block(geo_shape)],
-        out_shape=[
-            jax.ShapeDtypeStruct(send_shape, jnp.bfloat16),
-            jax.ShapeDtypeStruct(geo_shape, jnp.bfloat16),
+        in_specs=[
+            smem(), smem(), smem(), smem(),
+            pl.BlockSpec(lines_block, lambda i: (i, 0)),
+            pl.BlockSpec(table_block, lambda i: (i, 0, 0)),
         ],
-        scratch_shapes=[spots_shape, pltpu.VMEM((sz.spots, SLAB), jnp.int32)],
+        out_specs=[whole_block(send_shape)] + [whole_block(geo_shape)] * len(rounds),
+        out_shape=[jax.ShapeDtypeStruct(send_shape, jnp.bfloat16)]
+        + [jax.ShapeDtypeStruct(geo_shape, jnp.bfloat16)] * len(rounds),
+        scratch_shapes=[wide_shape, spots_shape, pltpu.VMEM((sz.spots, SLAB), jnp.int32)],
         compiler_params=params(56),
         name="inverse_legendre",
-    )(slot_wave, row_points, gauss_weight, layer_depth, *([tiled] * sz.tiles), tables)
-
+    )(slot_wave, row_points, gauss_weight, layer_depth, lines, tables)
+
+    sent, points_later, wave_later = lax.optimization_barrier((sent, row_points, slot_wave))
     both = ("band", "lev")
     total = sz.bands * sz.groups
     flat = (total * sz.chunk, SLAB)
     arrived = lax.all_to_all(sent.reshape(flat), both, split_axis=0, concat_axis=0, tiled=True)
 
-    pair_wave = slot_wave.reshape(-1, 2)
+    pair_wave = wave_later.reshape(-1, 2)
     even_wave = jnp.where(pair_wave[:, 0] % 2 == 0, pair_wave[:, 0], pair_wave[:, 1])
     even_wave = even_wave.reshape(sz.bands, sz.halves, sz.chunk_live)
     even_wave = jnp.pad(even_wave, ((0, 0), (0, 0), (0, sz.chunk - sz.chunk_live)), constant_values=-1)
@@ -525,9 +545,12 @@
             flops=20 * sz.sorted * sz.orbits, bytes_accessed=8 * sz.sorted * sz.orbits, transcendentals=0,
         ),
         name="basis",
-    )(row_points)
-
-    geo, arrived = lax.optimization_barrier((geo, arrived))
+    )(points_later)
+
+    even_row, even_col = even_wave.reshape(1, sz.pairs), even_wave.reshape(sz.pairs, 1)
+    *geo, arrived, basis, even_row, even_col = lax.optimization_barrier(
+        (*geo, arrived, basis, even_row, even_col)
+    )
     moved = [lax.ppermute(geo[turn], "lev", pairs) for turn, pairs in enumerate(rounds)]
     vmem = pl.BlockSpec(memory_space=pltpu.VMEM)
     returned = pl.pallas_call(
@@ -538,7 +561,7 @@
         scratch_shapes=[
             pltpu.VMEM((4, sz.sorted, sz.orbits), jnp.bfloat16),
             pltpu.VMEM((4, SLAB, sz.orbits), jnp.bfloat16),
-            pltpu.SemaphoreType.DMA((sz.orbits // SLAB,)),
+            pltpu.SemaphoreType.DMA((-(-sz.orbits // (2 * SLAB)),)),
         ],
         compiler_params=params(56),
         cost_estimate=pl.CostEstimate(
@@ -546,8 +569,7 @@
         ),
         name="grid_products",
     )(
-        row_points, gauss_weight, arrived.reshape(send_shape),
-        even_wave.reshape(1, sz.pairs), even_wave.reshape(sz.pairs, 1), basis,
+        row_points, gauss_weight, arrived.reshape(send_shape), even_row, even_col, basis,
     )
     *moved, returned = lax.optimization_barrier((*moved, returned))
 
@@ -558,7 +580,7 @@
         grid=(sz.steps,),
         in_specs=[
             smem(), smem(),
-            whole_block(send_shape), whole_block(geo_shape),
+            whole_block(send_shape), *([whole_block(geo_shape)] * len(rounds)),
             pl.BlockSpec(lines_block, lambda i: (i, 0)),
             pl.BlockSpec(table_block, lambda i: (i, 0, 0)),
         ],
@@ -571,7 +593,7 @@
         ],
         compiler_params=params(56),
         name="forward_legendre",
-    )(slot_wave, mode_speed, back.reshape(send_shape), jnp.stack(moved), lines, tables)
+    )(slot_wave, mode_speed, back.reshape(send_shape), *moved, lines, tables)
 
     out = out.reshape(slots, fields, sz.tiles, 2, SLAB).transpose(0, 1, 3, 2, 4)
     return out.reshape(slots, fields, 2, degrees).transpose(0, 2, 1, 3)

time: 120 us -> 108 us (0.900)
  waiting for transfers between devices: 22.3 us -> 4.74 us
  blocking collectives: 0 us -> 16.1 us
  starting transfers between devices: 12.5 us -> 8.65 us
  Pallas kernels: 78.1 us -> 74.6 us
  local copies, waits for them, and re-layouts: 4.3 us -> 2.49 us
    all_to_all x0 -> x1, blocking collectives: none -> 16.1 us  [shards(): lax.all_to_all(returned.reshape(flat), both, split_axis=0, concat_axis=0,...]
    all_to_all x1 -> x0, waiting for transfers between devices: 11.1 us -> none  [shards(): lax.all_to_all(returned.reshape(flat), both, split_axis=0, concat_axis=0,...]
    all_to_all x1, waiting for transfers between devices: 11.2 us -> 4.73 us  [shards(): lax.all_to_all(sent.reshape(flat), both, split_axis=0, concat_axis=0, til...]
    all_to_all x1 -> x0, starting transfers between devices: 3.87 us -> none  [shards(): lax.all_to_all(returned.reshape(flat), both, split_axis=0, concat_axis=0,...]
    pallas_call x1, Pallas kernels: 24.8 us -> 22.9 us  [shards(): pl.pallas_call(functools.partial(inverse_kernel, sz, rounds), grid=(sz.st...]
    pallas_call x1, Pallas kernels: 10.5 us -> 9 us  [shards(): pl.pallas_call(functools.partial(grid_kernel, sz), in_specs=[smem(), smem...]
    squeeze x1 -> x0, local copies, waits for them, and re-layouts: 1.23 us -> none  [shards(): geo[turn]]
  transfers between devices with their start and end apart: 4 -> 3, of which waited for: 2 -> 1; matrix products, arithmetic and copies ran while one was open for 3% -> 2% of each run, Pallas kernels for 14% -> 14%
where the time goes in v3:
time: 108 us; the launch traced here: 107 us
  Pallas kernels  74.6 us (69%)
  blocking collectives  16.1 us (15%)
  starting transfers between devices  8.65 us (8%)
  waiting for transfers between devices  4.74 us (4%)
  local copies, waits for them, and re-layouts  2.49 us (2%)
    pallas_call x1, Pallas kernels, shards(): pl.pallas_call(functools.partial(forward_kernel, sz), grid=(sz.steps,), i...  37 us
    pallas_call x1, Pallas kernels, shards(): pl.pallas_call(functools.partial(inverse_kernel, sz, rounds), grid=(sz.st...  22.9 us
    all_to_all x1, blocking collectives, shards(): lax.all_to_all(returned.reshape(flat), both, split_axis=0, concat_axis=0,...  16.1 us
    pallas_call x1, Pallas kernels, shards(): pl.pallas_call(functools.partial(grid_kernel, sz), in_specs=[smem(), smem...  9 us
    all_to_all x1, starting transfers between devices, shards(): lax.all_to_all(sent.reshape(flat), both, split_axis=0, concat_axis=0, til...  7.3 us
    pallas_call x1, Pallas kernels, shards(): pl.pallas_call(functools.partial(basis_kernel, sz), grid=(sz.sorted // hi...  5.64 us
    all_to_all x1, waiting for transfers between devices, shards(): lax.all_to_all(sent.reshape(flat), both, split_axis=0, concat_axis=0, til...  4.73 us
  transfers between devices with their start and end apart: 3, of which 1 were waited for; matrix products, arithmetic and copies ran while one was open for 2% of the time, Pallas kernels for 14%

profile of v3, /device:TPU:0, one launch (start us, length us, event | category | flops | bytes accessed | tf_op | source)
XLA Modules:
  0.0 106.7 jit_solution(4002469919151705381)
XLA Ops:
  0.0 0.0 copy-start.3
  0.0 22.9 %inverse_legendre.1 = (bf16[8,4,40,128]{3,2,1,0:T(8,128)(2,1)}, bf16[8,160,128]{2,1,0:T(8,128)(2,1)}, bf16[8,160,128]{2,1,0:T(8,128)(2,1)}) custom-call(s32[1280]{0:T(1024)} %wave.3, s32[16]{0:T(128)} %points.4, f32[16]{0:T(128)} %gauss.3, f32[24]{0:T(128)} %layer_depth.1, bf16[96000,128]{1,0:T(8,128)(2,1)} %bitcast.20, bf16[160,16,1280]{2,1,0:T(8,128)(2,1)} %bitcast.22), custom_call_target="tpu_custom_call" | custom-call | tf_op jit(solution)/shard_map/inverse_legendre/pallas_call | solution.py:506
  22.9 7.3 %all-to-all-start = ((bf16[32,40,128]{2,1,0:T(8,128)(2,1)}), bf16[32,40,128]{2,1,0:T(8,128)(2,1)S(1)}, u32[]{:S(2)}, u32[]{:S(2)}) async-start(bf16[32,40,128]{2,1,0:T(8,128)(2,1)} %bitcast.27), calls=%async_computation | async-start | bytes 655360 | tf_op jit(solution)/shard_map/all_to_all | solution.py:526
  30.2 0.0 copy-done.3
  30.2 0.3 reshape.35
  30.5 0.3 slice_reduce_fusion
  30.8 0.1 squeeze.8
  30.9 0.1 squeeze.7
  31.0 0.1 reshape_reshape.7
  31.1 0.7 reshape_reshape.6.even_row
  31.8 5.6 %basis.1.basis_hbm = bf16[4,640,1408]{2,1,0:T(8,128)(2,1)} custom-call(s32[16]{0:T(128)} %points.4), custom_call_target="tpu_custom_call" | custom-call | flops 18022400 | bytes 7208960 | tf_op jit(solution)/shard_map/basis/pallas_call | solution.py:536
  37.4 4.7 %all-to-all-done = bf16[32,40,128]{2,1,0:T(8,128)(2,1)S(1)} async-done(((bf16[32,40,128]{2,1,0:T(8,128)(2,1)}), bf16[32,40,128]{2,1,0:T(8,128)(2,1)S(1)}, u32[]{:S(2)}, u32[]{:S(2)}) %all-to-all-start) | async-done | bytes 327712 | tf_op jit(solution)/shard_map/all_to_all | solution.py:526
  42.2 0.0 copy-start
  42.2 0.7 collective-permute-start
  42.9 0.7 collective-permute-start.1
  43.5 0.9 copy.10.even_col
  44.5 0.0 copy-done
  44.5 9.0 %grid_products.1 = bf16[8,4,40,128]{3,2,1,0:T(8,128)(2,1)} custom-call(s32[16]{0:T(128)} %points.4, f32[16]{0:T(128)} %gauss.3, bf16[8,4,40,128]{3,2,1,0:T(8,128)(2,1)} %bitcast.25, s32[1,640]{1,0:T(1,128)} %reshape_reshape.6.even_row, s32[640,1]{1,0:T(8,128)} %copy.10.even_col, bf16[4,640,1408]{2,1,0:T(8,128)(2,1)} %basis.1.basis_hbm), custom_call_target="tpu_custom_call" | custom-call | flops 1845493760 | bytes 7208960 | tf_op jit(solution)/shard_map/grid_products/pallas_call | solution.py:556
  53.5 0.0 collective-permute-done.refs_0_
  53.5 0.0 copy-start.1
  53.5 0.0 collective-permute-done.1.refs_1_
  53.5 0.0 copy-start.2
  53.5 16.1 %all_to_all.21 = bf16[32,40,128]{2,1,0:T(8,128)(2,1)} all-to-all(bf16[32,40,128]{2,1,0:T(8,128)(2,1)} %bitcast.26), channel_id=1, replica_groups=mesh['band'=8,'lev'=4] {'band','lev'}, dimensions={0} | all-to-all | bytes 655360 | tf_op jit(solution)/shard_map/all_to_all | solution.py:576
  69.6 0.0 copy-done.1
  69.6 0.0 copy-done.2
  69.6 37.0 %forward_legendre.1 = f32[96000,128]{1,0:T(8,128)} custom-call(s32[1280]{0:T(1024)} %wave.3, f32[30]{0:T(128)} %speed.1, bf16[8,4,40,128]{3,2,1,0:T(8,128)(2,1)} %bitcast.24, bf16[8,160,128]{2,1,0:T(8,128)(2,1)} %copy-done.1, bf16[8,160,128]{2,1,0:T(8,128)(2,1)} %copy-done.2, bf16[96000,128]{1,0:T(8,128)(2,1)} %bitcast.21, bf16[160,16,1280]{2,1,0:T(8,128)(2,1)} %bitcast.23), custom_call_target="tpu_custom_call" | custom-call | tf_op jit(solution)/shard_map/forward_legendre/pallas_call | solution.py:578
  (2 shorter events, 0.0 us)
Async XLA Ops:
  0.0 30.2 %copy-start.3 = (s32[1280]{0:T(1024)S(1)}, s32[1280]{0:T(1024)}, u32[]{:S(2)}) copy-start(s32[1280]{0:T(1024)} %wave.3) | copy-start | bytes 15364
  22.9 19.3 %all-to-all-start = ((bf16[32,40,128]{2,1,0:T(8,128)(2,1)}), bf16[32,40,128]{2,1,0:T(8,128)(2,1)S(1)}, u32[]{:S(2)}, u32[]{:S(2)}) async-start(bf16[32,40,128]{2,1,0:T(8,128)(2,1)} %bitcast.27), calls=%async_computation | async-start | bytes 655360 | tf_op jit(solution)/shard_map/all_to_all | solution.py:526
  42.2 2.3 %copy-start = (bf16[32,40,128]{2,1,0:T(8,128)(2,1)}, bf16[32,40,128]{2,1,0:T(8,128)(2,1)S(1)}, u32[]{:S(2)}) copy-start(bf16[32,40,128]{2,1,0:T(8,128)(2,1)S(1)} %all-to-all-done) | copy-start | bytes 983044
  42.2 11.3 %collective-permute-start = (bf16[8,160,128]{2,1,0:T(8,128)(2,1)}, bf16[8,160,128]{2,1,0:T(8,128)(2,1)S(1)}, u32[]{:S(2)}, u32[]{:S(2)}) collective-permute-start(bf16[8,160,128]{2,1,0:T(8,128)(2,1)} %get-tuple-element.26), channel_id=1, source_target_pairs={{1,3},{5,7},{9,11},{13,15},{17,19},{21,23},{25,27},{29,31}} | collective-permute-start | bytes 983048 | tf_op jit(solution)/shard_map/ppermute | solution.py:554
  42.9 10.6 %collective-permute-start.1 = (bf16[8,160,128]{2,1,0:T(8,128)(2,1)}, bf16[8,160,128]{2,1,0:T(8,128)(2,1)S(1)}, u32[]{:S(2)}, u32[]{:S(2)}) collective-permute-start(bf16[8,160,128]{2,1,0:T(8,128)(2,1)} %get-tuple-element.27), channel_id=1, source_target_pairs={{2,3},{6,7},{10,11},{14,15},{18,19},{22,23},{26,27},{30,31}} | collective-permute-start | bytes 983048 | tf_op jit(solution)/shard_map/ppermute | solution.py:554
  53.5 16.1 %copy-start.1 = (bf16[8,160,128]{2,1,0:T(8,128)(2,1)}, bf16[8,160,128]{2,1,0:T(8,128)(2,1)S(1)}, u32[]{:S(2)}) copy-start(bf16[8,160,128]{2,1,0:T(8,128)(2,1)S(1)} %collective-permute-done.refs_0_) | copy-start | bytes 983044
  53.5 16.1 %copy-start.2 = (bf16[8,160,128]{2,1,0:T(8,128)(2,1)}, bf16[8,160,128]{2,1,0:T(8,128)(2,1)S(1)}, u32[]{:S(2)}) copy-start(bf16[8,160,128]{2,1,0:T(8,128)(2,1)S(1)} %collective-permute-done.1.refs_1_) | copy-start | bytes 983044

commit v4 on v3

--- a/solution.py
+++ b/solution.py
@@ -135,6 +135,19 @@
     return (odd * sizes.halves + half) * sizes.chunk + (place - half * sizes.chunk_live)
 
 
+def pair_state(sizes, wave, band, place):
+    slot = band * sizes.slots + 2 * place
+    first, second = wave[slot], wave[slot + 1]
+    odd = first & 1
+    start = quotient(jnp.maximum(first, 0), SLAB)
+    live = sizes.tiles - start
+    tiles = []
+    for k in range(sizes.tiles + 1):
+        side = jnp.where(k < live, 0, 1)
+        tiles.append((side, jnp.where(k < live, start + k, k - 1)))
+    return (first, second), (odd, 1 - odd), tiles
+
+
 def inverse_kernel(sizes, rounds, wave, points, gauss, layer_depth, x_ref, leg_ref, send_ref, *refs):
     sz = sizes
     geo_refs = refs[:len(rounds)]
@@ -153,31 +166,34 @@
             (wide.shape[0], wide.shape[1] - height, SLAB), jnp.float32
         )
 
-    degree = iota((1, sz.degrees), 1)
+    for pair in range(sz.block // 2):
+        rows = x_ref[pl.ds(pair * height, height), :]
+        wide[pair, pl.ds(0, height), :] = rows.astype(jnp.float32)
     found = []
     for pair in range(sz.block // 2):
-        buf = wide.at[pair % wide.shape[0]]
-        buf[pl.ds(0, height), :] = x_ref[pl.ds(pair * height, height), :].astype(jnp.float32)
         place = step * (sz.block // 2) + pair
-        slot = band * sz.slots + 2 * place
-        first_odd = wave[slot] & 1
+        numbers_here, odds, tiles = pair_state(sz, wave, band, place)
+        values, tables = [], []
+        for side, tile in tiles:
+            start = side * sz.slot_rows + 2 * tile
+            values.append(jnp.concatenate([
+                wide[pair, pl.ds(start + c, sz.field_pad, stride=2 * sz.tiles), :] for c in range(2)
+            ], axis=0).astype(jnp.bfloat16))
+            cols = pl.ds(pl.multiple_of(tile * SLAB, SLAB), SLAB)
+            table = leg_ref[2 * pair + side, :, cols].astype(jnp.float32)
+            number = jnp.where(side == 0, numbers_here[0], numbers_here[1])
+            table = jnp.where(iota((1, SLAB), 1) + tile * SLAB >= number, table, 0.0)
+            tables.append(jnp.concatenate([
+                jnp.where(side == 0, table, 0.0), jnp.where(side == 1, table, 0.0),
+            ], axis=0).astype(jnp.bfloat16))
+        total = dot(
+            jnp.concatenate(tables, axis=1), jnp.concatenate(values, axis=1), ((1,), (1,))
+        )
         for side in range(2):
-            number = wave[slot + side]
-            table = jnp.where(degree >= number, leg_ref[2 * pair + side].astype(jnp.float32), 0.0)
-            table = table.astype(jnp.bfloat16)
-            total = jnp.zeros((sz.rows, pad), jnp.float32)
-            for t in range(0, sz.tiles, 2):
-                parts = []
-                for tt in range(t, min(t + 2, sz.tiles)):
-                    first = side * sz.slot_rows + 2 * tt
-                    parts.append(jnp.concatenate([
-                        buf[pl.ds(first + c, sz.field_pad, stride=2 * sz.tiles), :] for c in range(2)
-                    ], axis=0).astype(jnp.bfloat16))
-                values = jnp.concatenate(parts, axis=1)
-                piece = table[:, t * SLAB:t * SLAB + values.shape[1]]
-                total += dot(piece, values, ((1,), (1,)))
-            odd = first_odd if side == 0 else 1 - first_odd
-            found.append((spot_of(sz, place, odd), number, total))
+            found.append((
+                spot_of(sz, place, odds[side]), numbers_here[side],
+                total[side * sz.rows:(side + 1) * sz.rows],
+            ))
     for spot, number, total in found:
         at = pl.multiple_of(spot * sz.rows, sz.rows)
         spots[pl.ds(at, sz.rows), 0:pad] = total
@@ -408,7 +424,7 @@
     sizes, wave, speed, back_ref, *refs,
 ):
     sz = sizes
-    *geo_refs, x_ref, leg_ref, out_ref, wide, spots, inverse, speeds = refs
+    *geo_refs, x_ref, leg_ref, out_ref, wide, spots, inverse = refs
     step = pl.program_id(0)
     band = lax.axis_index("band")
     pad = 2 * sz.field_pad
@@ -416,9 +432,6 @@
 
     @pl.when(step == 0)
     def _():
-        wide[:, pl.ds(height, wide.shape[1] - height), :] = jnp.zeros(
-            (wide.shape[0], wide.shape[1] - height, SLAB), jnp.float32
-        )
         gather = spread_matrix(sz, lax.axis_index("lev"))
         for rp in range(sz.rows // 2):
             cut = jnp.concatenate([back_ref[rp, g] for g in range(sz.groups)], axis=1)
@@ -432,44 +445,55 @@
                 part = rows[:, r * pad:(r + 1) * pad]
                 part = jnp.concatenate([part, jnp.zeros((sz.spots, SLAB - pad), jnp.float32)], axis=1)
                 spots[pl.ds(2 * rp + r, sz.spots, stride=sz.rows), :] = part
-        speeds[...] = jnp.ones_like(speeds)
         for f in range(sz.fields):
-            speeds[pl.ds(f, 1), :] = jnp.full((1, SLAB), speed[f], jnp.float32)
-        for t in range(sz.tiles):
-            degree = iota((1, SLAB), 1) + t * SLAB
+            rows = 2 * sz.tiles
+            degree = quotient(iota((rows, SLAB), 0), 2) * SLAB + iota((rows, SLAB), 1)
             helm = (degree * (degree + 1)).astype(jnp.float32) / float(sz.trunc * (sz.trunc + 1))
-            inverse[t] = 1.0 / (1.0 + time_step * time_step * helm * speeds[...])
-
+            inverse[pl.ds(f * rows, rows), :] = 1.0 / (1.0 + time_step * time_step * helm * speed[f])
+
+    pitch = sz.field_pad * 2 * sz.tiles
     work = []
     for pair in range(sz.block // 2):
         place = step * (sz.block // 2) + pair
-        slot = band * sz.slots + 2 * place
-        first_odd = wave[slot] & 1
+        numbers, odds, tiles = pair_state(sz, wave, band, place)
+        lefts = []
         for side in range(2):
-            number = wave[slot + side]
-            floor = jnp.where(number < 0, sz.degrees, number)
-            odd = first_odd if side == 0 else 1 - first_odd
-            at = pl.multiple_of(spot_of(sz, place, odd) * sz.rows, sz.rows)
-            work.append((floor, spots[pl.ds(at, sz.rows), :].T.astype(jnp.bfloat16)[0:pad]))
-
+            at = pl.multiple_of(spot_of(sz, place, odds[side]) * sz.rows, sz.rows)
+            lefts.append(spots[pl.ds(at, sz.rows), :])
+        left = jnp.concatenate(lefts, axis=0).T.astype(jnp.bfloat16)[0:pad]
+        tables = []
+        for side, tile in tiles:
+            cols = pl.ds(pl.multiple_of(tile * SLAB, SLAB), SLAB)
+            table = leg_ref[2 * pair + side, :, cols].astype(jnp.float32)
+            tables.append(jnp.concatenate([
+                jnp.where(side == 0, table, 0.0), jnp.where(side == 1, table, 0.0),
+            ], axis=0).astype(jnp.bfloat16))
+        work.append((numbers, tiles, left, tables))
     for pair in range(sz.block // 2):
-        buf = wide.at[pair % wide.shape[0]]
-        buf[pl.ds(0, height), :] = x_ref[pl.ds(pair * height, height), :].astype(jnp.float32)
+        _, tiles, left, tables = work[pair]
+        for k in range(0, len(tiles), 2):
+            count = min(2, len(tiles) - k)
+            tends = dot(left, jnp.concatenate(tables[k:k + count], axis=1))
+            for kk in range(count):
+                side, tile = tiles[k + kk]
+                for c in range(2):
+                    rows = pl.ds(side * pitch + 2 * tile + c, sz.field_pad, stride=2 * sz.tiles)
+                    wide[pair, rows, :] = tends[
+                        c * sz.field_pad:(c + 1) * sz.field_pad, kk * SLAB:(kk + 1) * SLAB
+                    ]
+    run = 4 * sz.tiles if sz.fields % 2 == 0 else 2 * sz.tiles
+    row = remainder(iota((run, SLAB), 0), 2 * sz.tiles)
+    degree = quotient(row, 2) * SLAB + iota((run, SLAB), 1)
+    for pair in range(sz.block // 2):
+        numbers = work[pair][0]
+        old = x_ref[pl.ds(pair * height, height), :].astype(jnp.float32)
         for side in range(2):
-            floor, left = work[2 * pair + side]
-            base = (2 * pair + side) * sz.slot_rows
-            for first in range(0, sz.tiles, 2):
-                count = min(2, sz.tiles - first)
-                tends = dot(left, leg_ref[2 * pair + side, :, first * SLAB:(first + count) * SLAB])
-                for t in range(first, first + count):
-                    tend = tends[:, (t - first) * SLAB:(t - first + 1) * SLAB]
-                    live = iota((1, SLAB), 1) + t * SLAB >= floor
-                    for c in range(2):
-                        rows = pl.ds(side * sz.slot_rows + 2 * t + c, sz.field_pad, stride=2 * sz.tiles)
-                        new = buf[rows, :] + time_step * tend[c * sz.field_pad:(c + 1) * sz.field_pad]
-                        new = jnp.where(live, new * inverse[t], 0.0)
-                        rows = pl.ds(base + 2 * t + c, sz.fields, stride=2 * sz.tiles)
-                        out_ref[rows, :] = new[0:sz.fields]
+            live = degree >= jnp.where(numbers[side] < 0, sz.degrees, numbers[side])
+            for at in range(0, sz.slot_rows, run):
+                tend = wide[pair, pl.ds(side * pitch + at, run), :]
+                new = old[side * sz.slot_rows + at:side * sz.slot_rows + at + run] + time_step * tend
+                new = jnp.where(live, new * inverse[pl.ds(at, run), :], 0.0)
+                out_ref[pl.ds(pair * height + side * sz.slot_rows + at, run), :] = new
 
 
 def params(mib):
@@ -496,7 +520,7 @@
 
     rounds = geo_rounds(sz)
     tail = up_to((sz.field_pad - sz.fields) * 2 * sz.tiles, 16)
-    wide_shape = pltpu.VMEM((4, 2 * sz.slot_rows + tail, SLAB), jnp.float32)
+    wide_shape = pltpu.VMEM((sz.block // 2, 2 * sz.slot_rows + tail, SLAB), jnp.float32)
     spots_shape = pltpu.VMEM((sz.spots * sz.rows, SLAB), jnp.float32)
     lines_block = (sz.block * sz.slot_rows, SLAB)
     table_block = (sz.block, sz.rows, degrees)
@@ -587,9 +611,8 @@
         out_specs=pl.BlockSpec(lines_block, lambda i: (i, 0)),
         out_shape=jax.ShapeDtypeStruct((slots * sz.slot_rows, SLAB), jnp.float32),
         scratch_shapes=[
-            wide_shape, spots_shape,
-            pltpu.VMEM((sz.tiles, sz.field_pad, SLAB), jnp.float32),
-            pltpu.VMEM((sz.field_pad, SLAB), jnp.float32),
+            pltpu.VMEM((sz.block // 2, 4 * sz.field_pad * sz.tiles, SLAB), jnp.float32), spots_shape,
+            pltpu.VMEM((sz.slot_rows, SLAB), jnp.float32),
         ],
         compiler_params=params(56),
         name="forward_legendre",

time: 108 us -> 110 us (1.019)
  Pallas kernels: 74.6 us -> 76 us
where the time goes in v4:
time: 110 us; the launch traced here: 108 us
  Pallas kernels  76 us (69%)
  blocking collectives  16.1 us (15%)
  starting transfers between devices  8.65 us (8%)
  waiting for transfers between devices  4.74 us (4%)
  local copies, waits for them, and re-layouts  2.49 us (2%)
    pallas_call x1, Pallas kernels, shards(): pl.pallas_call(functools.partial(forward_kernel, sz), grid=(sz.steps,), i...  37.7 us
    pallas_call x1, Pallas kernels, shards(): pl.pallas_call(functools.partial(inverse_kernel, sz, rounds), grid=(sz.st...  23.6 us
    all_to_all x1, blocking collectives, shards(): lax.all_to_all(returned.reshape(flat), both, split_axis=0, concat_axis=0,...  16.1 us
    pallas_call x1, Pallas kernels, shards(): pl.pallas_call(functools.partial(grid_kernel, sz), in_specs=[smem(), smem...  9 us
    all_to_all x1, starting transfers between devices, shards(): lax.all_to_all(sent.reshape(flat), both, split_axis=0, concat_axis=0, til...  7.3 us
    pallas_call x1, Pallas kernels, shards(): pl.pallas_call(functools.partial(basis_kernel, sz), grid=(sz.sorted // hi...  5.64 us
    all_to_all x1, waiting for transfers between devices, shards(): lax.all_to_all(sent.reshape(flat), both, split_axis=0, concat_axis=0, til...  4.73 us
  transfers between devices with their start and end apart: 3, of which 1 were waited for; matrix products, arithmetic and copies ran while one was open for 2% of the time, Pallas kernels for 14%

profile of v4, /device:TPU:0, one launch (start us, length us, event | category | flops | bytes accessed | tf_op | source)
XLA Modules:
  0.0 108.1 jit_solution(7117979440702848659)
XLA Ops:
  0.0 0.0 copy-start.3
  0.0 23.6 %inverse_legendre.1 = (bf16[8,4,40,128]{3,2,1,0:T(8,128)(2,1)}, bf16[8,160,128]{2,1,0:T(8,128)(2,1)}, bf16[8,160,128]{2,1,0:T(8,128)(2,1)}) custom-call(s32[1280]{0:T(1024)} %wave.3, s32[16]{0:T(128)} %points.4, f32[16]{0:T(128)} %gauss.3, f32[24]{0:T(128)} %layer_depth.1, bf16[96000,128]{1,0:T(8,128)(2,1)} %bitcast.20, bf16[160,16,1280]{2,1,0:T(8,128)(2,1)} %bitcast.22), custom_call_target="tpu_custom_call" | custom-call | tf_op jit(solution)/shard_map/inverse_legendre/pallas_call | solution.py:530
  23.6 7.3 %all-to-all-start = ((bf16[32,40,128]{2,1,0:T(8,128)(2,1)}), bf16[32,40,128]{2,1,0:T(8,128)(2,1)S(1)}, u32[]{:S(2)}, u32[]{:S(2)}) async-start(bf16[32,40,128]{2,1,0:T(8,128)(2,1)} %bitcast.27), calls=%async_computation | async-start | bytes 655360 | tf_op jit(solution)/shard_map/all_to_all | solution.py:550
  30.9 0.0 copy-done.3
  31.0 0.3 reshape.35
  31.2 0.3 slice_reduce_fusion
  31.6 0.1 squeeze.8
  31.7 0.1 squeeze.7
  31.8 0.1 reshape_reshape.7
  31.9 0.7 reshape_reshape.6.even_row
  32.6 5.6 %basis.1.basis_hbm = bf16[4,640,1408]{2,1,0:T(8,128)(2,1)} custom-call(s32[16]{0:T(128)} %points.4), custom_call_target="tpu_custom_call" | custom-call | flops 18022400 | bytes 7208960 | tf_op jit(solution)/shard_map/basis/pallas_call | solution.py:560
  38.2 4.7 %all-to-all-done = bf16[32,40,128]{2,1,0:T(8,128)(2,1)S(1)} async-done(((bf16[32,40,128]{2,1,0:T(8,128)(2,1)}), bf16[32,40,128]{2,1,0:T(8,128)(2,1)S(1)}, u32[]{:S(2)}, u32[]{:S(2)}) %all-to-all-start) | async-done | bytes 327712 | tf_op jit(solution)/shard_map/all_to_all | solution.py:550
  42.9 0.0 copy-start
  42.9 0.7 collective-permute-start
  43.6 0.7 collective-permute-start.1
  44.3 0.9 copy.10.even_col
  45.2 0.0 copy-done
  45.2 9.0 %grid_products.1 = bf16[8,4,40,128]{3,2,1,0:T(8,128)(2,1)} custom-call(s32[16]{0:T(128)} %points.4, f32[16]{0:T(128)} %gauss.3, bf16[8,4,40,128]{3,2,1,0:T(8,128)(2,1)} %bitcast.25, s32[1,640]{1,0:T(1,128)} %reshape_reshape.6.even_row, s32[640,1]{1,0:T(8,128)} %copy.10.even_col, bf16[4,640,1408]{2,1,0:T(8,128)(2,1)} %basis.1.basis_hbm), custom_call_target="tpu_custom_call" | custom-call | flops 1845493760 | bytes 7208960 | tf_op jit(solution)/shard_map/grid_products/pallas_call | solution.py:580
  54.2 0.0 collective-permute-done.refs_0_
  54.3 0.0 copy-start.1
  54.3 0.0 collective-permute-done.1.refs_1_
  54.3 0.0 copy-start.2
  54.3 16.1 %all_to_all.21 = bf16[32,40,128]{2,1,0:T(8,128)(2,1)} all-to-all(bf16[32,40,128]{2,1,0:T(8,128)(2,1)} %bitcast.26), channel_id=1, replica_groups=mesh['band'=8,'lev'=4] {'band','lev'}, dimensions={0} | all-to-all | bytes 655360 | tf_op jit(solution)/shard_map/all_to_all | solution.py:600
  70.4 0.0 copy-done.1
  70.4 0.0 copy-done.2
  70.4 37.7 %forward_legendre.1 = f32[96000,128]{1,0:T(8,128)} custom-call(s32[1280]{0:T(1024)} %wave.3, f32[30]{0:T(128)} %speed.1, bf16[8,4,40,128]{3,2,1,0:T(8,128)(2,1)} %bitcast.24, bf16[8,160,128]{2,1,0:T(8,128)(2,1)} %copy-done.1, bf16[8,160,128]{2,1,0:T(8,128)(2,1)} %copy-done.2, bf16[96000,128]{1,0:T(8,128)(2,1)} %bitcast.21, bf16[160,16,1280]{2,1,0:T(8,128)(2,1)} %bitcast.23), custom_call_target="tpu_custom_call" | custom-call | tf_op jit(solution)/shard_map/forward_legendre/pallas_call | solution.py:602
  (2 shorter events, 0.0 us)
Async XLA Ops:
  0.0 30.9 %copy-start.3 = (s32[1280]{0:T(1024)S(1)}, s32[1280]{0:T(1024)}, u32[]{:S(2)}) copy-start(s32[1280]{0:T(1024)} %wave.3) | copy-start | bytes 15364
  23.6 19.3 %all-to-all-start = ((bf16[32,40,128]{2,1,0:T(8,128)(2,1)}), bf16[32,40,128]{2,1,0:T(8,128)(2,1)S(1)}, u32[]{:S(2)}, u32[]{:S(2)}) async-start(bf16[32,40,128]{2,1,0:T(8,128)(2,1)} %bitcast.27), calls=%async_computation | async-start | bytes 655360 | tf_op jit(solution)/shard_map/all_to_all | solution.py:550
  42.9 2.3 %copy-start = (bf16[32,40,128]{2,1,0:T(8,128)(2,1)}, bf16[32,40,128]{2,1,0:T(8,128)(2,1)S(1)}, u32[]{:S(2)}) copy-start(bf16[32,40,128]{2,1,0:T(8,128)(2,1)S(1)} %all-to-all-done) | copy-start | bytes 983044
  42.9 11.3 %collective-permute-start = (bf16[8,160,128]{2,1,0:T(8,128)(2,1)}, bf16[8,160,128]{2,1,0:T(8,128)(2,1)S(1)}, u32[]{:S(2)}, u32[]{:S(2)}) collective-permute-start(bf16[8,160,128]{2,1,0:T(8,128)(2,1)} %get-tuple-element.26), channel_id=1, source_target_pairs={{1,3},{5,7},{9,11},{13,15},{17,19},{21,23},{25,27},{29,31}} | collective-permute-start | bytes 983048 | tf_op jit(solution)/shard_map/ppermute | solution.py:578
  43.6 10.6 %collective-permute-start.1 = (bf16[8,160,128]{2,1,0:T(8,128)(2,1)}, bf16[8,160,128]{2,1,0:T(8,128)(2,1)S(1)}, u32[]{:S(2)}, u32[]{:S(2)}) collective-permute-start(bf16[8,160,128]{2,1,0:T(8,128)(2,1)} %get-tuple-element.27), channel_id=1, source_target_pairs={{2,3},{6,7},{10,11},{14,15},{18,19},{22,23},{26,27},{30,31}} | collective-permute-start | bytes 983048 | tf_op jit(solution)/shard_map/ppermute | solution.py:578
  54.3 16.1 %copy-start.1 = (bf16[8,160,128]{2,1,0:T(8,128)(2,1)}, bf16[8,160,128]{2,1,0:T(8,128)(2,1)S(1)}, u32[]{:S(2)}) copy-start(bf16[8,160,128]{2,1,0:T(8,128)(2,1)S(1)} %collective-permute-done.refs_0_) | copy-start | bytes 983044
  54.3 16.1 %copy-start.2 = (bf16[8,160,128]{2,1,0:T(8,128)(2,1)}, bf16[8,160,128]{2,1,0:T(8,128)(2,1)S(1)}, u32[]{:S(2)}) copy-start(bf16[8,160,128]{2,1,0:T(8,128)(2,1)S(1)} %collective-permute-done.1.refs_1_) | copy-start | bytes 983044

commit v5 on v4

--- a/solution.py
+++ b/solution.py
@@ -148,103 +148,136 @@
     return (first, second), (odd, 1 - odd), tiles
 
 
-def inverse_kernel(sizes, rounds, wave, points, gauss, layer_depth, x_ref, leg_ref, send_ref, *refs):
+AHEAD = 6
+BEHIND = 4
+
+
+class Stream:
+    def __init__(self, sizes, x_hbm, leg_hbm, x_all, leg_all, x_sems, leg_sems):
+        self.sizes = sizes
+        self.pairs = ((x_hbm, x_all, x_sems), (leg_hbm, leg_all, leg_sems))
+
+    def copies(self, step):
+        return [
+            pltpu.make_async_copy(hbm.at[step], here.at[step], sems.at[step])
+            for hbm, here, sems in self.pairs
+        ]
+
+    def start(self, step):
+        for copy in self.copies(step):
+            copy.start()
+
+    def begin(self):
+        for step in range(min(AHEAD, self.sizes.steps)):
+            self.start(step)
+
+    def take(self, step):
+        @pl.when(step + AHEAD < self.sizes.steps)
+        def _():
+            self.start(step + AHEAD)
+
+        for copy in self.copies(step):
+            copy.wait()
+        return tuple(here.at[step] for _, here, _ in self.pairs)
+
+
+def inverse_kernel(sizes, rounds, wave, points, gauss, layer_depth, x_hbm, leg_hbm, send_ref, *refs):
     sz = sizes
     geo_refs = refs[:len(rounds)]
-    wide, spots, numbers = refs[len(rounds):]
-    step = pl.program_id(0)
+    wide, spots, numbers, *stream = refs[len(rounds):]
+    stream = Stream(sz, x_hbm, leg_hbm, *stream)
+    stream.begin()
     band = lax.axis_index("band")
     lev = lax.axis_index("lev")
     pad = 2 * sz.field_pad
     height = 2 * sz.slot_rows
-
-    @pl.when(step == 0)
-    def _():
-        spots[...] = jnp.zeros_like(spots)
-        numbers[...] = jnp.full_like(numbers, -1)
-        wide[:, pl.ds(height, wide.shape[1] - height), :] = jnp.zeros(
-            (wide.shape[0], wide.shape[1] - height, SLAB), jnp.float32
+    spots[...] = jnp.zeros_like(spots)
+    numbers[...] = jnp.full_like(numbers, -1)
+    wide[:, pl.ds(height, wide.shape[1] - height), :] = jnp.zeros(
+        (wide.shape[0], wide.shape[1] - height, SLAB), jnp.float32
+    )
+
+    def block(step, carry):
+        x_ref, leg_ref = stream.take(step)
+        for pair in range(sz.block // 2):
+            rows = x_ref[pl.ds(pair * height, height), :]
+            wide[pair, pl.ds(0, height), :] = rows.astype(jnp.float32)
+        found = []
+        for pair in range(sz.block // 2):
+            place = step * (sz.block // 2) + pair
+            numbers_here, odds, tiles = pair_state(sz, wave, band, place)
+            values, tables = [], []
+            for side, tile in tiles:
+                start = side * sz.slot_rows + 2 * tile
+                values.append(jnp.concatenate([
+                    wide[pair, pl.ds(start + c, sz.field_pad, stride=2 * sz.tiles), :] for c in range(2)
+                ], axis=0).astype(jnp.bfloat16))
+                cols = pl.ds(pl.multiple_of(tile * SLAB, SLAB), SLAB)
+                table = leg_ref[2 * pair + side, :, cols].astype(jnp.float32)
+                number = jnp.where(side == 0, numbers_here[0], numbers_here[1])
+                table = jnp.where(iota((1, SLAB), 1) + tile * SLAB >= number, table, 0.0)
+                tables.append(jnp.concatenate([
+                    jnp.where(side == 0, table, 0.0), jnp.where(side == 1, table, 0.0),
+                ], axis=0).astype(jnp.bfloat16))
+            total = dot(
+                jnp.concatenate(tables, axis=1), jnp.concatenate(values, axis=1), ((1,), (1,))
+            )
+            for side in range(2):
+                found.append((
+                    spot_of(sz, place, odds[side]), numbers_here[side],
+                    total[side * sz.rows:(side + 1) * sz.rows],
+                ))
+        for spot, number, total in found:
+            at = pl.multiple_of(spot * sz.rows, sz.rows)
+            spots[pl.ds(at, sz.rows), 0:pad] = total
+            numbers[pl.ds(spot, 1), :] = jnp.full((1, SLAB), number, jnp.int32)
+        return carry
+
+    lax.fori_loop(0, sz.steps, block, 0)
+    spread = spread_matrix(sz, lev)
+    shape = (2 * pad, SLAB)
+    src, dst = iota(shape, 0), iota(shape, 1)
+    bits = sz.field_pad.bit_length() - 1
+    from_field, from_side = src & (sz.field_pad - 1), src >> bits
+    to_field, to_side = dst & (sz.field_pad - 1), dst >> bits
+    weights = []
+    for pairs in rounds:
+        first = jnp.int32(2 * LEVELS + sz.fields)
+        for source, target in pairs:
+            first = jnp.where(lev == source, target * sz.fields - ENERGY * LEVELS, first)
+        under = lev * sz.fields + from_field - TEMPER * LEVELS
+        above = first + to_field
+        hit = (
+            (from_side == to_side)
+            & (from_field < sz.fields) & (to_field < sz.fields)
+            & (above >= 0) & (above <= under)
         )
-
-    for pair in range(sz.block // 2):
-        rows = x_ref[pl.ds(pair * height, height), :]
-        wide[pair, pl.ds(0, height), :] = rows.astype(jnp.float32)
-    found = []
-    for pair in range(sz.block // 2):
-        place = step * (sz.block // 2) + pair
-        numbers_here, odds, tiles = pair_state(sz, wave, band, place)
-        values, tables = [], []
-        for side, tile in tiles:
-            start = side * sz.slot_rows + 2 * tile
-            values.append(jnp.concatenate([
-                wide[pair, pl.ds(start + c, sz.field_pad, stride=2 * sz.tiles), :] for c in range(2)
-            ], axis=0).astype(jnp.bfloat16))
-            cols = pl.ds(pl.multiple_of(tile * SLAB, SLAB), SLAB)
-            table = leg_ref[2 * pair + side, :, cols].astype(jnp.float32)
-            number = jnp.where(side == 0, numbers_here[0], numbers_here[1])
-            table = jnp.where(iota((1, SLAB), 1) + tile * SLAB >= number, table, 0.0)
-            tables.append(jnp.concatenate([
-                jnp.where(side == 0, table, 0.0), jnp.where(side == 1, table, 0.0),
-            ], axis=0).astype(jnp.bfloat16))
-        total = dot(
-            jnp.concatenate(tables, axis=1), jnp.concatenate(values, axis=1), ((1,), (1,))
-        )
-        for side in range(2):
-            found.append((
-                spot_of(sz, place, odds[side]), numbers_here[side],
-                total[side * sz.rows:(side + 1) * sz.rows],
-            ))
-    for spot, number, total in found:
-        at = pl.multiple_of(spot * sz.rows, sz.rows)
-        spots[pl.ds(at, sz.rows), 0:pad] = total
-        numbers[pl.ds(spot, 1), :] = jnp.full((1, SLAB), number, jnp.int32)
-
-    @pl.when(step == sz.steps - 1)
-    def _():
-        spread = spread_matrix(sz, lev)
-        shape = (2 * pad, SLAB)
-        src, dst = iota(shape, 0), iota(shape, 1)
-        bits = sz.field_pad.bit_length() - 1
-        from_field, from_side = src & (sz.field_pad - 1), src >> bits
-        to_field, to_side = dst & (sz.field_pad - 1), dst >> bits
-        weights = []
-        for pairs in rounds:
-            first = jnp.int32(2 * LEVELS + sz.fields)
-            for source, target in pairs:
-                first = jnp.where(lev == source, target * sz.fields - ENERGY * LEVELS, first)
-            under = lev * sz.fields + from_field - TEMPER * LEVELS
-            above = first + to_field
-            hit = (
-                (from_side == to_side)
-                & (from_field < sz.fields) & (to_field < sz.fields)
-                & (above >= 0) & (above <= under)
-            )
-            weight = jnp.zeros(shape, jnp.float32)
-            for level in range(LEVELS):
-                weight = jnp.where(hit & (under == level), layer_depth[level], weight)
-            high = weight.astype(jnp.bfloat16)
-            low = (weight - high.astype(jnp.float32)).astype(jnp.bfloat16)
-            weights.append(jnp.concatenate([high, low], axis=0))
-        number = numbers[...]
-        lane = iota((sz.spots, SLAB), 1)
-        known = (number >= 0) & ~((number == 0) & (lane & sz.field_pad != 0))
-        for rp in range(sz.rows // 2):
-            exact = jnp.concatenate([
-                spots[pl.ds(2 * rp + r, sz.spots, stride=sz.rows), :][:, 0:pad] for r in range(2)
-            ], axis=1)
-            cut = jnp.concatenate([
-                exact[q * sz.chunk:(q + 1) * sz.chunk] for q in range(sz.quarters)
-            ], axis=1).astype(jnp.bfloat16)
-            chunk = dot(cut, spread).astype(jnp.bfloat16)
-            for g in range(sz.groups):
-                send_ref[rp, g] = chunk[:, g * SLAB:(g + 1) * SLAB]
-            count = jnp.where(lane < pad, points[2 * rp], points[2 * rp + 1])
-            scale = jnp.where(lane < pad, gauss[2 * rp], gauss[2 * rp + 1])
-            scale = jnp.where(known & (2 * number <= count - 1), scale, 0.0)
-            exact = exact.astype(jnp.bfloat16)
-            double = jnp.concatenate([exact, exact], axis=1)
-            for turn in range(len(rounds)):
-                geo_refs[turn][rp] = (dot(double, weights[turn]) * scale).astype(jnp.bfloat16)
+        weight = jnp.zeros(shape, jnp.float32)
+        for level in range(LEVELS):
+            weight = jnp.where(hit & (under == level), layer_depth[level], weight)
+        high = weight.astype(jnp.bfloat16)
+        low = (weight - high.astype(jnp.float32)).astype(jnp.bfloat16)
+        weights.append(jnp.concatenate([high, low], axis=0))
+    number = numbers[...]
+    lane = iota((sz.spots, SLAB), 1)
+    known = (number >= 0) & ~((number == 0) & (lane & sz.field_pad != 0))
+    for rp in range(sz.rows // 2):
+        exact = jnp.concatenate([
+            spots[pl.ds(2 * rp + r, sz.spots, stride=sz.rows), :][:, 0:pad] for r in range(2)
+        ], axis=1)
+        cut = jnp.concatenate([
+            exact[q * sz.chunk:(q + 1) * sz.chunk] for q in range(sz.quarters)
+        ], axis=1).astype(jnp.bfloat16)
+        chunk = dot(cut, spread).astype(jnp.bfloat16)
+        for g in range(sz.groups):
+            send_ref[rp, g] = chunk[:, g * SLAB:(g + 1) * SLAB]
+        count = jnp.where(lane < pad, points[2 * rp], points[2 * rp + 1])
+        scale = jnp.where(lane < pad, gauss[2 * rp], gauss[2 * rp + 1])
+        scale = jnp.where(known & (2 * number <= count - 1), scale, 0.0)
+        exact = exact.astype(jnp.bfloat16)
+        double = jnp.concatenate([exact, exact], axis=1)
+        for turn in range(len(rounds)):
+            geo_refs[turn][rp] = (dot(double, weights[turn]) * scale).astype(jnp.bfloat16)
 
 
 def cos_sin(z):
@@ -424,76 +457,95 @@
     sizes, wave, speed, back_ref, *refs,
 ):
     sz = sizes
-    *geo_refs, x_ref, leg_ref, out_ref, wide, spots, inverse = refs
-    step = pl.program_id(0)
+    geo_refs = refs[:-12]
+    x_hbm, leg_hbm, out_hbm, wide, spots, inverse, out_all, out_sems, *stream = refs[-12:]
+    stream = Stream(sz, x_hbm, leg_hbm, *stream)
+    stream.begin()
     band = lax.axis_index("band")
     pad = 2 * sz.field_pad
     height = 2 * sz.slot_rows
 
-    @pl.when(step == 0)
-    def _():
-        gather = spread_matrix(sz, lax.axis_index("lev"))
-        for rp in range(sz.rows // 2):
-            cut = jnp.concatenate([back_ref[rp, g] for g in range(sz.groups)], axis=1)
-            whole = dot(cut, gather, ((1,), (1,)))
-            rows = jnp.concatenate([
-                whole[:, q * 2 * pad:(q + 1) * 2 * pad] for q in range(sz.quarters)
-            ], axis=0)
-            for geo_ref in geo_refs:
-                rows = rows + geo_ref[rp].astype(jnp.float32)[:, 0:2 * pad]
-            for r in range(2):
-                part = rows[:, r * pad:(r + 1) * pad]
-                part = jnp.concatenate([part, jnp.zeros((sz.spots, SLAB - pad), jnp.float32)], axis=1)
-                spots[pl.ds(2 * rp + r, sz.spots, stride=sz.rows), :] = part
-        for f in range(sz.fields):
-            rows = 2 * sz.tiles
-            degree = quotient(iota((rows, SLAB), 0), 2) * SLAB + iota((rows, SLAB), 1)
-            helm = (degree * (degree + 1)).astype(jnp.float32) / float(sz.trunc * (sz.trunc + 1))
-            inverse[pl.ds(f * rows, rows), :] = 1.0 / (1.0 + time_step * time_step * helm * speed[f])
+    gather = spread_matrix(sz, lax.axis_index("lev"))
+    for rp in range(sz.rows // 2):
+        cut = jnp.concatenate([back_ref[rp, g] for g in range(sz.groups)], axis=1)
+        whole = dot(cut, gather, ((1,), (1,)))
+        rows = jnp.concatenate([
+            whole[:, q * 2 * pad:(q + 1) * 2 * pad] for q in range(sz.quarters)
+        ], axis=0)
+        for geo_ref in geo_refs:
+            rows = rows + geo_ref[rp].astype(jnp.float32)[:, 0:2 * pad]
+        for r in range(2):
+            part = rows[:, r * pad:(r + 1) * pad]
+            part = jnp.concatenate([part, jnp.zeros((sz.spots, SLAB - pad), jnp.float32)], axis=1)
+            spots[pl.ds(2 * rp + r, sz.spots, stride=sz.rows), :] = part
+    for f in range(sz.fields):
+        rows = 2 * sz.tiles
+        degree = quotient(iota((rows, SLAB), 0), 2) * SLAB + iota((rows, SLAB), 1)
+        helm = (degree * (degree + 1)).astype(jnp.float32) / float(sz.trunc * (sz.trunc + 1))
+        inverse[pl.ds(f * rows, rows), :] = 1.0 / (1.0 + time_step * time_step * helm * speed[f])
 
     pitch = sz.field_pad * 2 * sz.tiles
-    work = []
-    for pair in range(sz.block // 2):
-        place = step * (sz.block // 2) + pair
-        numbers, odds, tiles = pair_state(sz, wave, band, place)
-        lefts = []
-        for side in range(2):
-            at = pl.multiple_of(spot_of(sz, place, odds[side]) * sz.rows, sz.rows)
-            lefts.append(spots[pl.ds(at, sz.rows), :])
-        left = jnp.concatenate(lefts, axis=0).T.astype(jnp.bfloat16)[0:pad]
-        tables = []
-        for side, tile in tiles:
-            cols = pl.ds(pl.multiple_of(tile * SLAB, SLAB), SLAB)
-            table = leg_ref[2 * pair + side, :, cols].astype(jnp.float32)
-            tables.append(jnp.concatenate([
-                jnp.where(side == 0, table, 0.0), jnp.where(side == 1, table, 0.0),
-            ], axis=0).astype(jnp.bfloat16))
-        work.append((numbers, tiles, left, tables))
-    for pair in range(sz.block // 2):
-        _, tiles, left, tables = work[pair]
-        for k in range(0, len(tiles), 2):
-            count = min(2, len(tiles) - k)
-            tends = dot(left, jnp.concatenate(tables[k:k + count], axis=1))
-            for kk in range(count):
-                side, tile = tiles[k + kk]
-                for c in range(2):
-                    rows = pl.ds(side * pitch + 2 * tile + c, sz.field_pad, stride=2 * sz.tiles)
-                    wide[pair, rows, :] = tends[
-                        c * sz.field_pad:(c + 1) * sz.field_pad, kk * SLAB:(kk + 1) * SLAB
-                    ]
-    run = 4 * sz.tiles if sz.fields % 2 == 0 else 2 * sz.tiles
-    row = remainder(iota((run, SLAB), 0), 2 * sz.tiles)
-    degree = quotient(row, 2) * SLAB + iota((run, SLAB), 1)
-    for pair in range(sz.block // 2):
-        numbers = work[pair][0]
-        old = x_ref[pl.ds(pair * height, height), :].astype(jnp.float32)
-        for side in range(2):
-            live = degree >= jnp.where(numbers[side] < 0, sz.degrees, numbers[side])
-            for at in range(0, sz.slot_rows, run):
-                tend = wide[pair, pl.ds(side * pitch + at, run), :]
-                new = old[side * sz.slot_rows + at:side * sz.slot_rows + at + run] + time_step * tend
-                new = jnp.where(live, new * inverse[pl.ds(at, run), :], 0.0)
-                out_ref[pl.ds(pair * height + side * sz.slot_rows + at, run), :] = new
+
+    def leave(step):
+        at = lax.rem(step, BEHIND)
+        return pltpu.make_async_copy(out_all.at[at], out_hbm.at[step], out_sems.at[at])
+
+    def block(step, carry):
+        x_ref, leg_ref = stream.take(step)
+        place_out = lax.rem(step, BEHIND)
+        out_ref = out_all.at[place_out]
+        work = []
+        for pair in range(sz.block // 2):
+            place = step * (sz.block // 2) + pair
+            numbers, odds, tiles = pair_state(sz, wave, band, place)
+            lefts = []
+            for side in range(2):
+                at = pl.multiple_of(spot_of(sz, place, odds[side]) * sz.rows, sz.rows)
+                lefts.append(spots[pl.ds(at, sz.rows), :])
+            left = jnp.concatenate(lefts, axis=0).T.astype(jnp.bfloat16)[0:pad]
+            tables = []
+            for side, tile in tiles:
+                cols = pl.ds(pl.multiple_of(tile * SLAB, SLAB), SLAB)
+                table = leg_ref[2 * pair + side, :, cols].astype(jnp.float32)
+                tables.append(jnp.concatenate([
+                    jnp.where(side == 0, table, 0.0), jnp.where(side == 1, table, 0.0),
+                ], axis=0).astype(jnp.bfloat16))
+            work.append((numbers, tiles, left, tables))
+        for pair in range(sz.block // 2):
+            _, tiles, left, tables = work[pair]
+            for k in range(0, len(tiles), 2):
+                count = min(2, len(tiles) - k)
+                tends = dot(left, jnp.concatenate(tables[k:k + count], axis=1))
+                for kk in range(count):
+                    side, tile = tiles[k + kk]
+                    for c in range(2):
+                        rows = pl.ds(side * pitch + 2 * tile + c, sz.field_pad, stride=2 * sz.tiles)
+                        wide[pair, rows, :] = tends[
+                            c * sz.field_pad:(c + 1) * sz.field_pad, kk * SLAB:(kk + 1) * SLAB
+                        ]
+        @pl.when(step >= BEHIND)
+        def _():
+            leave(step - BEHIND).wait()
+
+        run = 4 * sz.tiles if sz.fields % 2 == 0 else 2 * sz.tiles
+        row = remainder(iota((run, SLAB), 0), 2 * sz.tiles)
+        degree = quotient(row, 2) * SLAB + iota((run, SLAB), 1)
+        for pair in range(sz.block // 2):
+            numbers = work[pair][0]
+            old = x_ref[pl.ds(pair * height, height), :].astype(jnp.float32)
+            for side in range(2):
+                live = degree >= jnp.where(numbers[side] < 0, sz.degrees, numbers[side])
+                for at in range(0, sz.slot_rows, run):
+                    tend = wide[pair, pl.ds(side * pitch + at, run), :]
+                    new = old[side * sz.slot_rows + at:side * sz.slot_rows + at + run] + time_step * tend
+                    new = jnp.where(live, new * inverse[pl.ds(at, run), :], 0.0)
+                    out_ref[pl.ds(pair * height + side * sz.slot_rows + at, run), :] = new
+        leave(step).start()
+        return carry
+
+    lax.fori_loop(0, sz.steps, block, 0)
+    for step in range(max(0, sz.steps - BEHIND), sz.steps):
+        leave(jnp.int32(step)).wait()
 
 
 def params(mib):
@@ -502,10 +554,6 @@
 
 def smem():
     return pl.BlockSpec(memory_space=pltpu.SMEM)
-
-
-def whole_block(shape):
-    return pl.BlockSpec(shape, lambda *_: (0,) * len(shape))
 
 
 def shards(spectra, legendre, slot_wave, row_points, gauss_weight, layer_depth, mode_speed):
@@ -515,30 +563,31 @@
 
     tiled = spectra.reshape(slots, 2, fields, sz.tiles, SLAB)
     tiled = with_layout_constraint(tiled, Layout((0, 2, 3, 1, 4)))
-    lines = tiled.transpose(0, 2, 3, 1, 4).reshape(slots * sz.slot_rows, SLAB)
-    tables = legendre.transpose(0, 2, 1)
+    lines = tiled.transpose(0, 2, 3, 1, 4).reshape(sz.steps, sz.block * sz.slot_rows, SLAB)
+    tables = legendre.transpose(0, 2, 1).reshape(sz.steps, sz.block, sz.rows, degrees)
 
     rounds = geo_rounds(sz)
     tail = up_to((sz.field_pad - sz.fields) * 2 * sz.tiles, 16)
     wide_shape = pltpu.VMEM((sz.block // 2, 2 * sz.slot_rows + tail, SLAB), jnp.float32)
     spots_shape = pltpu.VMEM((sz.spots * sz.rows, SLAB), jnp.float32)
-    lines_block = (sz.block * sz.slot_rows, SLAB)
-    table_block = (sz.block, sz.rows, degrees)
+    stream_scratch = [
+        pltpu.VMEM(lines.shape, jnp.bfloat16),
+        pltpu.VMEM(tables.shape, jnp.bfloat16),
+        pltpu.SemaphoreType.DMA((sz.steps,)),
+        pltpu.SemaphoreType.DMA((sz.steps,)),
+    ]
+    anywhere = pl.BlockSpec(memory_space=pl.ANY)
+    vmem = pl.BlockSpec(memory_space=pltpu.VMEM)
     send_shape = (sz.bands, sz.groups, sz.chunk, SLAB)
     geo_shape = (sz.rows // 2, sz.spots, SLAB)
 
     sent, *geo = pl.pallas_call(
         functools.partial(inverse_kernel, sz, rounds),
-        grid=(sz.steps,),
-        in_specs=[
-            smem(), smem(), smem(), smem(),
-            pl.BlockSpec(lines_block, lambda i: (i, 0)),
-            pl.BlockSpec(table_block, lambda i: (i, 0, 0)),
-        ],
-        out_specs=[whole_block(send_shape)] + [whole_block(geo_shape)] * len(rounds),
+        in_specs=[smem(), smem(), smem(), smem(), anywhere, anywhere],
+        out_specs=[vmem] * (1 + len(rounds)),
         out_shape=[jax.ShapeDtypeStruct(send_shape, jnp.bfloat16)]
         + [jax.ShapeDtypeStruct(geo_shape, jnp.bfloat16)] * len(rounds),
-        scratch_shapes=[wide_shape, spots_shape, pltpu.VMEM((sz.spots, SLAB), jnp.int32)],
+        scratch_shapes=[wide_shape, spots_shape, pltpu.VMEM((sz.spots, SLAB), jnp.int32), *stream_scratch],
         compiler_params=params(56),
         name="inverse_legendre",
     )(slot_wave, row_points, gauss_weight, layer_depth, lines, tables)
@@ -576,10 +625,9 @@
         (*geo, arrived, basis, even_row, even_col)
     )
     moved = [lax.ppermute(geo[turn], "lev", pairs) for turn, pairs in enumerate(rounds)]
-    vmem = pl.BlockSpec(memory_space=pltpu.VMEM)
     returned = pl.pallas_call(
         functools.partial(grid_kernel, sz),
-        in_specs=[smem(), smem(), vmem, vmem, vmem, pl.BlockSpec(memory_space=pl.ANY)],
+        in_specs=[smem(), smem(), vmem, vmem, vmem, anywhere],
         out_specs=vmem,
         out_shape=jax.ShapeDtypeStruct(send_shape, jnp.bfloat16),
         scratch_shapes=[
@@ -601,18 +649,15 @@
 
     out = pl.pallas_call(
         functools.partial(forward_kernel, sz),
-        grid=(sz.steps,),
-        in_specs=[
-            smem(), smem(),
-            whole_block(send_shape), *([whole_block(geo_shape)] * len(rounds)),
-            pl.BlockSpec(lines_block, lambda i: (i, 0)),
-            pl.BlockSpec(table_block, lambda i: (i, 0, 0)),
-        ],
-        out_specs=pl.BlockSpec(lines_block, lambda i: (i, 0)),
-        out_shape=jax.ShapeDtypeStruct((slots * sz.slot_rows, SLAB), jnp.float32),
+        in_specs=[smem(), smem()] + [vmem] * (1 + len(rounds)) + [anywhere, anywhere],
+        out_specs=anywhere,
+        out_shape=jax.ShapeDtypeStruct(lines.shape, jnp.float32),
         scratch_shapes=[
             pltpu.VMEM((sz.block // 2, 4 * sz.field_pad * sz.tiles, SLAB), jnp.float32), spots_shape,
             pltpu.VMEM((sz.slot_rows, SLAB), jnp.float32),
+            pltpu.VMEM((BEHIND, *lines.shape[1:]), jnp.float32),
+            pltpu.SemaphoreType.DMA((BEHIND,)),
+            *stream_scratch,
         ],
         compiler_params=params(56),
         name="forward_legendre",

time: 110 us -> 92.2 us (0.84); the launches traced: 108 us -> 91.8 us
  Pallas kernels: 76 us -> 59.7 us
    pallas_call x2, Pallas kernels: 61.4 us -> 45.1 us  [the longest x1 28.6 us: shards(): pl.pallas_call(functools.partial(forward_kernel, sz), in_specs=[smem(), s...]
  transfers between devices with their start and end apart: 3 -> 3, of which waited for: 1 -> 1; matrix products, arithmetic and copies ran while one was open for 2% -> 3% of each run, Pallas kernels for 14% -> 16%
where the time goes in v5:
time: 92.2 us; the launch traced here: 91.8 us
  Pallas kernels  59.7 us (65%)
  blocking collectives  16.1 us (17%)
  starting transfers between devices  8.65 us (9%)
  waiting for transfers between devices  4.74 us (5%)
  local copies, waits for them, and re-layouts  2.49 us (3%)
    pallas_call x1, Pallas kernels, shards(): pl.pallas_call(functools.partial(forward_kernel, sz), in_specs=[smem(), s...  28.6 us
    pallas_call x1, Pallas kernels, shards(): pl.pallas_call(functools.partial(inverse_kernel, sz, rounds), in_specs=[s...  16.5 us
    all_to_all x1, blocking collectives, shards(): lax.all_to_all(returned.reshape(flat), both, split_axis=0, concat_axis=0,...  16.1 us
    pallas_call x1, Pallas kernels, shards(): pl.pallas_call(functools.partial(grid_kernel, sz), in_specs=[smem(), smem...  9 us
    all_to_all x1, starting transfers between devices, shards(): lax.all_to_all(sent.reshape(flat), both, split_axis=0, concat_axis=0, til...  7.3 us
    pallas_call x1, Pallas kernels, shards(): pl.pallas_call(functools.partial(basis_kernel, sz), grid=(sz.sorted // hi...  5.64 us
    all_to_all x1, waiting for transfers between devices, shards(): lax.all_to_all(sent.reshape(flat), both, split_axis=0, concat_axis=0, til...  4.73 us
  transfers between devices with their start and end apart: 3, of which 1 were waited for; matrix products, arithmetic and copies ran while one was open for 3% of the time, Pallas kernels for 16%

profile of v5, /device:TPU:0, one launch (start us, length us, event | category | flops | bytes accessed | tf_op | source)
XLA Modules:
  0.0 91.8 jit_solution(14263918937616985274)
XLA Ops:
  0.0 0.0 copy-start.3
  0.0 16.5 %inverse_legendre.1 = (bf16[8,4,40,128]{3,2,1,0:T(8,128)(2,1)}, bf16[8,160,128]{2,1,0:T(8,128)(2,1)}, bf16[8,160,128]{2,1,0:T(8,128)(2,1)}) custom-call(s32[1280]{0:T(1024)} %wave.3, s32[16]{0:T(128)} %points.4, f32[16]{0:T(128)} %gauss.3, f32[24]{0:T(128)} %layer_depth.1, bf16[20,4800,128]{2,1,0:T(8,128)(2,1)} %bitcast.22, bf16[20,8,16,1280]{3,2,1,0:T(8,128)(2,1)} %bitcast.24), custom_call_target="tpu_custom_call" | custom-call | tf_op jit(solution)/shard_map/inverse_legendre/pallas_call | solution.py:584
  16.5 7.3 %all-to-all-start = ((bf16[32,40,128]{2,1,0:T(8,128)(2,1)}), bf16[32,40,128]{2,1,0:T(8,128)(2,1)S(1)}, u32[]{:S(2)}, u32[]{:S(2)}) async-start(bf16[32,40,128]{2,1,0:T(8,128)(2,1)} %bitcast.29), calls=%async_computation | async-start | bytes 655360 | tf_op jit(solution)/shard_map/all_to_all | solution.py:599
  23.8 0.0 copy-done.3
  23.8 0.3 reshape.39
  24.1 0.3 slice_reduce_fusion
  24.5 0.1 squeeze.8
  24.5 0.1 squeeze.7
  24.7 0.1 reshape_reshape.7
  24.8 0.7 reshape_reshape.6.even_row
  25.4 5.6 %basis.1.basis_hbm = bf16[4,640,1408]{2,1,0:T(8,128)(2,1)} custom-call(s32[16]{0:T(128)} %points.4), custom_call_target="tpu_custom_call" | custom-call | flops 18022400 | bytes 7208960 | tf_op jit(solution)/shard_map/basis/pallas_call | solution.py:609
  31.1 4.7 %all-to-all-done = bf16[32,40,128]{2,1,0:T(8,128)(2,1)S(1)} async-done(((bf16[32,40,128]{2,1,0:T(8,128)(2,1)}), bf16[32,40,128]{2,1,0:T(8,128)(2,1)S(1)}, u32[]{:S(2)}, u32[]{:S(2)}) %all-to-all-start) | async-done | bytes 327712 | tf_op jit(solution)/shard_map/all_to_all | solution.py:599
  35.8 0.0 copy-start
  35.8 0.7 collective-permute-start
  36.5 0.7 collective-permute-start.1
  37.2 0.9 %copy.10.even_col = s32[640,1]{1,0:T(8,128)} copy(s32[640,1]{0,1:T(1,128)S(1)} %reshape_reshape.7) | data formatting | bytes 5120 | tf_op jit(solution)/shard_map/optimization_barrier | solution.py:624
  38.1 0.0 copy-done
  38.1 9.0 %grid_products.1 = bf16[8,4,40,128]{3,2,1,0:T(8,128)(2,1)} custom-call(s32[16]{0:T(128)} %points.4, f32[16]{0:T(128)} %gauss.3, bf16[8,4,40,128]{3,2,1,0:T(8,128)(2,1)} %bitcast.27, s32[1,640]{1,0:T(1,128)} %reshape_reshape.6.even_row, s32[640,1]{1,0:T(8,128)} %copy.10.even_col, bf16[4,640,1408]{2,1,0:T(8,128)(2,1)} %basis.1.basis_hbm), custom_call_target="tpu_custom_call" | custom-call | flops 1845493760 | bytes 7208960 | tf_op jit(solution)/shard_map/grid_products/pallas_call | solution.py:628
  47.1 0.0 collective-permute-done.refs_0_
  47.1 0.0 copy-start.1
  47.1 0.0 collective-permute-done.1.refs_1_
  47.1 0.0 copy-start.2
  47.2 16.1 %all_to_all.21 = bf16[32,40,128]{2,1,0:T(8,128)(2,1)} all-to-all(bf16[32,40,128]{2,1,0:T(8,128)(2,1)} %bitcast.28), channel_id=1, replica_groups=mesh['band'=8,'lev'=4] {'band','lev'}, dimensions={0} | all-to-all | bytes 655360 | tf_op jit(solution)/shard_map/all_to_all | solution.py:648
  63.3 0.0 copy-done.1
  63.3 0.0 copy-done.2
  63.3 28.6 %forward_legendre.1 = f32[20,4800,128]{2,1,0:T(8,128)} custom-call(s32[1280]{0:T(1024)} %wave.3, f32[30]{0:T(128)} %speed.1, bf16[8,4,40,128]{3,2,1,0:T(8,128)(2,1)} %bitcast.26, bf16[8,160,128]{2,1,0:T(8,128)(2,1)} %copy-done.1, bf16[8,160,128]{2,1,0:T(8,128)(2,1)} %copy-done.2, bf16[20,4800,128]{2,1,0:T(8,128)(2,1)} %bitcast.23, ...), custom_call_target="tpu_custom_call" | custom-call | tf_op jit(solution)/shard_map/forward_legendre/pallas_call | solution.py:650
  (2 shorter events, 0.0 us)
Async XLA Ops:
  0.0 23.8 %copy-start.3 = (s32[1280]{0:T(1024)S(1)}, s32[1280]{0:T(1024)}, u32[]{:S(2)}) copy-start(s32[1280]{0:T(1024)} %wave.3) | copy-start | bytes 15364
  16.5 19.3 %all-to-all-start = ((bf16[32,40,128]{2,1,0:T(8,128)(2,1)}), bf16[32,40,128]{2,1,0:T(8,128)(2,1)S(1)}, u32[]{:S(2)}, u32[]{:S(2)}) async-start(bf16[32,40,128]{2,1,0:T(8,128)(2,1)} %bitcast.29), calls=%async_computation | async-start | bytes 655360 | tf_op jit(solution)/shard_map/all_to_all | solution.py:599
  35.8 2.3 %copy-start = (bf16[32,40,128]{2,1,0:T(8,128)(2,1)}, bf16[32,40,128]{2,1,0:T(8,128)(2,1)S(1)}, u32[]{:S(2)}) copy-start(bf16[32,40,128]{2,1,0:T(8,128)(2,1)S(1)} %all-to-all-done) | copy-start | bytes 983044
  35.8 11.3 %collective-permute-start = (bf16[8,160,128]{2,1,0:T(8,128)(2,1)}, bf16[8,160,128]{2,1,0:T(8,128)(2,1)S(1)}, u32[]{:S(2)}, u32[]{:S(2)}) collective-permute-start(bf16[8,160,128]{2,1,0:T(8,128)(2,1)} %get-tuple-element.26), channel_id=1, source_target_pairs={{1,3},{5,7},{9,11},{13,15},{17,19},{21,23},{25,27},{29,31}} | collective-permute-start | bytes 983048 | tf_op jit(solution)/shard_map/ppermute | solution.py:627
  36.5 10.6 %collective-permute-start.1 = (bf16[8,160,128]{2,1,0:T(8,128)(2,1)}, bf16[8,160,128]{2,1,0:T(8,128)(2,1)S(1)}, u32[]{:S(2)}, u32[]{:S(2)}) collective-permute-start(bf16[8,160,128]{2,1,0:T(8,128)(2,1)} %get-tuple-element.27), channel_id=1, source_target_pairs={{2,3},{6,7},{10,11},{14,15},{18,19},{22,23},{26,27},{30,31}} | collective-permute-start | bytes 983048 | tf_op jit(solution)/shard_map/ppermute | solution.py:627
  47.1 16.1 %copy-start.1 = (bf16[8,160,128]{2,1,0:T(8,128)(2,1)}, bf16[8,160,128]{2,1,0:T(8,128)(2,1)S(1)}, u32[]{:S(2)}) copy-start(bf16[8,160,128]{2,1,0:T(8,128)(2,1)S(1)} %collective-permute-done.refs_0_) | copy-start | bytes 983044
  47.1 16.1 %copy-start.2 = (bf16[8,160,128]{2,1,0:T(8,128)(2,1)}, bf16[8,160,128]{2,1,0:T(8,128)(2,1)S(1)}, u32[]{:S(2)}) copy-start(bf16[8,160,128]{2,1,0:T(8,128)(2,1)S(1)} %collective-permute-done.1.refs_1_) | copy-start | bytes 983044

commit v6 on v5

--- a/solution.py
+++ b/solution.py
@@ -38,6 +38,7 @@
         self.bands, self.groups = bands, groups
         self.slots, self.fields, self.degrees, self.rows = slots, fields, degrees, rows
         self.tiles = degrees // SLAB
+        self.packed = self.tiles + 1
         self.slot_rows = fields * self.tiles * 2
         self.field_pad = up_to(fields, 8)
         self.share = -(-fields // groups)
@@ -125,7 +126,7 @@
     item = remainder(rest, sz.share)
     start = remainder(lev * sz.fields, sz.groups)
     field = remainder(group - start + sz.groups, sz.groups) + sz.groups * item
-    want = ((quarter * 2 + row) * 2 + comp) * sz.field_pad + field
+    want = ((quarter * 2 + row) * sz.field_pad + field) * 2 + comp
     want = jnp.where((field < sz.fields) & (quarter < sz.quarters), want, -1)
     return one_hot(iota((tall, wide), 0) == want)
 
@@ -135,17 +136,52 @@
     return (odd * sizes.halves + half) * sizes.chunk + (place - half * sizes.chunk_live)
 
 
-def pair_state(sizes, wave, band, place):
-    slot = band * sizes.slots + 2 * place
-    first, second = wave[slot], wave[slot + 1]
-    odd = first & 1
-    start = quotient(jnp.maximum(first, 0), SLAB)
-    live = sizes.tiles - start
-    tiles = []
-    for k in range(sizes.tiles + 1):
-        side = jnp.where(k < live, 0, 1)
-        tiles.append((side, jnp.where(k < live, start + k, k - 1)))
-    return (first, second), (odd, 1 - odd), tiles
+class Pair:
+    def __init__(self, sizes, wave, band, place):
+        self.sizes, self.place = sizes, place
+        slot = band * sizes.slots + 2 * place
+        self.numbers = wave[slot], wave[slot + 1]
+        odd = self.numbers[0] & 1
+        self.odds = odd, 1 - odd
+        self.start = quotient(jnp.maximum(self.numbers[0], 0), SLAB)
+        self.split = sizes.tiles - self.start
+
+    def spot(self, side):
+        sz = self.sizes
+        half = self.place // sz.chunk_live
+        first = (self.odds[side] * sz.halves + half) * sz.chunk
+        return first + (self.place - half * sz.chunk_live)
+
+    def rows(self, side):
+        return pl.ds(pl.multiple_of(self.spot(side) * self.sizes.rows, self.sizes.rows), self.sizes.rows)
+
+    def tile(self, k):
+        return jnp.where(k < self.split, self.start + k, k - 1)
+
+    def columns(self):
+        place = iota((1, self.sizes.packed * SLAB), 1)
+        first = place < self.split * SLAB
+        degree = jnp.where(first, place + self.start * SLAB, place - SLAB)
+        floors = [jnp.where(n < 0, self.sizes.degrees, n) for n in self.numbers]
+        return first, degree >= jnp.where(first, floors[0], floors[1])
+
+    def by_start(self, emit):
+        def branch(low, high):
+            if high - low == 1:
+                emit(low)
+                return
+            middle = (low + high) // 2
+            pl.when(self.start < middle)(lambda: branch(low, middle))
+            pl.when(self.start >= middle)(lambda: branch(middle, high))
+
+        branch(0, self.sizes.tiles)
+
+    def tables(self, leg):
+        first, live = self.columns()
+        leg = leg.astype(jnp.float32)
+        own = jnp.where(first & live, leg, 0.0)
+        other = jnp.where(first, 0.0, jnp.where(live, leg, 0.0))
+        return jnp.concatenate([own, other], axis=0).astype(jnp.bfloat16)
 
 
 AHEAD = 6
@@ -153,93 +189,90 @@
 
 
 class Stream:
-    def __init__(self, sizes, x_hbm, leg_hbm, x_all, leg_all, x_sems, leg_sems):
-        self.sizes = sizes
-        self.pairs = ((x_hbm, x_all, x_sems), (leg_hbm, leg_all, leg_sems))
-
-    def copies(self, step):
-        return [
-            pltpu.make_async_copy(hbm.at[step], here.at[step], sems.at[step])
-            for hbm, here, sems in self.pairs
-        ]
-
-    def start(self, step):
-        for copy in self.copies(step):
-            copy.start()
+    def __init__(self, sizes, pair_at, x_hbm, leg_hbm, x_all, leg_all, x_sems, leg_sems):
+        self.sizes, self.pair_at = sizes, pair_at
+        self.x_hbm, self.leg_hbm, self.x_all, self.leg_all = x_hbm, leg_hbm, x_all, leg_all
+        self.x_sems, self.leg_sems = x_sems, leg_sems
+
+    def start(self, place):
+        pair = self.pair_at(place)
+        tiles = self.sizes.tiles
+
+        def emit(start):
+            split = tiles - start
+            for side, first, here in ((0, start, (0, split)), (1, split - 1, (split, tiles + 1))):
+                slot = 2 * place + side
+                pltpu.make_async_copy(
+                    self.x_hbm.at[slot, :, pl.ds(first, tiles - first)],
+                    self.x_all.at[place, :, pl.ds(here[0], here[1] - here[0])],
+                    self.x_sems.at[place],
+                ).start()
+                pltpu.make_async_copy(
+                    self.leg_hbm.at[slot, :, pl.ds(first * SLAB, (tiles - first) * SLAB)],
+                    self.leg_all.at[place, :, pl.ds(here[0] * SLAB, (here[1] - here[0]) * SLAB)],
+                    self.leg_sems.at[place],
+                ).start()
+
+        pair.by_start(emit)
 
     def begin(self):
-        for step in range(min(AHEAD, self.sizes.steps)):
-            self.start(step)
+        def one(place, carry):
+            self.start(place)
+            return carry
+
+        lax.fori_loop(0, min(AHEAD * self.sizes.block // 2, self.sizes.slots // 2), one, 0)
 
     def take(self, step):
+        each = self.sizes.block // 2
+
         @pl.when(step + AHEAD < self.sizes.steps)
         def _():
-            self.start(step + AHEAD)
-
-        for copy in self.copies(step):
-            copy.wait()
-        return tuple(here.at[step] for _, here, _ in self.pairs)
+            for k in range(each):
+                self.start((step + AHEAD) * each + k)
+
+        for k in range(each):
+            place = step * each + k
+            for here, sems in ((self.x_all, self.x_sems), (self.leg_all, self.leg_sems)):
+                pltpu.make_async_copy(here.at[place], here.at[place], sems.at[place]).wait()
 
 
 def inverse_kernel(sizes, rounds, wave, points, gauss, layer_depth, x_hbm, leg_hbm, send_ref, *refs):
     sz = sizes
     geo_refs = refs[:len(rounds)]
-    wide, spots, numbers, *stream = refs[len(rounds):]
-    stream = Stream(sz, x_hbm, leg_hbm, *stream)
-    stream.begin()
+    spots, numbers, x_all, leg_all, *sems = refs[len(rounds):]
     band = lax.axis_index("band")
     lev = lax.axis_index("lev")
+    pair_at = functools.partial(Pair, sz, wave, band)
+    stream = Stream(sz, pair_at, x_hbm, leg_hbm, x_all, leg_all, *sems)
+    stream.begin()
     pad = 2 * sz.field_pad
-    height = 2 * sz.slot_rows
     spots[...] = jnp.zeros_like(spots)
     numbers[...] = jnp.full_like(numbers, -1)
-    wide[:, pl.ds(height, wide.shape[1] - height), :] = jnp.zeros(
-        (wide.shape[0], wide.shape[1] - height, SLAB), jnp.float32
-    )
 
     def block(step, carry):
-        x_ref, leg_ref = stream.take(step)
-        for pair in range(sz.block // 2):
-            rows = x_ref[pl.ds(pair * height, height), :]
-            wide[pair, pl.ds(0, height), :] = rows.astype(jnp.float32)
+        stream.take(step)
         found = []
-        for pair in range(sz.block // 2):
-            place = step * (sz.block // 2) + pair
-            numbers_here, odds, tiles = pair_state(sz, wave, band, place)
-            values, tables = [], []
-            for side, tile in tiles:
-                start = side * sz.slot_rows + 2 * tile
-                values.append(jnp.concatenate([
-                    wide[pair, pl.ds(start + c, sz.field_pad, stride=2 * sz.tiles), :] for c in range(2)
-                ], axis=0).astype(jnp.bfloat16))
-                cols = pl.ds(pl.multiple_of(tile * SLAB, SLAB), SLAB)
-                table = leg_ref[2 * pair + side, :, cols].astype(jnp.float32)
-                number = jnp.where(side == 0, numbers_here[0], numbers_here[1])
-                table = jnp.where(iota((1, SLAB), 1) + tile * SLAB >= number, table, 0.0)
-                tables.append(jnp.concatenate([
-                    jnp.where(side == 0, table, 0.0), jnp.where(side == 1, table, 0.0),
-                ], axis=0).astype(jnp.bfloat16))
-            total = dot(
-                jnp.concatenate(tables, axis=1), jnp.concatenate(values, axis=1), ((1,), (1,))
-            )
+        for k in range(sz.block // 2):
+            place = step * (sz.block // 2) + k
+            pair = pair_at(place)
+            values = jnp.concatenate([
+                x_all[place, :, t].reshape(2 * sz.fields, SLAB) for t in range(sz.packed)
+            ], axis=1)
+            total = dot(pair.tables(leg_all[place]), values, ((1,), (1,)))
             for side in range(2):
-                found.append((
-                    spot_of(sz, place, odds[side]), numbers_here[side],
-                    total[side * sz.rows:(side + 1) * sz.rows],
-                ))
-        for spot, number, total in found:
-            at = pl.multiple_of(spot * sz.rows, sz.rows)
-            spots[pl.ds(at, sz.rows), 0:pad] = total
-            numbers[pl.ds(spot, 1), :] = jnp.full((1, SLAB), number, jnp.int32)
+                found.append((pair, side, total[side * sz.rows:(side + 1) * sz.rows]))
+        for pair, side, total in found:
+            spots[pair.rows(side), 0:2 * sz.fields] = total
+            number = jnp.full((1, SLAB), pair.numbers[side], jnp.int32)
+            numbers[pl.ds(pair.spot(side), 1), :] = number
         return carry
 
     lax.fori_loop(0, sz.steps, block, 0)
     spread = spread_matrix(sz, lev)
     shape = (2 * pad, SLAB)
     src, dst = iota(shape, 0), iota(shape, 1)
-    bits = sz.field_pad.bit_length() - 1
-    from_field, from_side = src & (sz.field_pad - 1), src >> bits
-    to_field, to_side = dst & (sz.field_pad - 1), dst >> bits
+    from_row, from_field, from_comp = src // pad, (src & (pad - 1)) >> 1, src & 1
+    to_row, to_field, to_comp = dst // pad, (dst & (pad - 1)) >> 1, dst & 1
     weights = []
     for pairs in rounds:
         first = jnp.int32(2 * LEVELS + sz.fields)
@@ -248,7 +281,7 @@
         under = lev * sz.fields + from_field - TEMPER * LEVELS
         above = first + to_field
         hit = (
-            (from_side == to_side)
+            (from_row == to_row) & (from_comp == to_comp)
             & (from_field < sz.fields) & (to_field < sz.fields)
             & (above >= 0) & (above <= under)
         )
@@ -260,7 +293,7 @@
         weights.append(jnp.concatenate([high, low], axis=0))
     number = numbers[...]
     lane = iota((sz.spots, SLAB), 1)
-    known = (number >= 0) & ~((number == 0) & (lane & sz.field_pad != 0))
+    known = (number >= 0) & ~((number == 0) & (lane & 1 == 1))
     for rp in range(sz.rows // 2):
         exact = jnp.concatenate([
             spots[pl.ds(2 * rp + r, sz.spots, stride=sz.rows), :][:, 0:pad] for r in range(2)
@@ -453,17 +486,42 @@
         send_ref[:, g] = part.astype(jnp.bfloat16)
 
 
-def forward_kernel(
-    sizes, wave, speed, back_ref, *refs,
-):
+def zeros_kernel(sizes, wave, out_hbm, zeros, sems):
+    sz = sizes
+    band = lax.axis_index("band")
+    zeros[...] = jnp.zeros_like(zeros)
+
+    def one(place, carry):
+        def emit(start):
+            for side, count in ((0, start), (1, sz.tiles - 1 - start)):
+                if count:
+                    pltpu.make_async_copy(
+                        zeros.at[:, pl.ds(0, count)],
+                        out_hbm.at[2 * place + side, :, pl.ds(0, count)],
+                        sems.at[place],
+                    ).start()
+
+        Pair(sz, wave, band, place).by_start(emit)
+        return carry
+
+    def done(place, carry):
+        pltpu.make_async_copy(zeros, zeros, sems.at[place]).wait()
+        return carry
+
+    lax.fori_loop(0, sz.slots // 2, one, 0)
+    lax.fori_loop(0, sz.slots // 2, done, 0)
+
+
+def forward_kernel(sizes, wave, speed, back_ref, *refs):
     sz = sizes
     geo_refs = refs[:-12]
-    x_hbm, leg_hbm, out_hbm, wide, spots, inverse, out_all, out_sems, *stream = refs[-12:]
-    stream = Stream(sz, x_hbm, leg_hbm, *stream)
+    x_hbm, leg_hbm, _, out_hbm, spots, inverse, out_all, out_sems, x_all, leg_all, *sems = refs[-12:]
+    band = lax.axis_index("band")
+    pair_at = functools.partial(Pair, sz, wave, band)
+    stream = Stream(sz, pair_at, x_hbm, leg_hbm, x_all, leg_all, *sems)
     stream.begin()
-    band = lax.axis_index("band")
     pad = 2 * sz.field_pad
-    height = 2 * sz.slot_rows
+    each = sz.block // 2
 
     gather = spread_matrix(sz, lax.axis_index("lev"))
     for rp in range(sz.rows // 2):
@@ -478,74 +536,68 @@
             part = rows[:, r * pad:(r + 1) * pad]
             part = jnp.concatenate([part, jnp.zeros((sz.spots, SLAB - pad), jnp.float32)], axis=1)
             spots[pl.ds(2 * rp + r, sz.spots, stride=sz.rows), :] = part
+    row = iota((pad, SLAB), 0)
+    speeds = jnp.ones((pad, SLAB), jnp.float32)
     for f in range(sz.fields):
-        rows = 2 * sz.tiles
-        degree = quotient(iota((rows, SLAB), 0), 2) * SLAB + iota((rows, SLAB), 1)
+        speeds = jnp.where(row >> 1 == f, speed[f], speeds)
+    for t in range(sz.tiles):
+        degree = iota((1, SLAB), 1) + t * SLAB
         helm = (degree * (degree + 1)).astype(jnp.float32) / float(sz.trunc * (sz.trunc + 1))
-        inverse[pl.ds(f * rows, rows), :] = 1.0 / (1.0 + time_step * time_step * helm * speed[f])
-
-    pitch = sz.field_pad * 2 * sz.tiles
-
-    def leave(step):
+        inverse[t] = 1.0 / (1.0 + time_step * time_step * helm * speeds)
+
+    def leave(place, k):
+        at = lax.rem(place // each, BEHIND)
+
+        def emit(start):
+            split = sz.tiles - start
+            for side, first, here in ((0, start, (0, split)), (1, split - 1, (split, sz.packed))):
+                pltpu.make_async_copy(
+                    out_all.at[at, k, :, pl.ds(here[0], here[1] - here[0])],
+                    out_hbm.at[2 * place + side, :, pl.ds(first, sz.tiles - first)],
+                    out_sems.at[at, k],
+                ).start()
+
+        pair_at(place).by_start(emit)
+
+    def left(step):
         at = lax.rem(step, BEHIND)
-        return pltpu.make_async_copy(out_all.at[at], out_hbm.at[step], out_sems.at[at])
+        for k in range(each):
+            pltpu.make_async_copy(out_all.at[at, k], out_all.at[at, k], out_sems.at[at, k]).wait()
 
     def block(step, carry):
-        x_ref, leg_ref = stream.take(step)
-        place_out = lax.rem(step, BEHIND)
-        out_ref = out_all.at[place_out]
+        stream.take(step)
         work = []
-        for pair in range(sz.block // 2):
-            place = step * (sz.block // 2) + pair
-            numbers, odds, tiles = pair_state(sz, wave, band, place)
-            lefts = []
-            for side in range(2):
-                at = pl.multiple_of(spot_of(sz, place, odds[side]) * sz.rows, sz.rows)
-                lefts.append(spots[pl.ds(at, sz.rows), :])
-            left = jnp.concatenate(lefts, axis=0).T.astype(jnp.bfloat16)[0:pad]
-            tables = []
-            for side, tile in tiles:
-                cols = pl.ds(pl.multiple_of(tile * SLAB, SLAB), SLAB)
-                table = leg_ref[2 * pair + side, :, cols].astype(jnp.float32)
-                tables.append(jnp.concatenate([
-                    jnp.where(side == 0, table, 0.0), jnp.where(side == 1, table, 0.0),
-                ], axis=0).astype(jnp.bfloat16))
-            work.append((numbers, tiles, left, tables))
-        for pair in range(sz.block // 2):
-            _, tiles, left, tables = work[pair]
-            for k in range(0, len(tiles), 2):
-                count = min(2, len(tiles) - k)
-                tends = dot(left, jnp.concatenate(tables[k:k + count], axis=1))
-                for kk in range(count):
-                    side, tile = tiles[k + kk]
-                    for c in range(2):
-                        rows = pl.ds(side * pitch + 2 * tile + c, sz.field_pad, stride=2 * sz.tiles)
-                        wide[pair, rows, :] = tends[
-                            c * sz.field_pad:(c + 1) * sz.field_pad, kk * SLAB:(kk + 1) * SLAB
-                        ]
+        for k in range(each):
+            place = step * each + k
+            pair = pair_at(place)
+            values = jnp.concatenate([spots[pair.rows(side), :] for side in range(2)], axis=0)
+            values = values.T.astype(jnp.bfloat16)[0:pad]
+            work.append((place, pair, values, pair.tables(leg_all[place])))
+
         @pl.when(step >= BEHIND)
         def _():
-            leave(step - BEHIND).wait()
-
-        run = 4 * sz.tiles if sz.fields % 2 == 0 else 2 * sz.tiles
-        row = remainder(iota((run, SLAB), 0), 2 * sz.tiles)
-        degree = quotient(row, 2) * SLAB + iota((run, SLAB), 1)
-        for pair in range(sz.block // 2):
-            numbers = work[pair][0]
-            old = x_ref[pl.ds(pair * height, height), :].astype(jnp.float32)
-            for side in range(2):
-                live = degree >= jnp.where(numbers[side] < 0, sz.degrees, numbers[side])
-                for at in range(0, sz.slot_rows, run):
-                    tend = wide[pair, pl.ds(side * pitch + at, run), :]
-                    new = old[side * sz.slot_rows + at:side * sz.slot_rows + at + run] + time_step * tend
-                    new = jnp.where(live, new * inverse[pl.ds(at, run), :], 0.0)
-                    out_ref[pl.ds(pair * height + side * sz.slot_rows + at, run), :] = new
-        leave(step).start()
+            left(step)
+
+        at = lax.rem(step, BEHIND)
+        for k in range(each):
+            place, pair, values, tables = work[k]
+            _, live = pair.columns()
+            for first in range(0, sz.packed, 2):
+                count = min(2, sz.packed - first)
+                tends = dot(values, tables[:, first * SLAB:(first + count) * SLAB])
+                for t in range(first, first + count):
+                    old = x_all[place, :, t].reshape(2 * sz.fields, SLAB).astype(jnp.float32)
+                    tend = tends[0:2 * sz.fields, (t - first) * SLAB:(t - first + 1) * SLAB]
+                    new = (old + time_step * tend) * inverse[pair.tile(t), 0:2 * sz.fields]
+                    new = jnp.where(live[:, t * SLAB:(t + 1) * SLAB], new, 0.0)
+                    out_all[at, k, :, t] = new.reshape(sz.fields, 2, SLAB)
+        for k in range(each):
+            leave(step * each + k, k)
         return carry
 
     lax.fori_loop(0, sz.steps, block, 0)
     for step in range(max(0, sz.steps - BEHIND), sz.steps):
-        leave(jnp.int32(step)).wait()
+        left(jnp.int32(step))
 
 
 def params(mib):
@@ -563,18 +615,17 @@
 
     tiled = spectra.reshape(slots, 2, fields, sz.tiles, SLAB)
     tiled = with_layout_constraint(tiled, Layout((0, 2, 3, 1, 4)))
-    lines = tiled.transpose(0, 2, 3, 1, 4).reshape(sz.steps, sz.block * sz.slot_rows, SLAB)
-    tables = legendre.transpose(0, 2, 1).reshape(sz.steps, sz.block, sz.rows, degrees)
+    tiled = tiled.transpose(0, 2, 3, 1, 4)
+    tables = legendre.transpose(0, 2, 1)
 
     rounds = geo_rounds(sz)
-    tail = up_to((sz.field_pad - sz.fields) * 2 * sz.tiles, 16)
-    wide_shape = pltpu.VMEM((sz.block // 2, 2 * sz.slot_rows + tail, SLAB), jnp.float32)
     spots_shape = pltpu.VMEM((sz.spots * sz.rows, SLAB), jnp.float32)
+    pairs = slots // 2
     stream_scratch = [
-        pltpu.VMEM(lines.shape, jnp.bfloat16),
-        pltpu.VMEM(tables.shape, jnp.bfloat16),
-        pltpu.SemaphoreType.DMA((sz.steps,)),
-        pltpu.SemaphoreType.DMA((sz.steps,)),
+        pltpu.VMEM((pairs, fields, sz.packed, 2, SLAB), jnp.bfloat16),
+        pltpu.VMEM((pairs, rows, sz.packed * SLAB), jnp.bfloat16),
+        pltpu.SemaphoreType.DMA((pairs,)),
+        pltpu.SemaphoreType.DMA((pairs,)),
     ]
     anywhere = pl.BlockSpec(memory_space=pl.ANY)
     vmem = pl.BlockSpec(memory_space=pltpu.VMEM)
@@ -587,10 +638,10 @@
         out_specs=[vmem] * (1 + len(rounds)),
         out_shape=[jax.ShapeDtypeStruct(send_shape, jnp.bfloat16)]
         + [jax.ShapeDtypeStruct(geo_shape, jnp.bfloat16)] * len(rounds),
-        scratch_shapes=[wide_shape, spots_shape, pltpu.VMEM((sz.spots, SLAB), jnp.int32), *stream_scratch],
+        scratch_shapes=[spots_shape, pltpu.VMEM((sz.spots, SLAB), jnp.int32), *stream_scratch],
         compiler_params=params(56),
         name="inverse_legendre",
-    )(slot_wave, row_points, gauss_weight, layer_depth, lines, tables)
+    )(slot_wave, row_points, gauss_weight, layer_depth, tiled, tables)
 
     sent, points_later, wave_later = lax.optimization_barrier((sent, row_points, slot_wave))
     both = ("band", "lev")
@@ -643,27 +694,44 @@
     )(
         row_points, gauss_weight, arrived.reshape(send_shape), even_row, even_col, basis,
     )
-    *moved, returned = lax.optimization_barrier((*moved, returned))
+    *moved, returned, wave_last = lax.optimization_barrier((*moved, returned, slot_wave))
 
     back = lax.all_to_all(returned.reshape(flat), both, split_axis=0, concat_axis=0, tiled=True)
 
+    out_shape = jax.ShapeDtypeStruct(tiled.shape, jnp.float32)
+    zeroed = pl.pallas_call(
+        functools.partial(zeros_kernel, sz),
+        in_specs=[smem()],
+        out_specs=anywhere,
+        out_shape=out_shape,
+        scratch_shapes=[
+            pltpu.VMEM((fields, sz.tiles - 1, 2, SLAB), jnp.float32),
+            pltpu.SemaphoreType.DMA((pairs,)),
+        ],
+        compiler_params=params(56),
+        cost_estimate=pl.CostEstimate(
+            flops=0, bytes_accessed=2 * slots * fields * degrees * 2, transcendentals=0,
+        ),
+        name="dead_zeros",
+    )(wave_last)
     out = pl.pallas_call(
         functools.partial(forward_kernel, sz),
-        in_specs=[smem(), smem()] + [vmem] * (1 + len(rounds)) + [anywhere, anywhere],
+        in_specs=[smem(), smem()] + [vmem] * (1 + len(rounds)) + [anywhere] * 3,
         out_specs=anywhere,
-        out_shape=jax.ShapeDtypeStruct(lines.shape, jnp.float32),
+        out_shape=out_shape,
+        input_output_aliases={5 + len(rounds): 0},
         scratch_shapes=[
-            pltpu.VMEM((sz.block // 2, 4 * sz.field_pad * sz.tiles, SLAB), jnp.float32), spots_shape,
-            pltpu.VMEM((sz.slot_rows, SLAB), jnp.float32),
-            pltpu.VMEM((BEHIND, *lines.shape[1:]), jnp.float32),
-            pltpu.SemaphoreType.DMA((BEHIND,)),
+            spots_shape,
+            pltpu.VMEM((sz.tiles, 2 * sz.field_pad, SLAB), jnp.float32),
+            pltpu.VMEM((BEHIND, sz.block // 2, fields, sz.packed, 2, SLAB), jnp.float32),
+            pltpu.SemaphoreType.DMA((BEHIND, sz.block // 2)),
             *stream_scratch,
         ],
         compiler_params=params(56),
         name="forward_legendre",
-    )(slot_wave, mode_speed, back.reshape(send_shape), *moved, lines, tables)
-
-    out = out.reshape(slots, fields, sz.tiles, 2, SLAB).transpose(0, 1, 3, 2, 4)
+    )(slot_wave, mode_speed, back.reshape(send_shape), *moved, tiled, tables, zeroed)
+
+    out = out.transpose(0, 1, 3, 2, 4)
     return out.reshape(slots, fields, 2, degrees).transpose(0, 2, 1, 3)
 
 

time: 92.2 us -> 115 us (1.25)
  Pallas kernels: 59.7 us -> 90.2 us
  blocking collectives: 16.1 us -> 0 us
  starting transfers between devices: 8.65 us -> 12.8 us
  waiting for transfers between devices: 4.74 us -> 7.6 us
    pallas_call x1, Pallas kernels: 28.6 us -> 48.5 us  [shards(): pl.pallas_call(functools.partial(forward_kernel, sz), in_specs=[smem(), s...]
    all_to_all x1 -> x0, blocking collectives: 16.1 us -> none  [shards(): lax.all_to_all(returned.reshape(flat), both, split_axis=0, concat_axis=0,...]
    pallas_call x0 -> x1, Pallas kernels: none -> 8.91 us  [shards(): pl.pallas_call(functools.partial(zeros_kernel, sz), in_specs=[smem()], ou...]
    all_to_all x0 -> x1, starting transfers between devices: none -> 4.17 us  [shards(): lax.all_to_all(returned.reshape(flat), both, split_axis=0, concat_axis=0,...]
    all_to_all x0 -> x1, waiting for transfers between devices: none -> 2.87 us  [shards(): lax.all_to_all(returned.reshape(flat), both, split_axis=0, concat_axis=0,...]
    pallas_call x1, Pallas kernels: 16.5 us -> 18.2 us  [shards(): pl.pallas_call(functools.partial(inverse_kernel, sz, rounds), in_specs=[s...]
  transfers between devices with their start and end apart: 3 -> 4, of which waited for: 1 -> 2; matrix products, arithmetic and copies ran while one was open for 3% -> 2% of each run, Pallas kernels for 16% -> 21%
where the time goes in v6:
time: 115 us; the launch traced here: 114 us
  Pallas kernels  90.2 us (78%)
  starting transfers between devices  12.8 us (11%)
  waiting for transfers between devices  7.6 us (7%)
  local copies, waits for them, and re-layouts  3.21 us (3%)
    pallas_call x1, Pallas kernels, shards(): pl.pallas_call(functools.partial(forward_kernel, sz), in_specs=[smem(), s...  48.5 us
    pallas_call x1, Pallas kernels, shards(): pl.pallas_call(functools.partial(inverse_kernel, sz, rounds), in_specs=[s...  18.2 us
    pallas_call x1, Pallas kernels, shards(): pl.pallas_call(functools.partial(grid_kernel, sz), in_specs=[smem(), smem...  8.99 us
    pallas_call x1, Pallas kernels, shards(): pl.pallas_call(functools.partial(zeros_kernel, sz), in_specs=[smem()], ou...  8.91 us
    all_to_all x1, starting transfers between devices, shards(): lax.all_to_all(sent.reshape(flat), both, split_axis=0, concat_axis=0, til...  7.3 us
    pallas_call x1, Pallas kernels, shards(): pl.pallas_call(functools.partial(basis_kernel, sz), grid=(sz.sorted // hi...  5.64 us
    all_to_all x1, waiting for transfers between devices, shards(): lax.all_to_all(sent.reshape(flat), both, split_axis=0, concat_axis=0, til...  4.72 us
    all_to_all x1, starting transfers between devices, shards(): lax.all_to_all(returned.reshape(flat), both, split_axis=0, concat_axis=0,...  4.17 us
  transfers between devices with their start and end apart: 4, of which 2 were waited for; matrix products, arithmetic and copies ran while one was open for 2% of the time, Pallas kernels for 21%

profile of v6, /device:TPU:0, one launch (start us, length us, event | category | flops | bytes accessed | tf_op | source)
XLA Modules:
  0.0 114.2 jit_solution(15113327861932781004)
XLA Ops:
  0.0 0.0 copy-start.4
  0.0 18.2 %inverse_legendre.1 = (bf16[8,4,40,128]{3,2,1,0:T(8,128)(2,1)}, bf16[8,160,128]{2,1,0:T(8,128)(2,1)}, bf16[8,160,128]{2,1,0:T(8,128)(2,1)}) custom-call(s32[1280]{0:T(1024)} %wave.4, s32[16]{0:T(128)} %points.4, f32[16]{0:T(128)} %gauss.3, f32[24]{0:T(128)} %layer_depth.1, bf16[160,30,10,2,128]{4,3,2,1,0:T(2,128)(2,1)} %bitcast.16, ...), custom_call_target="tpu_custom_call" | custom-call | tf_op jit(solution)/shard_map/inverse_legendre/pallas_call | solution.py:635
  18.2 7.3 %all-to-all-start = ((bf16[32,40,128]{2,1,0:T(8,128)(2,1)}), bf16[32,40,128]{2,1,0:T(8,128)(2,1)S(1)}, u32[]{:S(2)}, u32[]{:S(2)}) async-start(bf16[32,40,128]{2,1,0:T(8,128)(2,1)} %bitcast.23), calls=%async_computation | async-start | bytes 655360 | tf_op jit(solution)/shard_map/all_to_all | solution.py:650
  25.5 0.0 copy-done.4
  25.5 0.3 reshape.28
  25.8 0.3 slice_reduce_fusion
  26.2 0.1 squeeze.8
  26.2 0.1 squeeze.7
  26.4 0.1 reshape_reshape.7
  26.5 0.7 reshape_reshape.6.even_row
  27.2 5.6 %basis.1.basis_hbm = bf16[4,640,1408]{2,1,0:T(8,128)(2,1)} custom-call(s32[16]{0:T(128)} %points.4), custom_call_target="tpu_custom_call" | custom-call | flops 18022400 | bytes 7208960 | tf_op jit(solution)/shard_map/basis/pallas_call | solution.py:660
  32.8 4.7 %all-to-all-done = bf16[32,40,128]{2,1,0:T(8,128)(2,1)S(1)} async-done(((bf16[32,40,128]{2,1,0:T(8,128)(2,1)}), bf16[32,40,128]{2,1,0:T(8,128)(2,1)S(1)}, u32[]{:S(2)}, u32[]{:S(2)}) %all-to-all-start) | async-done | bytes 327712 | tf_op jit(solution)/shard_map/all_to_all | solution.py:650
  37.5 0.0 copy-start.1
  37.5 0.7 collective-permute-start
  38.2 0.7 collective-permute-start.1
  38.9 0.9 copy.11.even_col
  39.8 0.0 copy-done.1
  39.8 9.0 %grid_products.1 = bf16[8,4,40,128]{3,2,1,0:T(8,128)(2,1)} custom-call(s32[16]{0:T(128)} %points.4, f32[16]{0:T(128)} %gauss.3, bf16[8,4,40,128]{3,2,1,0:T(8,128)(2,1)} %bitcast.21, s32[1,640]{1,0:T(1,128)} %reshape_reshape.6.even_row, s32[640,1]{1,0:T(8,128)} %copy.11.even_col, bf16[4,640,1408]{2,1,0:T(8,128)(2,1)} %basis.1.basis_hbm), custom_call_target="tpu_custom_call" | custom-call | flops 1845493760 | bytes 7208960 | tf_op jit(solution)/shard_map/grid_products/pallas_call | solution.py:679
  48.8 0.0 collective-permute-done.refs_0_
  48.8 0.0 copy-start.2
  48.8 0.0 collective-permute-done.1.refs_1_
  48.8 0.0 copy-start.3
  48.8 4.2 %all-to-all-start.1 = ((bf16[32,40,128]{2,1,0:T(8,128)(2,1)}), bf16[32,40,128]{2,1,0:T(8,128)(2,1)S(1)}, u32[]{:S(2)}, u32[]{:S(2)}) async-start(bf16[32,40,128]{2,1,0:T(8,128)(2,1)} %bitcast.22), calls=%async_computation.1 | async-start | bytes 655360 | tf_op jit(solution)/shard_map/all_to_all | solution.py:699
  53.0 8.9 %dead_zeros.1.refs_4_ = f32[160,30,10,2,128]{4,3,2,1,0:T(2,128)} custom-call(s32[1280]{0:T(1024)} %wave.4), custom_call_target="tpu_custom_call" | custom-call | bytes 24576000 | tf_op jit(solution)/shard_map/dead_zeros/pallas_call | solution.py:702
  61.9 0.0 copy-done.2
  61.9 0.0 copy-done.3
  61.9 2.9 %all-to-all-done.1 = bf16[32,40,128]{2,1,0:T(8,128)(2,1)S(1)} async-done(((bf16[32,40,128]{2,1,0:T(8,128)(2,1)}), bf16[32,40,128]{2,1,0:T(8,128)(2,1)S(1)}, u32[]{:S(2)}, u32[]{:S(2)}) %all-to-all-start.1) | async-done | bytes 327712 | tf_op jit(solution)/shard_map/all_to_all | solution.py:699
  64.8 0.0 copy-start
  64.8 0.7 copy-done
  65.5 48.5 %forward_legendre.1 = f32[160,30,10,2,128]{4,3,2,1,0:T(2,128)} custom-call(s32[1280]{0:T(1024)} %wave.4, f32[30]{0:T(128)} %speed.1, bf16[8,4,40,128]{3,2,1,0:T(8,128)(2,1)} %bitcast.20, bf16[8,160,128]{2,1,0:T(8,128)(2,1)} %copy-done.2, bf16[8,160,128]{2,1,0:T(8,128)(2,1)} %copy-done.3, ...), custom_call_target="tpu_custom_call", output_to_operand_aliasing={{}: (7, {})} | custom-call | tf_op jit(solution)/shard_map/forward_legendre/pallas_call | solution.py:717
  (2 shorter events, 0.0 us)
Async XLA Ops:
  0.0 25.5 %copy-start.4 = (s32[1280]{0:T(1024)S(1)}, s32[1280]{0:T(1024)}, u32[]{:S(2)}) copy-start(s32[1280]{0:T(1024)} %wave.4) | copy-start | bytes 15364
  18.2 19.3 %all-to-all-start = ((bf16[32,40,128]{2,1,0:T(8,128)(2,1)}), bf16[32,40,128]{2,1,0:T(8,128)(2,1)S(1)}, u32[]{:S(2)}, u32[]{:S(2)}) async-start(bf16[32,40,128]{2,1,0:T(8,128)(2,1)} %bitcast.23), calls=%async_computation | async-start | bytes 655360 | tf_op jit(solution)/shard_map/all_to_all | solution.py:650
  37.5 2.3 %copy-start.1 = (bf16[32,40,128]{2,1,0:T(8,128)(2,1)}, bf16[32,40,128]{2,1,0:T(8,128)(2,1)S(1)}, u32[]{:S(2)}) copy-start(bf16[32,40,128]{2,1,0:T(8,128)(2,1)S(1)} %all-to-all-done) | copy-start | bytes 983044
  37.5 11.3 %collective-permute-start = (bf16[8,160,128]{2,1,0:T(8,128)(2,1)}, bf16[8,160,128]{2,1,0:T(8,128)(2,1)S(1)}, u32[]{:S(2)}, u32[]{:S(2)}) collective-permute-start(bf16[8,160,128]{2,1,0:T(8,128)(2,1)} %get-tuple-element.27), channel_id=1, source_target_pairs={{1,3},{5,7},{9,11},{13,15},{17,19},{21,23},{25,27},{29,31}} | collective-permute-start | bytes 983048 | tf_op jit(solution)/shard_map/ppermute | solution.py:678
  38.2 10.6 %collective-permute-start.1 = (bf16[8,160,128]{2,1,0:T(8,128)(2,1)}, bf16[8,160,128]{2,1,0:T(8,128)(2,1)S(1)}, u32[]{:S(2)}, u32[]{:S(2)}) collective-permute-start(bf16[8,160,128]{2,1,0:T(8,128)(2,1)} %get-tuple-element.28), channel_id=1, source_target_pairs={{2,3},{6,7},{10,11},{14,15},{18,19},{22,23},{26,27},{30,31}} | collective-permute-start | bytes 983048 | tf_op jit(solution)/shard_map/ppermute | solution.py:678
  48.8 13.1 %copy-start.2 = (bf16[8,160,128]{2,1,0:T(8,128)(2,1)}, bf16[8,160,128]{2,1,0:T(8,128)(2,1)S(1)}, u32[]{:S(2)}) copy-start(bf16[8,160,128]{2,1,0:T(8,128)(2,1)S(1)} %collective-permute-done.refs_0_) | copy-start | bytes 983044
  48.8 13.1 %copy-start.3 = (bf16[8,160,128]{2,1,0:T(8,128)(2,1)}, bf16[8,160,128]{2,1,0:T(8,128)(2,1)S(1)}, u32[]{:S(2)}) copy-start(bf16[8,160,128]{2,1,0:T(8,128)(2,1)S(1)} %collective-permute-done.1.refs_1_) | copy-start | bytes 983044
  48.8 16.0 %all-to-all-start.1 = ((bf16[32,40,128]{2,1,0:T(8,128)(2,1)}), bf16[32,40,128]{2,1,0:T(8,128)(2,1)S(1)}, u32[]{:S(2)}, u32[]{:S(2)}) async-start(bf16[32,40,128]{2,1,0:T(8,128)(2,1)} %bitcast.22), calls=%async_computation.1 | async-start | bytes 655360 | tf_op jit(solution)/shard_map/all_to_all | solution.py:699
  64.8 0.7 copy-start

commit v7 on v6

--- a/solution.py
+++ b/solution.py
@@ -39,6 +39,8 @@
         self.slots, self.fields, self.degrees, self.rows = slots, fields, degrees, rows
         self.tiles = degrees // SLAB
         self.packed = self.tiles + 1
+        self.pitch = up_to(2 * self.packed, 8)
+        self.pitch_bf16 = up_to(2 * self.packed, 16)
         self.slot_rows = fields * self.tiles * 2
         self.field_pad = up_to(fields, 8)
         self.share = -(-fields // groups)
@@ -126,7 +128,7 @@
     item = remainder(rest, sz.share)
     start = remainder(lev * sz.fields, sz.groups)
     field = remainder(group - start + sz.groups, sz.groups) + sz.groups * item
-    want = ((quarter * 2 + row) * sz.field_pad + field) * 2 + comp
+    want = ((quarter * 2 + row) * 2 + comp) * sz.field_pad + field
     want = jnp.where((field < sz.fields) & (quarter < sz.quarters), want, -1)
     return one_hot(iota((tall, wide), 0) == want)
 
@@ -188,6 +190,11 @@
 BEHIND = 4
 
 
+def await_tiles(hbm, sem):
+    for some in (hbm.at[0], hbm.at[0, :, pl.ds(0, 1)]):
+        pltpu.make_async_copy(some, some, sem).wait()
+
+
 class Stream:
     def __init__(self, sizes, pair_at, x_hbm, leg_hbm, x_all, leg_all, x_sems, leg_sems):
         self.sizes, self.pair_at = sizes, pair_at
@@ -196,15 +203,17 @@
 
     def start(self, place):
         pair = self.pair_at(place)
-        tiles = self.sizes.tiles
+        sz = self.sizes
+        tiles = sz.tiles
+        x_rows = self.x_hbm.reshape(sz.slots, sz.fields, 2 * tiles, SLAB)
 
         def emit(start):
             split = tiles - start
             for side, first, here in ((0, start, (0, split)), (1, split - 1, (split, tiles + 1))):
                 slot = 2 * place + side
                 pltpu.make_async_copy(
-                    self.x_hbm.at[slot, :, pl.ds(first, tiles - first)],
-                    self.x_all.at[place, :, pl.ds(here[0], here[1] - here[0])],
+                    x_rows.at[slot, :, pl.ds(2 * first, 2 * (tiles - first))],
+                    self.x_all.at[place, :, pl.ds(2 * here[0], 2 * (here[1] - here[0]))],
                     self.x_sems.at[place],
                 ).start()
                 pltpu.make_async_copy(
@@ -232,14 +241,15 @@
 
         for k in range(each):
             place = step * each + k
-            for here, sems in ((self.x_all, self.x_sems), (self.leg_all, self.leg_sems)):
-                pltpu.make_async_copy(here.at[place], here.at[place], sems.at[place]).wait()
+            await_tiles(self.x_hbm, self.x_sems.at[place])
+            here = self.leg_all.at[place]
+            pltpu.make_async_copy(here, here, self.leg_sems.at[place]).wait()
 
 
 def inverse_kernel(sizes, rounds, wave, points, gauss, layer_depth, x_hbm, leg_hbm, send_ref, *refs):
     sz = sizes
     geo_refs = refs[:len(rounds)]
-    spots, numbers, x_all, leg_all, *sems = refs[len(rounds):]
+    wide, spots, numbers, x_all, leg_all, *sems = refs[len(rounds):]
     band = lax.axis_index("band")
     lev = lax.axis_index("lev")
     pair_at = functools.partial(Pair, sz, wave, band)
@@ -248,21 +258,30 @@
     pad = 2 * sz.field_pad
     spots[...] = jnp.zeros_like(spots)
     numbers[...] = jnp.full_like(numbers, -1)
+    wide[...] = jnp.zeros_like(wide)
 
     def block(step, carry):
         stream.take(step)
         found = []
         for k in range(sz.block // 2):
             place = step * (sz.block // 2) + k
+            for f in range(sz.fields):
+                rows = x_all[place, f].astype(jnp.float32)
+                wide[k, pl.ds(f * sz.pitch, sz.pitch), :] = rows[0:sz.pitch]
+        for k in range(sz.block // 2):
+            place = step * (sz.block // 2) + k
             pair = pair_at(place)
             values = jnp.concatenate([
-                x_all[place, :, t].reshape(2 * sz.fields, SLAB) for t in range(sz.packed)
+                jnp.concatenate([
+                    wide[k, pl.ds(2 * t + c, sz.field_pad, stride=sz.pitch), :] for c in range(2)
+                ], axis=0).astype(jnp.bfloat16)
+                for t in range(sz.packed)
             ], axis=1)
             total = dot(pair.tables(leg_all[place]), values, ((1,), (1,)))
             for side in range(2):
                 found.append((pair, side, total[side * sz.rows:(side + 1) * sz.rows]))
         for pair, side, total in found:
-            spots[pair.rows(side), 0:2 * sz.fields] = total
+            spots[pair.rows(side), 0:pad] = total
             number = jnp.full((1, SLAB), pair.numbers[side], jnp.int32)
             numbers[pl.ds(pair.spot(side), 1), :] = number
         return carry
@@ -271,8 +290,9 @@
     spread = spread_matrix(sz, lev)
     shape = (2 * pad, SLAB)
     src, dst = iota(shape, 0), iota(shape, 1)
-    from_row, from_field, from_comp = src // pad, (src & (pad - 1)) >> 1, src & 1
-    to_row, to_field, to_comp = dst // pad, (dst & (pad - 1)) >> 1, dst & 1
+    bits = sz.field_pad.bit_length() - 1
+    from_field, from_side = src & (sz.field_pad - 1), src >> bits
+    to_field, to_side = dst & (sz.field_pad - 1), dst >> bits
     weights = []
     for pairs in rounds:
         first = jnp.int32(2 * LEVELS + sz.fields)
@@ -281,7 +301,7 @@
         under = lev * sz.fields + from_field - TEMPER * LEVELS
         above = first + to_field
         hit = (
-            (from_row == to_row) & (from_comp == to_comp)
+            (from_side == to_side)
             & (from_field < sz.fields) & (to_field < sz.fields)
             & (above >= 0) & (above <= under)
         )
@@ -293,7 +313,7 @@
         weights.append(jnp.concatenate([high, low], axis=0))
     number = numbers[...]
     lane = iota((sz.spots, SLAB), 1)
-    known = (number >= 0) & ~((number == 0) & (lane & 1 == 1))
+    known = (number >= 0) & ~((number == 0) & (lane & sz.field_pad != 0))
     for rp in range(sz.rows // 2):
         exact = jnp.concatenate([
             spots[pl.ds(2 * rp + r, sz.spots, stride=sz.rows), :][:, 0:pad] for r in range(2)
@@ -514,8 +534,8 @@
 
 def forward_kernel(sizes, wave, speed, back_ref, *refs):
     sz = sizes
-    geo_refs = refs[:-12]
-    x_hbm, leg_hbm, _, out_hbm, spots, inverse, out_all, out_sems, x_all, leg_all, *sems = refs[-12:]
+    geo_refs = refs[:-13]
+    x_hbm, leg_hbm, _, out_hbm, wide, spots, inverse, out_all, out_sems, x_all, leg_all, *sems = refs[-13:]
     band = lax.axis_index("band")
     pair_at = functools.partial(Pair, sz, wave, band)
     stream = Stream(sz, pair_at, x_hbm, leg_hbm, x_all, leg_all, *sems)
@@ -536,14 +556,15 @@
             part = rows[:, r * pad:(r + 1) * pad]
             part = jnp.concatenate([part, jnp.zeros((sz.spots, SLAB - pad), jnp.float32)], axis=1)
             spots[pl.ds(2 * rp + r, sz.spots, stride=sz.rows), :] = part
-    row = iota((pad, SLAB), 0)
-    speeds = jnp.ones((pad, SLAB), jnp.float32)
-    for f in range(sz.fields):
-        speeds = jnp.where(row >> 1 == f, speed[f], speeds)
-    for t in range(sz.tiles):
-        degree = iota((1, SLAB), 1) + t * SLAB
+    row = quotient(iota((sz.pitch, SLAB), 0), 2)
+    lane = iota((sz.pitch, SLAB), 1)
+    for start in range(sz.tiles):
+        degree = jnp.where(row < sz.tiles - start, row + start, row - 1) * SLAB + lane
         helm = (degree * (degree + 1)).astype(jnp.float32) / float(sz.trunc * (sz.trunc + 1))
-        inverse[t] = 1.0 / (1.0 + time_step * time_step * helm * speeds)
+        for f in range(sz.fields):
+            denominator = 1.0 + time_step * time_step * helm * speed[f]
+            inverse[start, pl.ds(f * sz.pitch, sz.pitch), :] = 1.0 / denominator
+    out_tiles = out_all.reshape(BEHIND, each, sz.fields, sz.pitch // 2, 2, SLAB)
 
     def leave(place, k):
         at = lax.rem(place // each, BEHIND)
@@ -552,7 +573,7 @@
             split = sz.tiles - start
             for side, first, here in ((0, start, (0, split)), (1, split - 1, (split, sz.packed))):
                 pltpu.make_async_copy(
-                    out_all.at[at, k, :, pl.ds(here[0], here[1] - here[0])],
+                    out_tiles.at[at, k, :, pl.ds(here[0], here[1] - here[0])],
                     out_hbm.at[2 * place + side, :, pl.ds(first, sz.tiles - first)],
                     out_sems.at[at, k],
                 ).start()
@@ -562,7 +583,7 @@
     def left(step):
         at = lax.rem(step, BEHIND)
         for k in range(each):
-            pltpu.make_async_copy(out_all.at[at, k], out_all.at[at, k], out_sems.at[at, k]).wait()
+            await_tiles(out_hbm, out_sems.at[at, k])
 
     def block(step, carry):
         stream.take(step)
@@ -574,23 +595,34 @@
             values = values.T.astype(jnp.bfloat16)[0:pad]
             work.append((place, pair, values, pair.tables(leg_all[place])))
 
-        @pl.when(step >= BEHIND)
-        def _():
-            left(step)
-
-        at = lax.rem(step, BEHIND)
         for k in range(each):
-            place, pair, values, tables = work[k]
-            _, live = pair.columns()
+            _, _, values, tables = work[k]
             for first in range(0, sz.packed, 2):
                 count = min(2, sz.packed - first)
                 tends = dot(values, tables[:, first * SLAB:(first + count) * SLAB])
                 for t in range(first, first + count):
-                    old = x_all[place, :, t].reshape(2 * sz.fields, SLAB).astype(jnp.float32)
-                    tend = tends[0:2 * sz.fields, (t - first) * SLAB:(t - first + 1) * SLAB]
-                    new = (old + time_step * tend) * inverse[pair.tile(t), 0:2 * sz.fields]
-                    new = jnp.where(live[:, t * SLAB:(t + 1) * SLAB], new, 0.0)
-                    out_all[at, k, :, t] = new.reshape(sz.fields, 2, SLAB)
+                    for c in range(2):
+                        rows = pl.ds(2 * t + c, sz.field_pad, stride=sz.pitch)
+                        wide[k, rows, :] = tends[
+                            c * sz.field_pad:(c + 1) * sz.field_pad, (t - first) * SLAB:(t - first + 1) * SLAB
+                        ]
+
+        @pl.when(step >= BEHIND)
+        def _():
+            left(step)
+
+        at = lax.rem(step, BEHIND)
+        for k in range(each):
+            place, pair, _, _ = work[k]
+            mine = row < pair.split
+            degree = jnp.where(mine, row + pair.start, row - 1) * SLAB + lane
+            floors = [jnp.where(n < 0, sz.degrees, n) for n in pair.numbers]
+            live = degree >= jnp.where(mine, floors[0], floors[1])
+            for f in range(sz.fields):
+                rows = pl.ds(f * sz.pitch, sz.pitch)
+                old = x_all[place, f].astype(jnp.float32)[0:sz.pitch]
+                new = (old + time_step * wide[k, rows, :]) * inverse[pair.start, rows, :]
+                out_all[at, k, rows, :] = jnp.where(live, new, 0.0)
         for k in range(each):
             leave(step * each + k, k)
         return carry
@@ -622,11 +654,12 @@
     spots_shape = pltpu.VMEM((sz.spots * sz.rows, SLAB), jnp.float32)
     pairs = slots // 2
     stream_scratch = [
-        pltpu.VMEM((pairs, fields, sz.packed, 2, SLAB), jnp.bfloat16),
+        pltpu.VMEM((pairs, fields, sz.pitch_bf16, SLAB), jnp.bfloat16),
         pltpu.VMEM((pairs, rows, sz.packed * SLAB), jnp.bfloat16),
         pltpu.SemaphoreType.DMA((pairs,)),
         pltpu.SemaphoreType.DMA((pairs,)),
     ]
+    wide_shape = pltpu.VMEM((sz.block // 2, sz.field_pad * sz.pitch, SLAB), jnp.float32)
     anywhere = pl.BlockSpec(memory_space=pl.ANY)
     vmem = pl.BlockSpec(memory_space=pltpu.VMEM)
     send_shape = (sz.bands, sz.groups, sz.chunk, SLAB)
@@ -638,7 +671,7 @@
         out_specs=[vmem] * (1 + len(rounds)),
         out_shape=[jax.ShapeDtypeStruct(send_shape, jnp.bfloat16)]
         + [jax.ShapeDtypeStruct(geo_shape, jnp.bfloat16)] * len(rounds),
-        scratch_shapes=[spots_shape, pltpu.VMEM((sz.spots, SLAB), jnp.int32), *stream_scratch],
+        scratch_shapes=[wide_shape, spots_shape, pltpu.VMEM((sz.spots, SLAB), jnp.int32), *stream_scratch],
         compiler_params=params(56),
         name="inverse_legendre",
     )(slot_wave, row_points, gauss_weight, layer_depth, tiled, tables)
@@ -721,9 +754,9 @@
         out_shape=out_shape,
         input_output_aliases={5 + len(rounds): 0},
         scratch_shapes=[
-            spots_shape,
-            pltpu.VMEM((sz.tiles, 2 * sz.field_pad, SLAB), jnp.float32),
-            pltpu.VMEM((BEHIND, sz.block // 2, fields, sz.packed, 2, SLAB), jnp.float32),
+            wide_shape, spots_shape,
+            pltpu.VMEM((sz.tiles, fields * sz.pitch, SLAB), jnp.float32),
+            pltpu.VMEM((BEHIND, sz.block // 2, fields * sz.pitch, SLAB), jnp.float32),
             pltpu.SemaphoreType.DMA((BEHIND, sz.block // 2)),
             *stream_scratch,
         ],

time: 115 us -> 93.7 us (0.81)
  Pallas kernels: 90.2 us -> 69.4 us
    pallas_call x1, Pallas kernels: 48.5 us -> 27.4 us  [shards(): pl.pallas_call(functools.partial(forward_kernel, sz), in_specs=[smem(), s...]
  transfers between devices with their start and end apart: 4 -> 4, of which waited for: 2 -> 2; matrix products, arithmetic and copies ran while one was open for 2% -> 3% of each run, Pallas kernels for 21% -> 25%
where the time goes in v7:
time: 93.7 us; the launch traced here: 93.4 us
  Pallas kernels  69.4 us (74%)
  starting transfers between devices  12.8 us (14%)
  waiting for transfers between devices  7.6 us (8%)
  local copies, waits for them, and re-layouts  3.21 us (3%)
    pallas_call x1, Pallas kernels, shards(): pl.pallas_call(functools.partial(forward_kernel, sz), in_specs=[smem(), s...  27.4 us
    pallas_call x1, Pallas kernels, shards(): pl.pallas_call(functools.partial(inverse_kernel, sz, rounds), in_specs=[s...  18.5 us
    pallas_call x1, Pallas kernels, shards(): pl.pallas_call(functools.partial(grid_kernel, sz), in_specs=[smem(), smem...  8.99 us
    pallas_call x1, Pallas kernels, shards(): pl.pallas_call(functools.partial(zeros_kernel, sz), in_specs=[smem()], ou...  8.91 us
    all_to_all x1, starting transfers between devices, shards(): lax.all_to_all(sent.reshape(flat), both, split_axis=0, concat_axis=0, til...  7.32 us
    pallas_call x1, Pallas kernels, shards(): pl.pallas_call(functools.partial(basis_kernel, sz), grid=(sz.sorted // hi...  5.64 us
    all_to_all x1, waiting for transfers between devices, shards(): lax.all_to_all(sent.reshape(flat), both, split_axis=0, concat_axis=0, til...  4.72 us
    all_to_all x1, starting transfers between devices, shards(): lax.all_to_all(returned.reshape(flat), both, split_axis=0, concat_axis=0,...  4.17 us
  transfers between devices with their start and end apart: 4, of which 2 were waited for; matrix products, arithmetic and copies ran while one was open for 3% of the time, Pallas kernels for 25%

profile of v7, /device:TPU:0, one launch (start us, length us, event | category | flops | bytes accessed | tf_op | source)
XLA Modules:
  0.0 93.4 jit_solution(3283814024566735289)
XLA Ops:
  0.0 0.0 copy-start.4
  0.0 18.5 %inverse_legendre.1 = (bf16[8,4,40,128]{3,2,1,0:T(8,128)(2,1)}, bf16[8,160,128]{2,1,0:T(8,128)(2,1)}, bf16[8,160,128]{2,1,0:T(8,128)(2,1)}) custom-call(s32[1280]{0:T(1024)} %wave.4, s32[16]{0:T(128)} %points.4, f32[16]{0:T(128)} %gauss.3, f32[24]{0:T(128)} %layer_depth.1, bf16[160,30,10,2,128]{4,3,2,1,0:T(2,128)(2,1)} %bitcast.16, ...), custom_call_target="tpu_custom_call" | custom-call | tf_op jit(solution)/shard_map/inverse_legendre/pallas_call | solution.py:668
  18.5 7.3 %all-to-all-start = ((bf16[32,40,128]{2,1,0:T(8,128)(2,1)}), bf16[32,40,128]{2,1,0:T(8,128)(2,1)S(1)}, u32[]{:S(2)}, u32[]{:S(2)}) async-start(bf16[32,40,128]{2,1,0:T(8,128)(2,1)} %bitcast.23), calls=%async_computation | async-start | bytes 655360 | tf_op jit(solution)/shard_map/all_to_all | solution.py:683
  25.8 0.0 copy-done.4
  25.8 0.3 reshape.28
  26.1 0.3 slice_reduce_fusion
  26.5 0.1 squeeze.8
  26.5 0.1 squeeze.7
  26.7 0.1 reshape_reshape.7
  26.8 0.7 reshape_reshape.6.even_row
  27.4 5.6 %basis.1.basis_hbm = bf16[4,640,1408]{2,1,0:T(8,128)(2,1)} custom-call(s32[16]{0:T(128)} %points.4), custom_call_target="tpu_custom_call" | custom-call | flops 18022400 | bytes 7208960 | tf_op jit(solution)/shard_map/basis/pallas_call | solution.py:693
  33.1 4.7 %all-to-all-done = bf16[32,40,128]{2,1,0:T(8,128)(2,1)S(1)} async-done(((bf16[32,40,128]{2,1,0:T(8,128)(2,1)}), bf16[32,40,128]{2,1,0:T(8,128)(2,1)S(1)}, u32[]{:S(2)}, u32[]{:S(2)}) %all-to-all-start) | async-done | bytes 327712 | tf_op jit(solution)/shard_map/all_to_all | solution.py:683
  37.8 0.0 copy-start.1
  37.8 0.7 collective-permute-start
  38.5 0.7 collective-permute-start.1
  39.2 0.9 copy.11.even_col
  40.1 0.0 copy-done.1
  40.1 9.0 %grid_products.1 = bf16[8,4,40,128]{3,2,1,0:T(8,128)(2,1)} custom-call(s32[16]{0:T(128)} %points.4, f32[16]{0:T(128)} %gauss.3, bf16[8,4,40,128]{3,2,1,0:T(8,128)(2,1)} %bitcast.21, s32[1,640]{1,0:T(1,128)} %reshape_reshape.6.even_row, s32[640,1]{1,0:T(8,128)} %copy.11.even_col, bf16[4,640,1408]{2,1,0:T(8,128)(2,1)} %basis.1.basis_hbm), custom_call_target="tpu_custom_call" | custom-call | flops 1845493760 | bytes 7208960 | tf_op jit(solution)/shard_map/grid_products/pallas_call | solution.py:712
  49.1 0.0 collective-permute-done.refs_0_
  49.1 0.0 copy-start.2
  49.1 0.0 collective-permute-done.1.refs_1_
  49.1 0.0 copy-start.3
  49.1 4.2 %all-to-all-start.1 = ((bf16[32,40,128]{2,1,0:T(8,128)(2,1)}), bf16[32,40,128]{2,1,0:T(8,128)(2,1)S(1)}, u32[]{:S(2)}, u32[]{:S(2)}) async-start(bf16[32,40,128]{2,1,0:T(8,128)(2,1)} %bitcast.22), calls=%async_computation.1 | async-start | bytes 655360 | tf_op jit(solution)/shard_map/all_to_all | solution.py:732
  53.3 8.9 %dead_zeros.1.refs_4_ = f32[160,30,10,2,128]{4,3,2,1,0:T(2,128)} custom-call(s32[1280]{0:T(1024)} %wave.4), custom_call_target="tpu_custom_call" | custom-call | bytes 24576000 | tf_op jit(solution)/shard_map/dead_zeros/pallas_call | solution.py:735
  62.2 0.0 copy-done.2
  62.2 0.0 copy-done.3
  62.2 2.9 %all-to-all-done.1 = bf16[32,40,128]{2,1,0:T(8,128)(2,1)S(1)} async-done(((bf16[32,40,128]{2,1,0:T(8,128)(2,1)}), bf16[32,40,128]{2,1,0:T(8,128)(2,1)S(1)}, u32[]{:S(2)}, u32[]{:S(2)}) %all-to-all-start.1) | async-done | bytes 327712 | tf_op jit(solution)/shard_map/all_to_all | solution.py:732
  65.1 0.0 copy-start
  65.1 0.7 copy-done
  65.8 27.4 %forward_legendre.1 = f32[160,30,10,2,128]{4,3,2,1,0:T(2,128)} custom-call(s32[1280]{0:T(1024)} %wave.4, f32[30]{0:T(128)} %speed.1, bf16[8,4,40,128]{3,2,1,0:T(8,128)(2,1)} %bitcast.20, bf16[8,160,128]{2,1,0:T(8,128)(2,1)} %copy-done.2, bf16[8,160,128]{2,1,0:T(8,128)(2,1)} %copy-done.3, ...), custom_call_target="tpu_custom_call", output_to_operand_aliasing={{}: (7, {})} | custom-call | tf_op jit(solution)/shard_map/forward_legendre/pallas_call | solution.py:750
  (2 shorter events, 0.0 us)
Async XLA Ops:
  0.0 25.8 %copy-start.4 = (s32[1280]{0:T(1024)S(1)}, s32[1280]{0:T(1024)}, u32[]{:S(2)}) copy-start(s32[1280]{0:T(1024)} %wave.4) | copy-start | bytes 15364
  18.5 19.3 %all-to-all-start = ((bf16[32,40,128]{2,1,0:T(8,128)(2,1)}), bf16[32,40,128]{2,1,0:T(8,128)(2,1)S(1)}, u32[]{:S(2)}, u32[]{:S(2)}) async-start(bf16[32,40,128]{2,1,0:T(8,128)(2,1)} %bitcast.23), calls=%async_computation | async-start | bytes 655360 | tf_op jit(solution)/shard_map/all_to_all | solution.py:683
  37.8 2.3 %copy-start.1 = (bf16[32,40,128]{2,1,0:T(8,128)(2,1)}, bf16[32,40,128]{2,1,0:T(8,128)(2,1)S(1)}, u32[]{:S(2)}) copy-start(bf16[32,40,128]{2,1,0:T(8,128)(2,1)S(1)} %all-to-all-done) | copy-start | bytes 983044
  37.8 11.3 %collective-permute-start = (bf16[8,160,128]{2,1,0:T(8,128)(2,1)}, bf16[8,160,128]{2,1,0:T(8,128)(2,1)S(1)}, u32[]{:S(2)}, u32[]{:S(2)}) collective-permute-start(bf16[8,160,128]{2,1,0:T(8,128)(2,1)} %get-tuple-element.27), channel_id=1, source_target_pairs={{1,3},{5,7},{9,11},{13,15},{17,19},{21,23},{25,27},{29,31}} | collective-permute-start | bytes 983048 | tf_op jit(solution)/shard_map/ppermute | solution.py:711
  38.5 10.6 %collective-permute-start.1 = (bf16[8,160,128]{2,1,0:T(8,128)(2,1)}, bf16[8,160,128]{2,1,0:T(8,128)(2,1)S(1)}, u32[]{:S(2)}, u32[]{:S(2)}) collective-permute-start(bf16[8,160,128]{2,1,0:T(8,128)(2,1)} %get-tuple-element.28), channel_id=1, source_target_pairs={{2,3},{6,7},{10,11},{14,15},{18,19},{22,23},{26,27},{30,31}} | collective-permute-start | bytes 983048 | tf_op jit(solution)/shard_map/ppermute | solution.py:711
  49.1 13.1 %copy-start.2 = (bf16[8,160,128]{2,1,0:T(8,128)(2,1)}, bf16[8,160,128]{2,1,0:T(8,128)(2,1)S(1)}, u32[]{:S(2)}) copy-start(bf16[8,160,128]{2,1,0:T(8,128)(2,1)S(1)} %collective-permute-done.refs_0_) | copy-start | bytes 983044
  49.1 13.1 %copy-start.3 = (bf16[8,160,128]{2,1,0:T(8,128)(2,1)}, bf16[8,160,128]{2,1,0:T(8,128)(2,1)S(1)}, u32[]{:S(2)}) copy-start(bf16[8,160,128]{2,1,0:T(8,128)(2,1)S(1)} %collective-permute-done.1.refs_1_) | copy-start | bytes 983044
  49.1 16.0 %all-to-all-start.1 = ((bf16[32,40,128]{2,1,0:T(8,128)(2,1)}), bf16[32,40,128]{2,1,0:T(8,128)(2,1)S(1)}, u32[]{:S(2)}, u32[]{:S(2)}) async-start(bf16[32,40,128]{2,1,0:T(8,128)(2,1)} %bitcast.22), calls=%async_computation.1 | async-start | bytes 655360 | tf_op jit(solution)/shard_map/all_to_all | solution.py:732
  65.1 0.7 copy-start

commit v8 on v7

--- a/solution.py
+++ b/solution.py
@@ -167,16 +167,13 @@
         floors = [jnp.where(n < 0, self.sizes.degrees, n) for n in self.numbers]
         return first, degree >= jnp.where(first, floors[0], floors[1])
 
-    def by_start(self, emit):
-        def branch(low, high):
-            if high - low == 1:
-                emit(low)
-                return
-            middle = (low + high) // 2
-            pl.when(self.start < middle)(lambda: branch(low, middle))
-            pl.when(self.start >= middle)(lambda: branch(middle, high))
-
-        branch(0, self.sizes.tiles)
+    def parts(self):
+        tiles = self.sizes.tiles
+        first = 2 * self.place
+        return (
+            (first, self.start, self.split, 0),
+            (first + 1, self.split - 1, tiles + 1 - self.split, self.split),
+        )
 
     def tables(self, leg):
         first, live = self.columns()
@@ -190,6 +187,10 @@
 BEHIND = 4
 
 
+def span(first, count, unit):
+    return pl.ds(pl.multiple_of(first * unit, unit), pl.multiple_of(count * unit, unit))
+
+
 def await_tiles(hbm, sem):
     for some in (hbm.at[0], hbm.at[0, :, pl.ds(0, 1)]):
         pltpu.make_async_copy(some, some, sem).wait()
@@ -202,27 +203,19 @@
         self.x_sems, self.leg_sems = x_sems, leg_sems
 
     def start(self, place):
-        pair = self.pair_at(place)
         sz = self.sizes
-        tiles = sz.tiles
-        x_rows = self.x_hbm.reshape(sz.slots, sz.fields, 2 * tiles, SLAB)
-
-        def emit(start):
-            split = tiles - start
-            for side, first, here in ((0, start, (0, split)), (1, split - 1, (split, tiles + 1))):
-                slot = 2 * place + side
-                pltpu.make_async_copy(
-                    x_rows.at[slot, :, pl.ds(2 * first, 2 * (tiles - first))],
-                    self.x_all.at[place, :, pl.ds(2 * here[0], 2 * (here[1] - here[0]))],
-                    self.x_sems.at[place],
-                ).start()
-                pltpu.make_async_copy(
-                    self.leg_hbm.at[slot, :, pl.ds(first * SLAB, (tiles - first) * SLAB)],
-                    self.leg_all.at[place, :, pl.ds(here[0] * SLAB, (here[1] - here[0]) * SLAB)],
-                    self.leg_sems.at[place],
-                ).start()
-
-        pair.by_start(emit)
+        x_rows = self.x_hbm.reshape(sz.slots, sz.fields, 2 * sz.tiles, SLAB)
+        for slot, first, count, here in self.pair_at(place).parts():
+            pltpu.make_async_copy(
+                x_rows.at[slot, :, span(first, count, 2)],
+                self.x_all.at[place, :, span(here, count, 2)],
+                self.x_sems.at[place],
+            ).start()
+            pltpu.make_async_copy(
+                self.leg_hbm.at[slot, :, span(first, count, SLAB)],
+                self.leg_all.at[place, :, span(here, count, SLAB)],
+                self.leg_sems.at[place],
+            ).start()
 
     def begin(self):
         def one(place, carry):
@@ -411,7 +404,7 @@
 
 
 def grid_kernel(
-    sizes, points, gauss, recv_ref, even_row, even_col, basis_hbm, send_ref, basis, terms, arrivals,
+    sizes, points, gauss, recv_ref, even_row, basis_hbm, send_ref, basis, terms, arrivals,
 ):
     sz = sizes
     step = 2 * SLAB
@@ -487,7 +480,8 @@
     scale = jnp.where(lane < half_slab, gauss[first_row], gauss[first_row + 1])
     bound = jnp.where(lane < half_slab, length_a, length_b) - 1
     number = iota((sz.sorted, SLAB), 0) * 2
-    back_order = one_hot(iota((sz.pairs, sz.sorted), 1) * 2 == even_col[...])
+    even_col = jnp.broadcast_to(even_row[...].astype(jnp.float32), (8, sz.pairs)).T[:, 0:1]
+    back_order = one_hot(iota((sz.pairs, sz.sorted), 1) * 2 == even_col.astype(jnp.int32))
     pieces = []
     for parity in range(2):
         mine = number if parity == 0 else sz.trunc - number
@@ -512,16 +506,17 @@
     zeros[...] = jnp.zeros_like(zeros)
 
     def one(place, carry):
-        def emit(start):
-            for side, count in ((0, start), (1, sz.tiles - 1 - start)):
-                if count:
-                    pltpu.make_async_copy(
-                        zeros.at[:, pl.ds(0, count)],
-                        out_hbm.at[2 * place + side, :, pl.ds(0, count)],
-                        sems.at[place],
-                    ).start()
-
-        Pair(sz, wave, band, place).by_start(emit)
+        pair = Pair(sz, wave, band, place)
+        for side, count in ((0, pair.start), (1, pair.split - 1)):
+
+            @pl.when(count > 0)
+            def _():
+                pltpu.make_async_copy(
+                    zeros.at[:, pl.ds(0, count)],
+                    out_hbm.at[2 * place + side, :, pl.ds(0, count)],
+                    sems.at[place],
+                ).start()
+
         return carry
 
     def done(place, carry):
@@ -569,16 +564,12 @@
     def leave(place, k):
         at = lax.rem(place // each, BEHIND)
 
-        def emit(start):
-            split = sz.tiles - start
-            for side, first, here in ((0, start, (0, split)), (1, split - 1, (split, sz.packed))):
-                pltpu.make_async_copy(
-                    out_tiles.at[at, k, :, pl.ds(here[0], here[1] - here[0])],
-                    out_hbm.at[2 * place + side, :, pl.ds(first, sz.tiles - first)],
-                    out_sems.at[at, k],
-                ).start()
-
-        pair_at(place).by_start(emit)
+        for slot, first, count, here in pair_at(place).parts():
+            pltpu.make_async_copy(
+                out_tiles.at[at, k, :, pl.ds(here, count)],
+                out_hbm.at[slot, :, pl.ds(first, count)],
+                out_sems.at[at, k],
+            ).start()
 
     def left(step):
         at = lax.rem(step, BEHIND)
@@ -704,14 +695,12 @@
         name="basis",
     )(points_later)
 
-    even_row, even_col = even_wave.reshape(1, sz.pairs), even_wave.reshape(sz.pairs, 1)
-    *geo, arrived, basis, even_row, even_col = lax.optimization_barrier(
-        (*geo, arrived, basis, even_row, even_col)
-    )
+    even_row = even_wave.reshape(1, sz.pairs)
+    *geo, arrived, basis, even_row = lax.optimization_barrier((*geo, arrived, basis, even_row))
     moved = [lax.ppermute(geo[turn], "lev", pairs) for turn, pairs in enumerate(rounds)]
     returned = pl.pallas_call(
         functools.partial(grid_kernel, sz),
-        in_specs=[smem(), smem(), vmem, vmem, vmem, anywhere],
+        in_specs=[smem(), smem(), vmem, vmem, anywhere],
         out_specs=vmem,
         out_shape=jax.ShapeDtypeStruct(send_shape, jnp.bfloat16),
         scratch_shapes=[
@@ -725,7 +714,7 @@
         ),
         name="grid_products",
     )(
-        row_points, gauss_weight, arrived.reshape(send_shape), even_row, even_col, basis,
+        row_points, gauss_weight, arrived.reshape(send_shape), even_row, basis,
     )
     *moved, returned, wave_last = lax.optimization_barrier((*moved, returned, slot_wave))
 

time: 93.7 us -> 87.7 us (0.936)
  Pallas kernels: 69.4 us -> 64.2 us
  local copies, waits for them, and re-layouts: 3.21 us -> 2.19 us
    pallas_call x1, Pallas kernels: 27.4 us -> 23.8 us  [shards(): pl.pallas_call(functools.partial(forward_kernel, sz), in_specs=[smem(), s...]
    pallas_call x1, Pallas kernels: 18.5 us -> 16.9 us  [shards(): pl.pallas_call(functools.partial(inverse_kernel, sz, rounds), in_specs=[s...]
  transfers between devices with their start and end apart: 4 -> 4, of which waited for: 2 -> 2; matrix products, arithmetic and copies ran while one was open for 3% -> 2% of each run, Pallas kernels for 25% -> 27%
where the time goes in v8:
time: 87.7 us; the launch traced here: 87.3 us
  Pallas kernels  64.2 us (73%)
  starting transfers between devices  12.8 us (15%)
  waiting for transfers between devices  7.72 us (9%)
  local copies, waits for them, and re-layouts  2.19 us (2%)
    pallas_call x1, Pallas kernels, shards(): pl.pallas_call(functools.partial(forward_kernel, sz), in_specs=[smem(), s...  23.8 us
    pallas_call x1, Pallas kernels, shards(): pl.pallas_call(functools.partial(inverse_kernel, sz, rounds), in_specs=[s...  16.9 us
    pallas_call x1, Pallas kernels, shards(): pl.pallas_call(functools.partial(grid_kernel, sz), in_specs=[smem(), smem...  8.99 us
    pallas_call x1, Pallas kernels, shards(): pl.pallas_call(functools.partial(zeros_kernel, sz), in_specs=[smem()], ou...  8.89 us
    all_to_all x1, starting transfers between devices, shards(): lax.all_to_all(sent.reshape(flat), both, split_axis=0, concat_axis=0, til...  7.27 us
    pallas_call x1, Pallas kernels, shards(): pl.pallas_call(functools.partial(basis_kernel, sz), grid=(sz.sorted // hi...  5.64 us
    all_to_all x1, waiting for transfers between devices, shards(): lax.all_to_all(sent.reshape(flat), both, split_axis=0, concat_axis=0, til...  4.82 us
    all_to_all x1, starting transfers between devices, shards(): lax.all_to_all(returned.reshape(flat), both, split_axis=0, concat_axis=0,...  4.16 us
  transfers between devices with their start and end apart: 4, of which 2 were waited for; matrix products, arithmetic and copies ran while one was open for 2% of the time, Pallas kernels for 27%

profile of v8, /device:TPU:0, one launch (start us, length us, event | category | flops | bytes accessed | tf_op | source)
XLA Modules:
  0.0 87.3 jit_solution(11915259244066573148)
XLA Ops:
  0.0 0.0 copy-start.4
  0.0 16.9 %inverse_legendre.1 = (bf16[8,4,40,128]{3,2,1,0:T(8,128)(2,1)}, bf16[8,160,128]{2,1,0:T(8,128)(2,1)}, bf16[8,160,128]{2,1,0:T(8,128)(2,1)}) custom-call(s32[1280]{0:T(1024)} %wave.4, s32[16]{0:T(128)} %points.4, f32[16]{0:T(128)} %gauss.3, f32[24]{0:T(128)} %layer_depth.1, bf16[160,30,10,2,128]{4,3,2,1,0:T(2,128)(2,1)} %bitcast.16, ...), custom_call_target="tpu_custom_call" | custom-call | tf_op jit(solution)/shard_map/inverse_legendre/pallas_call | solution.py:659
  16.9 7.3 %all-to-all-start = ((bf16[32,40,128]{2,1,0:T(8,128)(2,1)}), bf16[32,40,128]{2,1,0:T(8,128)(2,1)S(1)}, u32[]{:S(2)}, u32[]{:S(2)}) async-start(bf16[32,40,128]{2,1,0:T(8,128)(2,1)} %bitcast.23), calls=%async_computation | async-start | bytes 655360 | tf_op jit(solution)/shard_map/all_to_all | solution.py:674
  24.2 0.0 copy-done.4
  24.2 0.3 reshape.28
  24.5 0.3 slice_reduce_fusion
  24.8 0.1 squeeze.8
  24.9 0.1 squeeze.7
  25.1 0.7 reshape_reshape.3.even_row
  25.7 5.6 %basis.1.basis_hbm = bf16[4,640,1408]{2,1,0:T(8,128)(2,1)} custom-call(s32[16]{0:T(128)} %points.4), custom_call_target="tpu_custom_call" | custom-call | flops 18022400 | bytes 7208960 | tf_op jit(solution)/shard_map/basis/pallas_call | solution.py:684
  31.4 4.8 %all-to-all-done = bf16[32,40,128]{2,1,0:T(8,128)(2,1)S(1)} async-done(((bf16[32,40,128]{2,1,0:T(8,128)(2,1)}), bf16[32,40,128]{2,1,0:T(8,128)(2,1)S(1)}, u32[]{:S(2)}, u32[]{:S(2)}) %all-to-all-start) | async-done | bytes 327712 | tf_op jit(solution)/shard_map/all_to_all | solution.py:674
  36.2 0.0 copy-start.1
  36.2 0.7 collective-permute-start
  36.9 0.7 collective-permute-start.1
  37.6 0.0 copy-done.1
  37.6 9.0 %grid_products.1 = bf16[8,4,40,128]{3,2,1,0:T(8,128)(2,1)} custom-call(s32[16]{0:T(128)} %points.4, f32[16]{0:T(128)} %gauss.3, bf16[8,4,40,128]{3,2,1,0:T(8,128)(2,1)} %bitcast.21, s32[1,640]{1,0:T(1,128)} %reshape_reshape.3.even_row, bf16[4,640,1408]{2,1,0:T(8,128)(2,1)} %basis.1.basis_hbm), custom_call_target="tpu_custom_call" | custom-call | flops 1845493760 | bytes 7208960 | tf_op jit(solution)/shard_map/grid_products/pallas_call | solution.py:701
  46.6 0.0 collective-permute-done.refs_0_
  46.6 0.0 copy-start.2
  46.6 0.0 collective-permute-done.1.refs_1_
  46.6 0.0 copy-start.3
  46.6 4.2 %all-to-all-start.1 = ((bf16[32,40,128]{2,1,0:T(8,128)(2,1)}), bf16[32,40,128]{2,1,0:T(8,128)(2,1)S(1)}, u32[]{:S(2)}, u32[]{:S(2)}) async-start(bf16[32,40,128]{2,1,0:T(8,128)(2,1)} %bitcast.22), calls=%async_computation.1 | async-start | bytes 655360 | tf_op jit(solution)/shard_map/all_to_all | solution.py:721
  50.8 8.9 %dead_zeros.1.refs_4_ = f32[160,30,10,2,128]{4,3,2,1,0:T(2,128)} custom-call(s32[1280]{0:T(1024)} %wave.4), custom_call_target="tpu_custom_call" | custom-call | bytes 24576000 | tf_op jit(solution)/shard_map/dead_zeros/pallas_call | solution.py:724
  59.7 0.0 copy-done.2
  59.7 0.0 copy-done.3
  59.7 2.9 %all-to-all-done.1 = bf16[32,40,128]{2,1,0:T(8,128)(2,1)S(1)} async-done(((bf16[32,40,128]{2,1,0:T(8,128)(2,1)}), bf16[32,40,128]{2,1,0:T(8,128)(2,1)S(1)}, u32[]{:S(2)}, u32[]{:S(2)}) %all-to-all-start.1) | async-done | bytes 327712 | tf_op jit(solution)/shard_map/all_to_all | solution.py:721
  62.6 0.0 copy-start
  62.6 0.7 copy-done
  63.3 23.8 %forward_legendre.1 = f32[160,30,10,2,128]{4,3,2,1,0:T(2,128)} custom-call(s32[1280]{0:T(1024)} %wave.4, f32[30]{0:T(128)} %speed.1, bf16[8,4,40,128]{3,2,1,0:T(8,128)(2,1)} %bitcast.20, bf16[8,160,128]{2,1,0:T(8,128)(2,1)} %copy-done.2, bf16[8,160,128]{2,1,0:T(8,128)(2,1)} %copy-done.3, ...), custom_call_target="tpu_custom_call", output_to_operand_aliasing={{}: (7, {})} | custom-call | tf_op jit(solution)/shard_map/forward_legendre/pallas_call | solution.py:739
  (2 shorter events, 0.0 us)
Async XLA Ops:
  0.0 24.2 %copy-start.4 = (s32[1280]{0:T(1024)S(1)}, s32[1280]{0:T(1024)}, u32[]{:S(2)}) copy-start(s32[1280]{0:T(1024)} %wave.4) | copy-start | bytes 15364
  16.9 19.3 %all-to-all-start = ((bf16[32,40,128]{2,1,0:T(8,128)(2,1)}), bf16[32,40,128]{2,1,0:T(8,128)(2,1)S(1)}, u32[]{:S(2)}, u32[]{:S(2)}) async-start(bf16[32,40,128]{2,1,0:T(8,128)(2,1)} %bitcast.23), calls=%async_computation | async-start | bytes 655360 | tf_op jit(solution)/shard_map/all_to_all | solution.py:674
  36.2 1.4 %copy-start.1 = (bf16[32,40,128]{2,1,0:T(8,128)(2,1)}, bf16[32,40,128]{2,1,0:T(8,128)(2,1)S(1)}, u32[]{:S(2)}) copy-start(bf16[32,40,128]{2,1,0:T(8,128)(2,1)S(1)} %all-to-all-done) | copy-start | bytes 983044
  36.2 10.4 %collective-permute-start = (bf16[8,160,128]{2,1,0:T(8,128)(2,1)}, bf16[8,160,128]{2,1,0:T(8,128)(2,1)S(1)}, u32[]{:S(2)}, u32[]{:S(2)}) collective-permute-start(bf16[8,160,128]{2,1,0:T(8,128)(2,1)} %get-tuple-element.26), channel_id=1, source_target_pairs={{1,3},{5,7},{9,11},{13,15},{17,19},{21,23},{25,27},{29,31}} | collective-permute-start | bytes 983048 | tf_op jit(solution)/shard_map/ppermute | solution.py:700
  36.9 9.7 %collective-permute-start.1 = (bf16[8,160,128]{2,1,0:T(8,128)(2,1)}, bf16[8,160,128]{2,1,0:T(8,128)(2,1)S(1)}, u32[]{:S(2)}, u32[]{:S(2)}) collective-permute-start(bf16[8,160,128]{2,1,0:T(8,128)(2,1)} %get-tuple-element.27), channel_id=1, source_target_pairs={{2,3},{6,7},{10,11},{14,15},{18,19},{22,23},{26,27},{30,31}} | collective-permute-start | bytes 983048 | tf_op jit(solution)/shard_map/ppermute | solution.py:700
  46.6 13.1 %copy-start.2 = (bf16[8,160,128]{2,1,0:T(8,128)(2,1)}, bf16[8,160,128]{2,1,0:T(8,128)(2,1)S(1)}, u32[]{:S(2)}) copy-start(bf16[8,160,128]{2,1,0:T(8,128)(2,1)S(1)} %collective-permute-done.refs_0_) | copy-start | bytes 983044
  46.6 13.1 %copy-start.3 = (bf16[8,160,128]{2,1,0:T(8,128)(2,1)}, bf16[8,160,128]{2,1,0:T(8,128)(2,1)S(1)}, u32[]{:S(2)}) copy-start(bf16[8,160,128]{2,1,0:T(8,128)(2,1)S(1)} %collective-permute-done.1.refs_1_) | copy-start | bytes 983044
  46.6 16.0 %all-to-all-start.1 = ((bf16[32,40,128]{2,1,0:T(8,128)(2,1)}), bf16[32,40,128]{2,1,0:T(8,128)(2,1)S(1)}, u32[]{:S(2)}, u32[]{:S(2)}) async-start(bf16[32,40,128]{2,1,0:T(8,128)(2,1)} %bitcast.22), calls=%async_computation.1 | async-start | bytes 655360 | tf_op jit(solution)/shard_map/all_to_all | solution.py:721
  62.6 0.7 copy-start

commit v9 on v8

--- a/solution.py
+++ b/solution.py
@@ -40,6 +40,7 @@
         self.tiles = degrees // SLAB
         self.packed = self.tiles + 1
         self.pitch = up_to(2 * self.packed, 8)
+        self.stride = self.pitch + 1
         self.pitch_bf16 = up_to(2 * self.packed, 16)
         self.slot_rows = fields * self.tiles * 2
         self.field_pad = up_to(fields, 8)
@@ -183,7 +184,7 @@
         return jnp.concatenate([own, other], axis=0).astype(jnp.bfloat16)
 
 
-AHEAD = 6
+AHEAD = 4
 BEHIND = 4
 
 
@@ -260,13 +261,13 @@
             place = step * (sz.block // 2) + k
             for f in range(sz.fields):
                 rows = x_all[place, f].astype(jnp.float32)
-                wide[k, pl.ds(f * sz.pitch, sz.pitch), :] = rows[0:sz.pitch]
+                wide[k, pl.ds(f * sz.stride, sz.pitch), :] = rows[0:sz.pitch]
         for k in range(sz.block // 2):
             place = step * (sz.block // 2) + k
             pair = pair_at(place)
             values = jnp.concatenate([
                 jnp.concatenate([
-                    wide[k, pl.ds(2 * t + c, sz.field_pad, stride=sz.pitch), :] for c in range(2)
+                    wide[k, pl.ds(2 * t + c, sz.field_pad, stride=sz.stride), :] for c in range(2)
                 ], axis=0).astype(jnp.bfloat16)
                 for t in range(sz.packed)
             ], axis=1)
@@ -593,7 +594,7 @@
                 tends = dot(values, tables[:, first * SLAB:(first + count) * SLAB])
                 for t in range(first, first + count):
                     for c in range(2):
-                        rows = pl.ds(2 * t + c, sz.field_pad, stride=sz.pitch)
+                        rows = pl.ds(2 * t + c, sz.field_pad, stride=sz.stride)
                         wide[k, rows, :] = tends[
                             c * sz.field_pad:(c + 1) * sz.field_pad, (t - first) * SLAB:(t - first + 1) * SLAB
                         ]
@@ -612,7 +613,8 @@
             for f in range(sz.fields):
                 rows = pl.ds(f * sz.pitch, sz.pitch)
                 old = x_all[place, f].astype(jnp.float32)[0:sz.pitch]
-                new = (old + time_step * wide[k, rows, :]) * inverse[pair.start, rows, :]
+                tend = wide[k, pl.ds(f * sz.stride, sz.pitch), :]
+                new = (old + time_step * tend) * inverse[pair.start, rows, :]
                 out_all[at, k, rows, :] = jnp.where(live, new, 0.0)
         for k in range(each):
             leave(step * each + k, k)
@@ -642,6 +644,8 @@
     tables = legendre.transpose(0, 2, 1)
 
     rounds = geo_rounds(sz)
+    senders = [source for pairs in rounds for source, _ in pairs]
+    sums = [sum(rounds, [])] if len(set(senders)) == len(senders) else rounds
     spots_shape = pltpu.VMEM((sz.spots * sz.rows, SLAB), jnp.float32)
     pairs = slots // 2
     stream_scratch = [
@@ -650,18 +654,18 @@
         pltpu.SemaphoreType.DMA((pairs,)),
         pltpu.SemaphoreType.DMA((pairs,)),
     ]
-    wide_shape = pltpu.VMEM((sz.block // 2, sz.field_pad * sz.pitch, SLAB), jnp.float32)
+    wide_shape = pltpu.VMEM((sz.block // 2, up_to(sz.field_pad * sz.stride, 8), SLAB), jnp.float32)
     anywhere = pl.BlockSpec(memory_space=pl.ANY)
     vmem = pl.BlockSpec(memory_space=pltpu.VMEM)
     send_shape = (sz.bands, sz.groups, sz.chunk, SLAB)
     geo_shape = (sz.rows // 2, sz.spots, SLAB)
 
     sent, *geo = pl.pallas_call(
-        functools.partial(inverse_kernel, sz, rounds),
+        functools.partial(inverse_kernel, sz, sums),
         in_specs=[smem(), smem(), smem(), smem(), anywhere, anywhere],
-        out_specs=[vmem] * (1 + len(rounds)),
+        out_specs=[vmem] * (1 + len(sums)),
         out_shape=[jax.ShapeDtypeStruct(send_shape, jnp.bfloat16)]
-        + [jax.ShapeDtypeStruct(geo_shape, jnp.bfloat16)] * len(rounds),
+        + [jax.ShapeDtypeStruct(geo_shape, jnp.bfloat16)] * len(sums),
         scratch_shapes=[wide_shape, spots_shape, pltpu.VMEM((sz.spots, SLAB), jnp.int32), *stream_scratch],
         compiler_params=params(56),
         name="inverse_legendre",
@@ -697,7 +701,7 @@
 
     even_row = even_wave.reshape(1, sz.pairs)
     *geo, arrived, basis, even_row = lax.optimization_barrier((*geo, arrived, basis, even_row))
-    moved = [lax.ppermute(geo[turn], "lev", pairs) for turn, pairs in enumerate(rounds)]
+    moved = [lax.ppermute(geo[turn % len(sums)], "lev", pairs) for turn, pairs in enumerate(rounds)]
     returned = pl.pallas_call(
         functools.partial(grid_kernel, sz),
         in_specs=[smem(), smem(), vmem, vmem, anywhere],

time: 87.7 us -> 84.5 us (0.964)
  Pallas kernels: 64.2 us -> 61 us
    pallas_call x1, Pallas kernels: 16.9 us -> 14.9 us  [shards(): pl.pallas_call(functools.partial(inverse_kernel, sz, sums), in_specs=[sme...]
    pallas_call x1, Pallas kernels: 23.8 us -> 22.6 us  [shards(): pl.pallas_call(functools.partial(forward_kernel, sz), in_specs=[smem(), s...]
  transfers between devices with their start and end apart: 4 -> 4, of which waited for: 2 -> 2; matrix products, arithmetic and copies ran while one was open for 2% -> 2% of each run, Pallas kernels for 27% -> 28%
where the time goes in v9:
time: 84.5 us; the launch traced here: 84 us
  Pallas kernels  61 us (72%)
  starting transfers between devices  12.7 us (15%)
  waiting for transfers between devices  7.71 us (9%)
  local copies, waits for them, and re-layouts  2.22 us (3%)
    pallas_call x1, Pallas kernels, shards(): pl.pallas_call(functools.partial(forward_kernel, sz), in_specs=[smem(), s...  22.6 us
    pallas_call x1, Pallas kernels, shards(): pl.pallas_call(functools.partial(inverse_kernel, sz, sums), in_specs=[sme...  14.9 us
    pallas_call x1, Pallas kernels, shards(): pl.pallas_call(functools.partial(grid_kernel, sz), in_specs=[smem(), smem...  9 us
    pallas_call x1, Pallas kernels, shards(): pl.pallas_call(functools.partial(zeros_kernel, sz), in_specs=[smem()], ou...  8.88 us
    all_to_all x1, starting transfers between devices, shards(): lax.all_to_all(sent.reshape(flat), both, split_axis=0, concat_axis=0, til...  7.29 us
    pallas_call x1, Pallas kernels, shards(): pl.pallas_call(functools.partial(basis_kernel, sz), grid=(sz.sorted // hi...  5.64 us
    all_to_all x1, waiting for transfers between devices, shards(): lax.all_to_all(sent.reshape(flat), both, split_axis=0, concat_axis=0, til...  4.81 us
    all_to_all x1, starting transfers between devices, shards(): lax.all_to_all(returned.reshape(flat), both, split_axis=0, concat_axis=0,...  4.06 us
  transfers between devices with their start and end apart: 4, of which 2 were waited for; matrix products, arithmetic and copies ran while one was open for 2% of the time, Pallas kernels for 28%

profile of v9, /device:TPU:0, one launch (start us, length us, event | category | flops | bytes accessed | tf_op | source)
XLA Modules:
  0.0 84.0 jit_solution(17264925659862265506)
XLA Ops:
  0.0 0.0 copy-start.4
  0.0 14.9 %inverse_legendre.1 = (bf16[8,4,40,128]{3,2,1,0:T(8,128)(2,1)}, bf16[8,160,128]{2,1,0:T(8,128)(2,1)}) custom-call(s32[1280]{0:T(1024)} %wave.4, s32[16]{0:T(128)} %points.4, f32[16]{0:T(128)} %gauss.3, f32[24]{0:T(128)} %layer_depth.1, bf16[160,30,10,2,128]{4,3,2,1,0:T(2,128)(2,1)} %bitcast.16, bf16[160,16,1280]{2,1,0:T(8,128)(2,1)} %bitcast.18), custom_call_target="tpu_custom_call" | custom-call | tf_op jit(solution)/shard_map/inverse_legendre/pallas_call | solution.py:663
  14.9 7.3 %all-to-all-start = ((bf16[32,40,128]{2,1,0:T(8,128)(2,1)}), bf16[32,40,128]{2,1,0:T(8,128)(2,1)S(1)}, u32[]{:S(2)}, u32[]{:S(2)}) async-start(bf16[32,40,128]{2,1,0:T(8,128)(2,1)} %bitcast.23), calls=%async_computation | async-start | bytes 655360 | tf_op jit(solution)/shard_map/all_to_all | solution.py:678
  22.2 0.0 copy-done.4
  22.3 0.3 reshape.28
  22.5 0.3 slice_reduce_fusion
  22.9 0.1 squeeze.8
  23.0 0.1 squeeze.7
  23.1 0.7 reshape_reshape.3.even_row
  23.8 5.6 %basis.1.basis_hbm = bf16[4,640,1408]{2,1,0:T(8,128)(2,1)} custom-call(s32[16]{0:T(128)} %points.4), custom_call_target="tpu_custom_call" | custom-call | flops 18022400 | bytes 7208960 | tf_op jit(solution)/shard_map/basis/pallas_call | solution.py:688
  29.4 4.8 %all-to-all-done = bf16[32,40,128]{2,1,0:T(8,128)(2,1)S(1)} async-done(((bf16[32,40,128]{2,1,0:T(8,128)(2,1)}), bf16[32,40,128]{2,1,0:T(8,128)(2,1)S(1)}, u32[]{:S(2)}, u32[]{:S(2)}) %all-to-all-start) | async-done | bytes 327712 | tf_op jit(solution)/shard_map/all_to_all | solution.py:678
  34.2 0.0 copy-start.1
  34.2 0.7 collective-permute-start.1
  34.9 0.7 collective-permute-start
  35.6 0.0 copy-done.1
  35.6 9.0 %grid_products.1 = bf16[8,4,40,128]{3,2,1,0:T(8,128)(2,1)} custom-call(s32[16]{0:T(128)} %points.4, f32[16]{0:T(128)} %gauss.3, bf16[8,4,40,128]{3,2,1,0:T(8,128)(2,1)} %bitcast.21, s32[1,640]{1,0:T(1,128)} %reshape_reshape.3.even_row, bf16[4,640,1408]{2,1,0:T(8,128)(2,1)} %basis.1.basis_hbm), custom_call_target="tpu_custom_call" | custom-call | flops 1845493760 | bytes 7208960 | tf_op jit(solution)/shard_map/grid_products/pallas_call | solution.py:705
  44.6 0.0 collective-permute-done.1.refs_1_
  44.6 0.0 copy-start.2
  44.6 0.0 collective-permute-done.refs_0_
  44.6 0.0 copy-start.3
  44.7 4.1 %all-to-all-start.1 = ((bf16[32,40,128]{2,1,0:T(8,128)(2,1)}), bf16[32,40,128]{2,1,0:T(8,128)(2,1)S(1)}, u32[]{:S(2)}, u32[]{:S(2)}) async-start(bf16[32,40,128]{2,1,0:T(8,128)(2,1)} %bitcast.22), calls=%async_computation.1 | async-start | bytes 655360 | tf_op jit(solution)/shard_map/all_to_all | solution.py:725
  48.7 8.9 %dead_zeros.1.refs_4_ = f32[160,30,10,2,128]{4,3,2,1,0:T(2,128)} custom-call(s32[1280]{0:T(1024)} %wave.4), custom_call_target="tpu_custom_call" | custom-call | bytes 24576000 | tf_op jit(solution)/shard_map/dead_zeros/pallas_call | solution.py:728
  57.6 0.0 copy-done.2
  57.6 0.0 copy-done.3
  57.6 2.9 %all-to-all-done.1 = bf16[32,40,128]{2,1,0:T(8,128)(2,1)S(1)} async-done(((bf16[32,40,128]{2,1,0:T(8,128)(2,1)}), bf16[32,40,128]{2,1,0:T(8,128)(2,1)S(1)}, u32[]{:S(2)}, u32[]{:S(2)}) %all-to-all-start.1) | async-done | bytes 327712 | tf_op jit(solution)/shard_map/all_to_all | solution.py:725
  60.5 0.0 copy-start
  60.5 0.7 copy-done
  61.3 22.6 %forward_legendre.1 = f32[160,30,10,2,128]{4,3,2,1,0:T(2,128)} custom-call(s32[1280]{0:T(1024)} %wave.4, f32[30]{0:T(128)} %speed.1, bf16[8,4,40,128]{3,2,1,0:T(8,128)(2,1)} %bitcast.20, bf16[8,160,128]{2,1,0:T(8,128)(2,1)} %copy-done.3, bf16[8,160,128]{2,1,0:T(8,128)(2,1)} %copy-done.2, ...), custom_call_target="tpu_custom_call", output_to_operand_aliasing={{}: (7, {})} | custom-call | tf_op jit(solution)/shard_map/forward_legendre/pallas_call | solution.py:743
  (2 shorter events, 0.0 us)
Async XLA Ops:
  0.0 22.2 %copy-start.4 = (s32[1280]{0:T(1024)S(1)}, s32[1280]{0:T(1024)}, u32[]{:S(2)}) copy-start(s32[1280]{0:T(1024)} %wave.4) | copy-start | bytes 15364
  14.9 19.3 %all-to-all-start = ((bf16[32,40,128]{2,1,0:T(8,128)(2,1)}), bf16[32,40,128]{2,1,0:T(8,128)(2,1)S(1)}, u32[]{:S(2)}, u32[]{:S(2)}) async-start(bf16[32,40,128]{2,1,0:T(8,128)(2,1)} %bitcast.23), calls=%async_computation | async-start | bytes 655360 | tf_op jit(solution)/shard_map/all_to_all | solution.py:678
  34.2 1.4 %copy-start.1 = (bf16[32,40,128]{2,1,0:T(8,128)(2,1)}, bf16[32,40,128]{2,1,0:T(8,128)(2,1)S(1)}, u32[]{:S(2)}) copy-start(bf16[32,40,128]{2,1,0:T(8,128)(2,1)S(1)} %all-to-all-done) | copy-start | bytes 983044
  34.2 10.4 %collective-permute-start.1 = (bf16[8,160,128]{2,1,0:T(8,128)(2,1)}, bf16[8,160,128]{2,1,0:T(8,128)(2,1)S(1)}, u32[]{:S(2)}, u32[]{:S(2)}) collective-permute-start(bf16[8,160,128]{2,1,0:T(8,128)(2,1)} %get-tuple-element.23), channel_id=1, source_target_pairs={{2,3},{6,7},{10,11},{14,15},{18,19},{22,23},{26,27},{30,31}} | collective-permute-start | bytes 983048 | tf_op jit(solution)/shard_map/ppermute | solution.py:704
  34.9 9.7 %collective-permute-start = (bf16[8,160,128]{2,1,0:T(8,128)(2,1)}, bf16[8,160,128]{2,1,0:T(8,128)(2,1)S(1)}, u32[]{:S(2)}, u32[]{:S(2)}) collective-permute-start(bf16[8,160,128]{2,1,0:T(8,128)(2,1)} %get-tuple-element.23), channel_id=1, source_target_pairs={{1,3},{5,7},{9,11},{13,15},{17,19},{21,23},{25,27},{29,31}} | collective-permute-start | bytes 983048 | tf_op jit(solution)/shard_map/ppermute | solution.py:704
  44.6 13.0 %copy-start.2 = (bf16[8,160,128]{2,1,0:T(8,128)(2,1)}, bf16[8,160,128]{2,1,0:T(8,128)(2,1)S(1)}, u32[]{:S(2)}) copy-start(bf16[8,160,128]{2,1,0:T(8,128)(2,1)S(1)} %collective-permute-done.1.refs_1_) | copy-start | bytes 983044
  44.6 13.0 %copy-start.3 = (bf16[8,160,128]{2,1,0:T(8,128)(2,1)}, bf16[8,160,128]{2,1,0:T(8,128)(2,1)S(1)}, u32[]{:S(2)}) copy-start(bf16[8,160,128]{2,1,0:T(8,128)(2,1)S(1)} %collective-permute-done.refs_0_) | copy-start | bytes 983044
  44.7 15.9 %all-to-all-start.1 = ((bf16[32,40,128]{2,1,0:T(8,128)(2,1)}), bf16[32,40,128]{2,1,0:T(8,128)(2,1)S(1)}, u32[]{:S(2)}, u32[]{:S(2)}) async-start(bf16[32,40,128]{2,1,0:T(8,128)(2,1)} %bitcast.22), calls=%async_computation.1 | async-start | bytes 655360 | tf_op jit(solution)/shard_map/all_to_all | solution.py:725
  60.5 0.7 copy-start

commit v10 on v9

--- a/solution.py
+++ b/solution.py
@@ -262,18 +262,22 @@
             for f in range(sz.fields):
                 rows = x_all[place, f].astype(jnp.float32)
                 wide[k, pl.ds(f * sz.stride, sz.pitch), :] = rows[0:sz.pitch]
+        pairs, tables, values = [], [], []
         for k in range(sz.block // 2):
             place = step * (sz.block // 2) + k
-            pair = pair_at(place)
-            values = jnp.concatenate([
+            pairs.append(pair_at(place))
+            tables.append(pairs[k].tables(leg_all[place]))
+            values.append(jnp.concatenate([
                 jnp.concatenate([
                     wide[k, pl.ds(2 * t + c, sz.field_pad, stride=sz.stride), :] for c in range(2)
                 ], axis=0).astype(jnp.bfloat16)
                 for t in range(sz.packed)
-            ], axis=1)
-            total = dot(pair.tables(leg_all[place]), values, ((1,), (1,)))
+            ], axis=1))
+        totals = dot(jnp.concatenate(tables, axis=0), jnp.concatenate(values, axis=0), ((1,), (1,)))
+        for k, pair in enumerate(pairs):
             for side in range(2):
-                found.append((pair, side, total[side * sz.rows:(side + 1) * sz.rows]))
+                first = (2 * k + side) * sz.rows
+                found.append((pair, side, totals[first:first + sz.rows, k * pad:(k + 1) * pad]))
         for pair, side, total in found:
             spots[pair.rows(side), 0:pad] = total
             number = jnp.full((1, SLAB), pair.numbers[side], jnp.int32)
@@ -308,23 +312,30 @@
     number = numbers[...]
     lane = iota((sz.spots, SLAB), 1)
     known = (number >= 0) & ~((number == 0) & (lane & sz.field_pad != 0))
+    exacts, cuts, scales = [], [], []
     for rp in range(sz.rows // 2):
         exact = jnp.concatenate([
             spots[pl.ds(2 * rp + r, sz.spots, stride=sz.rows), :][:, 0:pad] for r in range(2)
         ], axis=1)
-        cut = jnp.concatenate([
+        cuts.append(jnp.concatenate([
             exact[q * sz.chunk:(q + 1) * sz.chunk] for q in range(sz.quarters)
-        ], axis=1).astype(jnp.bfloat16)
-        chunk = dot(cut, spread).astype(jnp.bfloat16)
-        for g in range(sz.groups):
-            send_ref[rp, g] = chunk[:, g * SLAB:(g + 1) * SLAB]
+        ], axis=1))
+        exacts.append(exact)
         count = jnp.where(lane < pad, points[2 * rp], points[2 * rp + 1])
         scale = jnp.where(lane < pad, gauss[2 * rp], gauss[2 * rp + 1])
-        scale = jnp.where(known & (2 * number <= count - 1), scale, 0.0)
-        exact = exact.astype(jnp.bfloat16)
-        double = jnp.concatenate([exact, exact], axis=1)
-        for turn in range(len(rounds)):
-            geo_refs[turn][rp] = (dot(double, weights[turn]) * scale).astype(jnp.bfloat16)
+        scales.append(jnp.where(known & (2 * number <= count - 1), scale, 0.0))
+    chunks = dot(jnp.concatenate(cuts, axis=0).astype(jnp.bfloat16), spread)
+    exact = jnp.concatenate(exacts, axis=0).astype(jnp.bfloat16)
+    double = jnp.concatenate([exact, exact], axis=1)
+    for turn in range(len(rounds)):
+        sums = dot(double, weights[turn])
+        for rp in range(sz.rows // 2):
+            own = sums[rp * sz.spots:(rp + 1) * sz.spots] * scales[rp]
+            geo_refs[turn][rp] = own.astype(jnp.bfloat16)
+    for rp in range(sz.rows // 2):
+        for g in range(sz.groups):
+            chunk = chunks[rp * sz.chunk:(rp + 1) * sz.chunk, g * SLAB:(g + 1) * SLAB]
+            send_ref[rp, g] = chunk.astype(jnp.bfloat16)
 
 
 def cos_sin(z):
@@ -432,13 +443,16 @@
     number = iota((2 * SLAB, sz.sorted), 1) * 2
     bound = jnp.where(iota((2 * SLAB, sz.sorted), 0) & half_slab == 0, length_a, length_b) - 1
     kept = (0, half_slab, SLAB, SLAB + half_slab)
+    sources = []
     for parity in range(2):
         rows = []
         for half in range(sz.halves):
             piece = (parity * sz.halves + half) * 2
             rows.append(taken[:, piece * SLAB:(piece + 2) * SLAB])
-        values = jnp.concatenate(rows, axis=0).T.astype(jnp.bfloat16)
-        placed = dot(values, order, ((1,), (1,)))
+        sources.append(jnp.concatenate(rows, axis=0).T)
+    ordered = dot(jnp.concatenate(sources, axis=0).astype(jnp.bfloat16), order, ((1,), (1,)))
+    for parity in range(2):
+        placed = ordered[parity * 2 * SLAB:(parity + 1) * 2 * SLAB]
         mine = number if parity == 0 else sz.trunc - number
         mult = jnp.where(mine == 0, 1.0, 2.0)
         placed = jnp.where(2 * mine <= bound, placed * mult, 0.0)
@@ -483,18 +497,17 @@
     number = iota((sz.sorted, SLAB), 0) * 2
     even_col = jnp.broadcast_to(even_row[...].astype(jnp.float32), (8, sz.pairs)).T[:, 0:1]
     back_order = one_hot(iota((sz.pairs, sz.sorted), 1) * 2 == even_col.astype(jnp.int32))
-    pieces = []
+    sums = []
     for parity in range(2):
         mine = number if parity == 0 else sz.trunc - number
-        sums = jnp.concatenate([
-            jnp.where(
-                2 * mine <= bound,
-                dot(basis[parity * 2 + comp], terms[parity * 2 + comp], ((1,), (1,))) * scale, 0.0,
-            ).astype(jnp.bfloat16)
-            for comp in range(2)
-        ], axis=1)
-        slots = dot(back_order, sums).astype(jnp.bfloat16)
-        pieces += [slots[half * width:(half + 1) * width] for half in range(sz.halves)]
+        for k in (2 * parity, 2 * parity + 1):
+            total = dot(basis[k], terms[k], ((1,), (1,))) * scale
+            sums.append(jnp.where(2 * mine <= bound, total, 0.0).astype(jnp.bfloat16))
+    slots = dot(back_order, jnp.concatenate(sums, axis=1)).astype(jnp.bfloat16)
+    pieces = [
+        slots[half * width:(half + 1) * width, 2 * parity * SLAB:2 * (parity + 1) * SLAB]
+        for parity in range(2) for half in range(sz.halves)
+    ]
     sent = dot(jnp.concatenate(pieces, axis=1), take, ((1,), (1,)))
     for g in range(sz.groups):
         part = sent[:, g * SLAB:(g + 1) * SLAB].reshape(sz.bands, sz.chunk, SLAB)
@@ -540,9 +553,13 @@
     each = sz.block // 2
 
     gather = spread_matrix(sz, lax.axis_index("lev"))
+    cuts = [
+        jnp.concatenate([back_ref[rp, g].astype(jnp.float32) for g in range(sz.groups)], axis=1)
+        for rp in range(sz.rows // 2)
+    ]
+    wholes = dot(jnp.concatenate(cuts, axis=0).astype(jnp.bfloat16), gather, ((1,), (1,)))
     for rp in range(sz.rows // 2):
-        cut = jnp.concatenate([back_ref[rp, g] for g in range(sz.groups)], axis=1)
-        whole = dot(cut, gather, ((1,), (1,)))
+        whole = wholes[rp * sz.chunk:(rp + 1) * sz.chunk]
         rows = jnp.concatenate([
             whole[:, q * 2 * pad:(q + 1) * 2 * pad] for q in range(sz.quarters)
         ], axis=0)

time: 84.5 us -> 85.5 us (1.012)
  Pallas kernels: 61 us -> 62.2 us
    pallas_call x1, Pallas kernels: 14.9 us -> 17.3 us  [shards(): pl.pallas_call(functools.partial(inverse_kernel, sz, sums), in_specs=[sme...]
  transfers between devices with their start and end apart: 4 -> 4, of which waited for: 2 -> 2; matrix products, arithmetic and copies ran while one was open for 2% -> 2% of each run, Pallas kernels for 28% -> 27%
where the time goes in v10:
time: 85.5 us; the launch traced here: 85.1 us
  Pallas kernels  62.2 us (73%)
  starting transfers between devices  12.7 us (15%)
  waiting for transfers between devices  7.7 us (9%)
  local copies, waits for them, and re-layouts  2.22 us (3%)
    pallas_call x1, Pallas kernels, shards(): pl.pallas_call(functools.partial(forward_kernel, sz), in_specs=[smem(), s...  21.8 us
    pallas_call x1, Pallas kernels, shards(): pl.pallas_call(functools.partial(inverse_kernel, sz, sums), in_specs=[sme...  17.3 us
    pallas_call x1, Pallas kernels, shards(): pl.pallas_call(functools.partial(zeros_kernel, sz), in_specs=[smem()], ou...  8.89 us
    pallas_call x1, Pallas kernels, shards(): pl.pallas_call(functools.partial(grid_kernel, sz), in_specs=[smem(), smem...  8.57 us
    all_to_all x1, starting transfers between devices, shards(): lax.all_to_all(sent.reshape(flat), both, split_axis=0, concat_axis=0, til...  7.29 us
    pallas_call x1, Pallas kernels, shards(): pl.pallas_call(functools.partial(basis_kernel, sz), grid=(sz.sorted // hi...  5.64 us
    all_to_all x1, waiting for transfers between devices, shards(): lax.all_to_all(sent.reshape(flat), both, split_axis=0, concat_axis=0, til...  4.81 us
    all_to_all x1, starting transfers between devices, shards(): lax.all_to_all(returned.reshape(flat), both, split_axis=0, concat_axis=0,...  4.05 us
  transfers between devices with their start and end apart: 4, of which 2 were waited for; matrix products, arithmetic and copies ran while one was open for 2% of the time, Pallas kernels for 27%

profile of v10, /device:TPU:0, one launch (start us, length us, event | category | flops | bytes accessed | tf_op | source)
XLA Modules:
  0.0 85.1 jit_solution(3020670046462692751)
XLA Ops:
  0.0 0.0 copy-start.4
  0.0 17.3 %inverse_legendre.1 = (bf16[8,4,40,128]{3,2,1,0:T(8,128)(2,1)}, bf16[8,160,128]{2,1,0:T(8,128)(2,1)}) custom-call(s32[1280]{0:T(1024)} %wave.4, s32[16]{0:T(128)} %points.4, f32[16]{0:T(128)} %gauss.3, f32[24]{0:T(128)} %layer_depth.1, bf16[160,30,10,2,128]{4,3,2,1,0:T(2,128)(2,1)} %bitcast.16, bf16[160,16,1280]{2,1,0:T(8,128)(2,1)} %bitcast.18), custom_call_target="tpu_custom_call" | custom-call | tf_op jit(solution)/shard_map/inverse_legendre/pallas_call | solution.py:680
  17.4 7.3 %all-to-all-start = ((bf16[32,40,128]{2,1,0:T(8,128)(2,1)}), bf16[32,40,128]{2,1,0:T(8,128)(2,1)S(1)}, u32[]{:S(2)}, u32[]{:S(2)}) async-start(bf16[32,40,128]{2,1,0:T(8,128)(2,1)} %bitcast.23), calls=%async_computation | async-start | bytes 655360 | tf_op jit(solution)/shard_map/all_to_all | solution.py:695
  24.6 0.0 copy-done.4
  24.7 0.3 reshape.28
  24.9 0.3 slice_reduce_fusion
  25.3 0.1 squeeze.8
  25.4 0.1 squeeze.7
  25.5 0.7 reshape_reshape.3.even_row
  26.2 5.6 %basis.1.basis_hbm = bf16[4,640,1408]{2,1,0:T(8,128)(2,1)} custom-call(s32[16]{0:T(128)} %points.4), custom_call_target="tpu_custom_call" | custom-call | flops 18022400 | bytes 7208960 | tf_op jit(solution)/shard_map/basis/pallas_call | solution.py:705
  31.8 4.8 %all-to-all-done = bf16[32,40,128]{2,1,0:T(8,128)(2,1)S(1)} async-done(((bf16[32,40,128]{2,1,0:T(8,128)(2,1)}), bf16[32,40,128]{2,1,0:T(8,128)(2,1)S(1)}, u32[]{:S(2)}, u32[]{:S(2)}) %all-to-all-start) | async-done | bytes 327712 | tf_op jit(solution)/shard_map/all_to_all | solution.py:695
  36.6 0.0 copy-start.1
  36.6 0.7 collective-permute-start.1
  37.3 0.7 collective-permute-start
  38.0 0.0 copy-done.1
  38.0 8.6 %grid_products.1 = bf16[8,4,40,128]{3,2,1,0:T(8,128)(2,1)} custom-call(s32[16]{0:T(128)} %points.4, f32[16]{0:T(128)} %gauss.3, bf16[8,4,40,128]{3,2,1,0:T(8,128)(2,1)} %bitcast.21, s32[1,640]{1,0:T(1,128)} %reshape_reshape.3.even_row, bf16[4,640,1408]{2,1,0:T(8,128)(2,1)} %basis.1.basis_hbm), custom_call_target="tpu_custom_call" | custom-call | flops 1845493760 | bytes 7208960 | tf_op jit(solution)/shard_map/grid_products/pallas_call | solution.py:722
  46.6 0.0 collective-permute-done.1.refs_1_
  46.6 0.0 copy-start.2
  46.6 0.0 collective-permute-done.refs_0_
  46.6 0.0 copy-start.3
  46.6 4.0 %all-to-all-start.1 = ((bf16[32,40,128]{2,1,0:T(8,128)(2,1)}), bf16[32,40,128]{2,1,0:T(8,128)(2,1)S(1)}, u32[]{:S(2)}, u32[]{:S(2)}) async-start(bf16[32,40,128]{2,1,0:T(8,128)(2,1)} %bitcast.22), calls=%async_computation.1 | async-start | bytes 655360 | tf_op jit(solution)/shard_map/all_to_all | solution.py:742
  50.7 8.9 %dead_zeros.1.refs_4_ = f32[160,30,10,2,128]{4,3,2,1,0:T(2,128)} custom-call(s32[1280]{0:T(1024)} %wave.4), custom_call_target="tpu_custom_call" | custom-call | bytes 24576000 | tf_op jit(solution)/shard_map/dead_zeros/pallas_call | solution.py:745
  59.6 0.0 copy-done.2
  59.6 0.0 copy-done.3
  59.6 2.9 %all-to-all-done.1 = bf16[32,40,128]{2,1,0:T(8,128)(2,1)S(1)} async-done(((bf16[32,40,128]{2,1,0:T(8,128)(2,1)}), bf16[32,40,128]{2,1,0:T(8,128)(2,1)S(1)}, u32[]{:S(2)}, u32[]{:S(2)}) %all-to-all-start.1) | async-done | bytes 327712 | tf_op jit(solution)/shard_map/all_to_all | solution.py:742
  62.5 0.0 copy-start
  62.5 0.7 copy-done
  63.2 21.8 %forward_legendre.1 = f32[160,30,10,2,128]{4,3,2,1,0:T(2,128)} custom-call(s32[1280]{0:T(1024)} %wave.4, f32[30]{0:T(128)} %speed.1, bf16[8,4,40,128]{3,2,1,0:T(8,128)(2,1)} %bitcast.20, bf16[8,160,128]{2,1,0:T(8,128)(2,1)} %copy-done.3, bf16[8,160,128]{2,1,0:T(8,128)(2,1)} %copy-done.2, ...), custom_call_target="tpu_custom_call", output_to_operand_aliasing={{}: (7, {})} | custom-call | tf_op jit(solution)/shard_map/forward_legendre/pallas_call | solution.py:760
  (2 shorter events, 0.0 us)
Async XLA Ops:
  0.0 24.6 %copy-start.4 = (s32[1280]{0:T(1024)S(1)}, s32[1280]{0:T(1024)}, u32[]{:S(2)}) copy-start(s32[1280]{0:T(1024)} %wave.4) | copy-start | bytes 15364
  17.4 19.3 %all-to-all-start = ((bf16[32,40,128]{2,1,0:T(8,128)(2,1)}), bf16[32,40,128]{2,1,0:T(8,128)(2,1)S(1)}, u32[]{:S(2)}, u32[]{:S(2)}) async-start(bf16[32,40,128]{2,1,0:T(8,128)(2,1)} %bitcast.23), calls=%async_computation | async-start | bytes 655360 | tf_op jit(solution)/shard_map/all_to_all | solution.py:695
  36.6 1.4 %copy-start.1 = (bf16[32,40,128]{2,1,0:T(8,128)(2,1)}, bf16[32,40,128]{2,1,0:T(8,128)(2,1)S(1)}, u32[]{:S(2)}) copy-start(bf16[32,40,128]{2,1,0:T(8,128)(2,1)S(1)} %all-to-all-done) | copy-start | bytes 983044
  36.6 10.0 %collective-permute-start.1 = (bf16[8,160,128]{2,1,0:T(8,128)(2,1)}, bf16[8,160,128]{2,1,0:T(8,128)(2,1)S(1)}, u32[]{:S(2)}, u32[]{:S(2)}) collective-permute-start(bf16[8,160,128]{2,1,0:T(8,128)(2,1)} %get-tuple-element.23), channel_id=1, source_target_pairs={{2,3},{6,7},{10,11},{14,15},{18,19},{22,23},{26,27},{30,31}} | collective-permute-start | bytes 983048 | tf_op jit(solution)/shard_map/ppermute | solution.py:721
  37.3 9.3 %collective-permute-start = (bf16[8,160,128]{2,1,0:T(8,128)(2,1)}, bf16[8,160,128]{2,1,0:T(8,128)(2,1)S(1)}, u32[]{:S(2)}, u32[]{:S(2)}) collective-permute-start(bf16[8,160,128]{2,1,0:T(8,128)(2,1)} %get-tuple-element.23), channel_id=1, source_target_pairs={{1,3},{5,7},{9,11},{13,15},{17,19},{21,23},{25,27},{29,31}} | collective-permute-start | bytes 983048 | tf_op jit(solution)/shard_map/ppermute | solution.py:721
  46.6 13.0 %copy-start.2 = (bf16[8,160,128]{2,1,0:T(8,128)(2,1)}, bf16[8,160,128]{2,1,0:T(8,128)(2,1)S(1)}, u32[]{:S(2)}) copy-start(bf16[8,160,128]{2,1,0:T(8,128)(2,1)S(1)} %collective-permute-done.1.refs_1_) | copy-start | bytes 983044
  46.6 13.0 %copy-start.3 = (bf16[8,160,128]{2,1,0:T(8,128)(2,1)}, bf16[8,160,128]{2,1,0:T(8,128)(2,1)S(1)}, u32[]{:S(2)}) copy-start(bf16[8,160,128]{2,1,0:T(8,128)(2,1)S(1)} %collective-permute-done.refs_0_) | copy-start | bytes 983044
  46.6 15.9 %all-to-all-start.1 = ((bf16[32,40,128]{2,1,0:T(8,128)(2,1)}), bf16[32,40,128]{2,1,0:T(8,128)(2,1)S(1)}, u32[]{:S(2)}, u32[]{:S(2)}) async-start(bf16[32,40,128]{2,1,0:T(8,128)(2,1)} %bitcast.22), calls=%async_computation.1 | async-start | bytes 655360 | tf_op jit(solution)/shard_map/all_to_all | solution.py:742
  62.5 0.7 copy-start

commit v11 on v10

--- a/solution.py
+++ b/solution.py
@@ -53,6 +53,7 @@
         self.chunk_live = slots // self.quarters
         self.chunk = up_to(self.chunk_live, 8)
         self.spots = self.quarters * self.chunk
+        self.plane = self.spots | 1
         self.block = slots
         for size in (8, 4):
             if slots % size == 0 and (size * self.slot_rows) % 16 == 0:
@@ -156,7 +157,7 @@
         return first + (self.place - half * sz.chunk_live)
 
     def rows(self, side):
-        return pl.ds(pl.multiple_of(self.spot(side) * self.sizes.rows, self.sizes.rows), self.sizes.rows)
+        return pl.ds(self.spot(side), self.sizes.rows, stride=self.sizes.plane)
 
     def tile(self, k):
         return jnp.where(k < self.split, self.start + k, k - 1)
@@ -218,20 +219,24 @@
                 self.leg_sems.at[place],
             ).start()
 
-    def begin(self):
+    def begin(self, turn=0):
+        each = self.sizes.block // 2
+        first, last = (min((turn + k) * AHEAD, self.sizes.steps) * each for k in range(2))
+
         def one(place, carry):
             self.start(place)
             return carry
 
-        lax.fori_loop(0, min(AHEAD * self.sizes.block // 2, self.sizes.slots // 2), one, 0)
+        lax.fori_loop(first, last, one, 0)
+        self.ahead = (turn + 1) * AHEAD
 
     def take(self, step):
         each = self.sizes.block // 2
 
-        @pl.when(step + AHEAD < self.sizes.steps)
+        @pl.when(step + self.ahead < self.sizes.steps)
         def _():
             for k in range(each):
-                self.start((step + AHEAD) * each + k)
+                self.start((step + self.ahead) * each + k)
 
         for k in range(each):
             place = step * each + k
@@ -262,24 +267,22 @@
             for f in range(sz.fields):
                 rows = x_all[place, f].astype(jnp.float32)
                 wide[k, pl.ds(f * sz.stride, sz.pitch), :] = rows[0:sz.pitch]
-        pairs, tables, values = [], [], []
+        empty = jnp.zeros((sz.rows, SLAB - pad), jnp.float32)
         for k in range(sz.block // 2):
             place = step * (sz.block // 2) + k
-            pairs.append(pair_at(place))
-            tables.append(pairs[k].tables(leg_all[place]))
-            values.append(jnp.concatenate([
+            pair = pair_at(place)
+            values = jnp.concatenate([
                 jnp.concatenate([
                     wide[k, pl.ds(2 * t + c, sz.field_pad, stride=sz.stride), :] for c in range(2)
                 ], axis=0).astype(jnp.bfloat16)
                 for t in range(sz.packed)
-            ], axis=1))
-        totals = dot(jnp.concatenate(tables, axis=0), jnp.concatenate(values, axis=0), ((1,), (1,)))
-        for k, pair in enumerate(pairs):
+            ], axis=1)
+            total = dot(pair.tables(leg_all[place]), values, ((1,), (1,)))
             for side in range(2):
-                first = (2 * k + side) * sz.rows
-                found.append((pair, side, totals[first:first + sz.rows, k * pad:(k + 1) * pad]))
+                own = total[side * sz.rows:(side + 1) * sz.rows]
+                found.append((pair, side, jnp.concatenate([own, empty], axis=1)))
         for pair, side, total in found:
-            spots[pair.rows(side), 0:pad] = total
+            spots[pair.rows(side), :] = total
             number = jnp.full((1, SLAB), pair.numbers[side], jnp.int32)
             numbers[pl.ds(pair.spot(side), 1), :] = number
         return carry
@@ -315,7 +318,7 @@
     exacts, cuts, scales = [], [], []
     for rp in range(sz.rows // 2):
         exact = jnp.concatenate([
-            spots[pl.ds(2 * rp + r, sz.spots, stride=sz.rows), :][:, 0:pad] for r in range(2)
+            spots[pl.ds((2 * rp + r) * sz.plane, sz.spots), :][:, 0:pad] for r in range(2)
         ], axis=1)
         cuts.append(jnp.concatenate([
             exact[q * sz.chunk:(q + 1) * sz.chunk] for q in range(sz.quarters)
@@ -349,50 +352,61 @@
     return c, s * z
 
 
-def basis_kernel(sizes, points, out_ref, cosines, sines):
+def basis_kernel(sizes, points, out_hbm, out_all, cosines, sines, sems):
     sz = sizes
-    step = pl.program_id(0)
     turns = sz.sorted // 16
     bands_row = 16 + up_to(turns, 8)
 
-    @pl.when(step == 0)
-    def _():
-        first = lax.axis_index("band") * 2
-        length_a, length_b = points[first], points[first + 1]
-        count_a = length_a // 4 + 1
-        high = cosines.shape[0]
-        row = iota((high, SLAB), 0)
-        number = jnp.where(row < 16, 2 * row, jnp.where(row < bands_row, 32 * (row - 16), sz.trunc))
-        number = number.astype(jnp.float32)
+    first = lax.axis_index("band") * 2
+    length_a, length_b = points[first], points[first + 1]
+    count_a = length_a // 4 + 1
+    high = cosines.shape[0]
+    row = iota((high, SLAB), 0)
+    number = jnp.where(row < 16, 2 * row, jnp.where(row < bands_row, 32 * (row - 16), sz.trunc))
+    number = number.astype(jnp.float32)
+    for at in range(0, sz.orbits, SLAB):
+        place = iota((1, SLAB), 1) + at
+        second = place >= count_a
+        column = (place - jnp.where(second, count_a, 0)).astype(jnp.float32)
+        length = jnp.where(second, length_b, length_a).astype(jnp.float32)
+        inverse = 1.0 / length
+        scale = jnp.where(row < 16, 1.0 / jnp.sqrt(length), 1.0)
+        product = number * column
+        whole = jnp.floor(product * inverse + 0.5)
+        c, s = cos_sin((product - whole * length) * inverse)
+        cosines[:, pl.ds(at, SLAB)] = c * scale
+        sines[:, pl.ds(at, SLAB)] = s * scale
+
+    steps, _, tall, _ = out_all.shape
+    groups = tall // 16
+
+    def leave(step):
+        rows = pl.ds(pl.multiple_of(step * tall, tall), tall)
+        return pltpu.make_async_copy(out_all.at[step], out_hbm.at[:, rows], sems.at[step])
+
+    def part(step, carry):
+        out_ref = out_all.at[step]
         for at in range(0, sz.orbits, SLAB):
-            place = iota((1, SLAB), 1) + at
-            second = place >= count_a
-            column = (place - jnp.where(second, count_a, 0)).astype(jnp.float32)
-            length = jnp.where(second, length_b, length_a).astype(jnp.float32)
-            inverse = 1.0 / length
-            scale = jnp.where(row < 16, 1.0 / jnp.sqrt(length), 1.0)
-            product = number * column
-            whole = jnp.floor(product * inverse + 0.5)
-            c, s = cos_sin((product - whole * length) * inverse)
-            cosines[:, pl.ds(at, SLAB)] = c * scale
-            sines[:, pl.ds(at, SLAB)] = s * scale
-
-    groups = out_ref.shape[1] // 16
-    for at in range(0, sz.orbits, SLAB):
-        cols = pl.ds(at, SLAB)
-        base_c, base_n = cosines[0:16, cols], -sines[0:16, cols]
-        top_c, top_n = cosines[pl.ds(bands_row, 1), cols], -sines[pl.ds(bands_row, 1), cols]
-        turn_rows = pl.ds(pl.multiple_of(16 + step * groups, 8), groups)
-        all_c, all_s = cosines[turn_rows, cols], sines[turn_rows, cols]
-        for k in range(groups):
-            turn_c, turn_s = all_c[k:k + 1], all_s[k:k + 1]
-            c = turn_c * base_c + turn_s * base_n
-            n = turn_c * base_n - turn_s * base_c
-            rows = pl.ds(16 * k, 16)
-            out_ref[0, rows, cols] = c.astype(jnp.bfloat16)
-            out_ref[1, rows, cols] = n.astype(jnp.bfloat16)
-            out_ref[2, rows, cols] = (top_c * c + top_n * n).astype(jnp.bfloat16)
-            out_ref[3, rows, cols] = (top_n * c - top_c * n).astype(jnp.bfloat16)
+            cols = pl.ds(at, SLAB)
+            base_c, base_n = cosines[0:16, cols], -sines[0:16, cols]
+            top_c, top_n = cosines[pl.ds(bands_row, 1), cols], -sines[pl.ds(bands_row, 1), cols]
+            turn_rows = pl.ds(pl.multiple_of(16 + step * groups, 8), groups)
+            all_c, all_s = cosines[turn_rows, cols], sines[turn_rows, cols]
+            for k in range(groups):
+                turn_c, turn_s = all_c[k:k + 1], all_s[k:k + 1]
+                c = turn_c * base_c + turn_s * base_n
+                n = turn_c * base_n - turn_s * base_c
+                rows = pl.ds(16 * k, 16)
+                out_ref[0, rows, cols] = c.astype(jnp.bfloat16)
+                out_ref[1, rows, cols] = n.astype(jnp.bfloat16)
+                out_ref[2, rows, cols] = (top_c * c + top_n * n).astype(jnp.bfloat16)
+                out_ref[3, rows, cols] = (top_n * c - top_c * n).astype(jnp.bfloat16)
+        leave(step).start()
+        return carry
+
+    lax.fori_loop(0, steps, part, 0)
+    for step in range(steps):
+        leave(jnp.int32(step)).wait()
 
 
 def take_matrix(sizes, lev):
@@ -568,7 +582,8 @@
         for r in range(2):
             part = rows[:, r * pad:(r + 1) * pad]
             part = jnp.concatenate([part, jnp.zeros((sz.spots, SLAB - pad), jnp.float32)], axis=1)
-            spots[pl.ds(2 * rp + r, sz.spots, stride=sz.rows), :] = part
+            spots[pl.ds((2 * rp + r) * sz.plane, sz.spots), :] = part
+    stream.begin(1)
     row = quotient(iota((sz.pitch, SLAB), 0), 2)
     lane = iota((sz.pitch, SLAB), 1)
     for start in range(sz.tiles):
@@ -577,6 +592,7 @@
         for f in range(sz.fields):
             denominator = 1.0 + time_step * time_step * helm * speed[f]
             inverse[start, pl.ds(f * sz.pitch, sz.pitch), :] = 1.0 / denominator
+    stream.begin(2)
     out_tiles = out_all.reshape(BEHIND, each, sz.fields, sz.pitch // 2, 2, SLAB)
 
     def leave(place, k):
@@ -663,7 +679,7 @@
     rounds = geo_rounds(sz)
     senders = [source for pairs in rounds for source, _ in pairs]
     sums = [sum(rounds, [])] if len(set(senders)) == len(senders) else rounds
-    spots_shape = pltpu.VMEM((sz.spots * sz.rows, SLAB), jnp.float32)
+    spots_shape = pltpu.VMEM((up_to(sz.plane * sz.rows, 8), SLAB), jnp.float32)
     pairs = slots // 2
     stream_scratch = [
         pltpu.VMEM((pairs, fields, sz.pitch_bf16, SLAB), jnp.bfloat16),
@@ -704,11 +720,15 @@
     table_rows = 16 + up_to(sz.sorted // 16, 8) + 8
     basis = pl.pallas_call(
         functools.partial(basis_kernel, sz),
-        grid=(sz.sorted // high,),
         in_specs=[smem()],
-        out_specs=pl.BlockSpec((4, high, sz.orbits), lambda i: (0, i, 0)),
+        out_specs=anywhere,
         out_shape=jax.ShapeDtypeStruct((4, sz.sorted, sz.orbits), jnp.bfloat16),
-        scratch_shapes=[pltpu.VMEM((table_rows, sz.orbits), jnp.float32)] * 2,
+        scratch_shapes=[
+            pltpu.VMEM((sz.sorted // high, 4, high, sz.orbits), jnp.bfloat16),
+            pltpu.VMEM((table_rows, sz.orbits), jnp.float32),
+            pltpu.VMEM((table_rows, sz.orbits), jnp.float32),
+            pltpu.SemaphoreType.DMA((sz.sorted // high,)),
+        ],
         compiler_params=params(56),
         cost_estimate=pl.CostEstimate(
             flops=20 * sz.sorted * sz.orbits, bytes_accessed=8 * sz.sorted * sz.orbits, transcendentals=0,
@@ -717,8 +737,8 @@
     )(points_later)
 
     even_row = even_wave.reshape(1, sz.pairs)
-    *geo, arrived, basis, even_row = lax.optimization_barrier((*geo, arrived, basis, even_row))
     moved = [lax.ppermute(geo[turn % len(sums)], "lev", pairs) for turn, pairs in enumerate(rounds)]
+    *moved, arrived, basis, even_row = lax.optimization_barrier((*moved, arrived, basis, even_row))
     returned = pl.pallas_call(
         functools.partial(grid_kernel, sz),
         in_specs=[smem(), smem(), vmem, vmem, anywhere],
@@ -737,7 +757,7 @@
     )(
         row_points, gauss_weight, arrived.reshape(send_shape), even_row, basis,
     )
-    *moved, returned, wave_last = lax.optimization_barrier((*moved, returned, slot_wave))
+    returned, wave_last = lax.optimization_barrier((returned, slot_wave))
 
     back = lax.all_to_all(returned.reshape(flat), both, split_axis=0, concat_axis=0, tiled=True)
 

time: 85.5 us -> 81.8 us (0.957)
  Pallas kernels: 62.2 us -> 58.5 us
    pallas_call x1, Pallas kernels: 17.3 us -> 14.5 us  [shards(): pl.pallas_call(functools.partial(inverse_kernel, sz, sums), in_specs=[sme...]
    pallas_call x1, Pallas kernels: 5.64 us -> 4.51 us  [shards(): pl.pallas_call(functools.partial(basis_kernel, sz), in_specs=[smem()], ou...]
  transfers between devices with their start and end apart: 4 -> 4, of which waited for: 2 -> 2; matrix products, arithmetic and copies ran while one was open for 2% -> 2% of each run, Pallas kernels for 27% -> 16%
where the time goes in v11:
time: 81.8 us; the launch traced here: 81.4 us
  Pallas kernels  58.5 us (72%)
  starting transfers between devices  12.2 us (15%)
  waiting for transfers between devices  7.64 us (9%)
  local copies, waits for them, and re-layouts  2.9 us (4%)
    pallas_call x1, Pallas kernels, shards(): pl.pallas_call(functools.partial(forward_kernel, sz), in_specs=[smem(), s...  22.1 us
    pallas_call x1, Pallas kernels, shards(): pl.pallas_call(functools.partial(inverse_kernel, sz, sums), in_specs=[sme...  14.5 us
    pallas_call x1, Pallas kernels, shards(): pl.pallas_call(functools.partial(zeros_kernel, sz), in_specs=[smem()], ou...  8.88 us
    pallas_call x1, Pallas kernels, shards(): pl.pallas_call(functools.partial(grid_kernel, sz), in_specs=[smem(), smem...  8.56 us
    all_to_all x1, starting transfers between devices, shards(): lax.all_to_all(sent.reshape(flat), both, split_axis=0, concat_axis=0, til...  7.31 us
    all_to_all x1, waiting for transfers between devices, shards(): lax.all_to_all(sent.reshape(flat), both, split_axis=0, concat_axis=0, til...  4.53 us
    pallas_call x1, Pallas kernels, shards(): pl.pallas_call(functools.partial(basis_kernel, sz), in_specs=[smem()], ou...  4.51 us
    all_to_all x1, starting transfers between devices, shards(): lax.all_to_all(returned.reshape(flat), both, split_axis=0, concat_axis=0,...  3.51 us
  transfers between devices with their start and end apart: 4, of which 2 were waited for; matrix products, arithmetic and copies ran while one was open for 2% of the time, Pallas kernels for 16%

profile of v11, /device:TPU:0, one launch (start us, length us, event | category | flops | bytes accessed | tf_op | source)
XLA Modules:
  0.0 81.4 jit_solution(15303561027908632502)
XLA Ops:
  0.0 0.0 copy-start.4
  0.0 14.5 %inverse_legendre.1 = (bf16[8,4,40,128]{3,2,1,0:T(8,128)(2,1)}, bf16[8,160,128]{2,1,0:T(8,128)(2,1)}) custom-call(s32[1280]{0:T(1024)} %wave.4, s32[16]{0:T(128)} %points.4, f32[16]{0:T(128)} %gauss.3, f32[24]{0:T(128)} %layer_depth.1, bf16[160,30,10,2,128]{4,3,2,1,0:T(2,128)(2,1)} %bitcast.16, bf16[160,16,1280]{2,1,0:T(8,128)(2,1)} %bitcast.18), custom_call_target="tpu_custom_call" | custom-call | tf_op jit(solution)/shard_map/inverse_legendre/pallas_call | solution.py:696
  14.5 7.3 %all-to-all-start = ((bf16[32,40,128]{2,1,0:T(8,128)(2,1)}), bf16[32,40,128]{2,1,0:T(8,128)(2,1)S(1)}, u32[]{:S(2)}, u32[]{:S(2)}) async-start(bf16[32,40,128]{2,1,0:T(8,128)(2,1)} %bitcast.23), calls=%async_computation | async-start | bytes 655360 | tf_op jit(solution)/shard_map/all_to_all | solution.py:711
  21.8 0.7 collective-permute-start.1
  22.5 0.7 collective-permute-start
  23.2 0.0 copy-done.4
  23.2 0.3 reshape.28
  23.5 0.3 slice_reduce_fusion
  23.8 0.1 squeeze.8
  23.9 0.1 squeeze.7
  24.0 0.7 reshape_reshape.3.even_row
  24.7 4.5 %basis.1.basis_hbm = bf16[4,640,1408]{2,1,0:T(8,128)(2,1)} custom-call(s32[16]{0:T(128)} %points.4), custom_call_target="tpu_custom_call" | custom-call | flops 18022400 | bytes 7208960 | tf_op jit(solution)/shard_map/basis/pallas_call | solution.py:721
  29.2 0.0 collective-permute-done.1.refs_1_
  29.2 0.0 copy-start.2
  29.2 0.0 collective-permute-done.refs_0_
  29.3 0.0 copy-start.3
  29.3 4.5 %all-to-all-done = bf16[32,40,128]{2,1,0:T(8,128)(2,1)S(1)} async-done(((bf16[32,40,128]{2,1,0:T(8,128)(2,1)}), bf16[32,40,128]{2,1,0:T(8,128)(2,1)S(1)}, u32[]{:S(2)}, u32[]{:S(2)}) %all-to-all-start) | async-done | bytes 327712 | tf_op jit(solution)/shard_map/all_to_all | solution.py:711
  33.8 0.0 copy-start.1
  33.8 0.7 copy-done.1
  34.5 8.6 %grid_products.1 = bf16[8,4,40,128]{3,2,1,0:T(8,128)(2,1)} custom-call(s32[16]{0:T(128)} %points.4, f32[16]{0:T(128)} %gauss.3, bf16[8,4,40,128]{3,2,1,0:T(8,128)(2,1)} %bitcast.21, s32[1,640]{1,0:T(1,128)} %reshape_reshape.3.even_row, bf16[4,640,1408]{2,1,0:T(8,128)(2,1)} %basis.1.basis_hbm), custom_call_target="tpu_custom_call" | custom-call | flops 1845493760 | bytes 7208960 | tf_op jit(solution)/shard_map/grid_products/pallas_call | solution.py:742
  43.1 3.5 %all-to-all-start.1 = ((bf16[32,40,128]{2,1,0:T(8,128)(2,1)}), bf16[32,40,128]{2,1,0:T(8,128)(2,1)S(1)}, u32[]{:S(2)}, u32[]{:S(2)}) async-start(bf16[32,40,128]{2,1,0:T(8,128)(2,1)} %bitcast.22), calls=%async_computation.1 | async-start | bytes 655360 | tf_op jit(solution)/shard_map/all_to_all | solution.py:762
  46.6 8.9 %dead_zeros.1.refs_4_ = f32[160,30,10,2,128]{4,3,2,1,0:T(2,128)} custom-call(s32[1280]{0:T(1024)} %wave.4), custom_call_target="tpu_custom_call" | custom-call | bytes 24576000 | tf_op jit(solution)/shard_map/dead_zeros/pallas_call | solution.py:765
  55.5 3.1 %all-to-all-done.1 = bf16[32,40,128]{2,1,0:T(8,128)(2,1)S(1)} async-done(((bf16[32,40,128]{2,1,0:T(8,128)(2,1)}), bf16[32,40,128]{2,1,0:T(8,128)(2,1)S(1)}, u32[]{:S(2)}, u32[]{:S(2)}) %all-to-all-start.1) | async-done | bytes 327712 | tf_op jit(solution)/shard_map/all_to_all | solution.py:762
  58.6 0.0 copy-start
  58.6 0.0 copy-done.2
  58.6 0.0 copy-done.3
  58.6 0.7 copy-done
  59.3 22.1 %forward_legendre.1 = f32[160,30,10,2,128]{4,3,2,1,0:T(2,128)} custom-call(s32[1280]{0:T(1024)} %wave.4, f32[30]{0:T(128)} %speed.1, bf16[8,4,40,128]{3,2,1,0:T(8,128)(2,1)} %bitcast.20, bf16[8,160,128]{2,1,0:T(8,128)(2,1)} %copy-done.3, bf16[8,160,128]{2,1,0:T(8,128)(2,1)} %copy-done.2, ...), custom_call_target="tpu_custom_call", output_to_operand_aliasing={{}: (7, {})} | custom-call | tf_op jit(solution)/shard_map/forward_legendre/pallas_call | solution.py:780
  (2 shorter events, 0.0 us)
Async XLA Ops:
  0.0 23.2 %copy-start.4 = (s32[1280]{0:T(1024)S(1)}, s32[1280]{0:T(1024)}, u32[]{:S(2)}) copy-start(s32[1280]{0:T(1024)} %wave.4) | copy-start | bytes 15364
  14.5 19.3 %all-to-all-start = ((bf16[32,40,128]{2,1,0:T(8,128)(2,1)}), bf16[32,40,128]{2,1,0:T(8,128)(2,1)S(1)}, u32[]{:S(2)}, u32[]{:S(2)}) async-start(bf16[32,40,128]{2,1,0:T(8,128)(2,1)} %bitcast.23), calls=%async_computation | async-start | bytes 655360 | tf_op jit(solution)/shard_map/all_to_all | solution.py:711
  21.8 7.4 %collective-permute-start.1 = (bf16[8,160,128]{2,1,0:T(8,128)(2,1)}, bf16[8,160,128]{2,1,0:T(8,128)(2,1)S(1)}, u32[]{:S(2)}, u32[]{:S(2)}) collective-permute-start(bf16[8,160,128]{2,1,0:T(8,128)(2,1)} %get-tuple-element.17), channel_id=1, source_target_pairs={{2,3},{6,7},{10,11},{14,15},{18,19},{22,23},{26,27},{30,31}} | collective-permute-start | bytes 983048 | tf_op jit(solution)/shard_map/ppermute | solution.py:740
  22.5 6.8 %collective-permute-start = (bf16[8,160,128]{2,1,0:T(8,128)(2,1)}, bf16[8,160,128]{2,1,0:T(8,128)(2,1)S(1)}, u32[]{:S(2)}, u32[]{:S(2)}) collective-permute-start(bf16[8,160,128]{2,1,0:T(8,128)(2,1)} %get-tuple-element.17), channel_id=1, source_target_pairs={{1,3},{5,7},{9,11},{13,15},{17,19},{21,23},{25,27},{29,31}} | collective-permute-start | bytes 983048 | tf_op jit(solution)/shard_map/ppermute | solution.py:740
  29.2 29.4 %copy-start.2 = (bf16[8,160,128]{2,1,0:T(8,128)(2,1)}, bf16[8,160,128]{2,1,0:T(8,128)(2,1)S(1)}, u32[]{:S(2)}) copy-start(bf16[8,160,128]{2,1,0:T(8,128)(2,1)S(1)} %collective-permute-done.1.refs_1_) | copy-start | bytes 983044
  29.3 29.3 %copy-start.3 = (bf16[8,160,128]{2,1,0:T(8,128)(2,1)}, bf16[8,160,128]{2,1,0:T(8,128)(2,1)S(1)}, u32[]{:S(2)}) copy-start(bf16[8,160,128]{2,1,0:T(8,128)(2,1)S(1)} %collective-permute-done.refs_0_) | copy-start | bytes 983044
  33.8 0.7 copy-start.1
  43.1 15.5 %all-to-all-start.1 = ((bf16[32,40,128]{2,1,0:T(8,128)(2,1)}), bf16[32,40,128]{2,1,0:T(8,128)(2,1)S(1)}, u32[]{:S(2)}, u32[]{:S(2)}) async-start(bf16[32,40,128]{2,1,0:T(8,128)(2,1)} %bitcast.22), calls=%async_computation.1 | async-start | bytes 655360 | tf_op jit(solution)/shard_map/all_to_all | solution.py:762
  58.6 0.7 copy-start

commit v12 on v11

--- a/solution.py
+++ b/solution.py
@@ -262,14 +262,16 @@
     def block(step, carry):
         stream.take(step)
         found = []
-        for k in range(sz.block // 2):
-            place = step * (sz.block // 2) + k
+        each = sz.block // 2
+        empty = jnp.zeros((sz.rows, SLAB - pad), jnp.float32)
+
+        def unpack(k):
             for f in range(sz.fields):
-                rows = x_all[place, f].astype(jnp.float32)
+                rows = x_all[step * each + k, f].astype(jnp.float32)
                 wide[k, pl.ds(f * sz.stride, sz.pitch), :] = rows[0:sz.pitch]
-        empty = jnp.zeros((sz.rows, SLAB - pad), jnp.float32)
-        for k in range(sz.block // 2):
-            place = step * (sz.block // 2) + k
+
+        def multiply(k):
+            place = step * each + k
             pair = pair_at(place)
             values = jnp.concatenate([
                 jnp.concatenate([
@@ -281,6 +283,12 @@
             for side in range(2):
                 own = total[side * sz.rows:(side + 1) * sz.rows]
                 found.append((pair, side, jnp.concatenate([own, empty], axis=1)))
+
+        unpack(0)
+        for k in range(each):
+            if k + 1 < each:
+                unpack(k + 1)
+            multiply(k)
         for pair, side, total in found:
             spots[pair.rows(side), :] = total
             number = jnp.full((1, SLAB), pair.numbers[side], jnp.int32)
@@ -612,16 +620,18 @@
 
     def block(step, carry):
         stream.take(step)
-        work = []
-        for k in range(each):
-            place = step * each + k
-            pair = pair_at(place)
+
+        @pl.when(step >= BEHIND)
+        def _():
+            left(step)
+
+        at = lax.rem(step, BEHIND)
+
+        def products(k):
+            pair = pair_at(step * each + k)
             values = jnp.concatenate([spots[pair.rows(side), :] for side in range(2)], axis=0)
             values = values.T.astype(jnp.bfloat16)[0:pad]
-            work.append((place, pair, values, pair.tables(leg_all[place])))
-
-        for k in range(each):
-            _, _, values, tables = work[k]
+            tables = pair.tables(leg_all[step * each + k])
             for first in range(0, sz.packed, 2):
                 count = min(2, sz.packed - first)
                 tends = dot(values, tables[:, first * SLAB:(first + count) * SLAB])
@@ -632,13 +642,9 @@
                             c * sz.field_pad:(c + 1) * sz.field_pad, (t - first) * SLAB:(t - first + 1) * SLAB
                         ]
 
-        @pl.when(step >= BEHIND)
-        def _():
-            left(step)
-
-        at = lax.rem(step, BEHIND)
-        for k in range(each):
-            place, pair, _, _ = work[k]
+        def finish(k):
+            place = step * each + k
+            pair = pair_at(place)
             mine = row < pair.split
             degree = jnp.where(mine, row + pair.start, row - 1) * SLAB + lane
             floors = [jnp.where(n < 0, sz.degrees, n) for n in pair.numbers]
@@ -649,7 +655,12 @@
                 tend = wide[k, pl.ds(f * sz.stride, sz.pitch), :]
                 new = (old + time_step * tend) * inverse[pair.start, rows, :]
                 out_all[at, k, rows, :] = jnp.where(live, new, 0.0)
+
+        products(0)
         for k in range(each):
+            if k + 1 < each:
+                products(k + 1)
+            finish(k)
             leave(step * each + k, k)
         return carry
 

time: 81.8 us -> 79.4 us (0.971)
  Pallas kernels: 58.5 us -> 56.1 us
    pallas_call x1, Pallas kernels: 22.1 us -> 19.6 us  [shards(): pl.pallas_call(functools.partial(forward_kernel, sz), in_specs=[smem(), s...]
  transfers between devices with their start and end apart: 4 -> 4, of which waited for: 2 -> 2; matrix products, arithmetic and copies ran while one was open for 2% -> 2% of each run, Pallas kernels for 16% -> 17%
where the time goes in v12:
time: 79.4 us; the launch traced here: 78.9 us
  Pallas kernels  56.1 us (71%)
  starting transfers between devices  12.2 us (15%)
  waiting for transfers between devices  7.62 us (10%)
  local copies, waits for them, and re-layouts  2.9 us (4%)
    pallas_call x1, Pallas kernels, shards(): pl.pallas_call(functools.partial(forward_kernel, sz), in_specs=[smem(), s...  19.6 us
    pallas_call x1, Pallas kernels, shards(): pl.pallas_call(functools.partial(inverse_kernel, sz, sums), in_specs=[sme...  14.5 us
    pallas_call x1, Pallas kernels, shards(): pl.pallas_call(functools.partial(zeros_kernel, sz), in_specs=[smem()], ou...  8.9 us
    pallas_call x1, Pallas kernels, shards(): pl.pallas_call(functools.partial(grid_kernel, sz), in_specs=[smem(), smem...  8.55 us
    all_to_all x1, starting transfers between devices, shards(): lax.all_to_all(sent.reshape(flat), both, split_axis=0, concat_axis=0, til...  7.29 us
    all_to_all x1, waiting for transfers between devices, shards(): lax.all_to_all(sent.reshape(flat), both, split_axis=0, concat_axis=0, til...  4.53 us
    pallas_call x1, Pallas kernels, shards(): pl.pallas_call(functools.partial(basis_kernel, sz), in_specs=[smem()], ou...  4.51 us
    all_to_all x1, starting transfers between devices, shards(): lax.all_to_all(returned.reshape(flat), both, split_axis=0, concat_axis=0,...  3.53 us
  transfers between devices with their start and end apart: 4, of which 2 were waited for; matrix products, arithmetic and copies ran while one was open for 2% of the time, Pallas kernels for 17%

profile of v12, /device:TPU:0, one launch (start us, length us, event | category | flops | bytes accessed | tf_op | source)
XLA Modules:
  0.0 78.9 jit_solution(17533726565977711965)
XLA Ops:
  0.0 0.0 copy-start.4
  0.0 14.5 %inverse_legendre.1 = (bf16[8,4,40,128]{3,2,1,0:T(8,128)(2,1)}, bf16[8,160,128]{2,1,0:T(8,128)(2,1)}) custom-call(s32[1280]{0:T(1024)} %wave.4, s32[16]{0:T(128)} %points.4, f32[16]{0:T(128)} %gauss.3, f32[24]{0:T(128)} %layer_depth.1, bf16[160,30,10,2,128]{4,3,2,1,0:T(2,128)(2,1)} %bitcast.16, bf16[160,16,1280]{2,1,0:T(8,128)(2,1)} %bitcast.18), custom_call_target="tpu_custom_call" | custom-call | tf_op jit(solution)/shard_map/inverse_legendre/pallas_call | solution.py:707
  14.5 7.3 %all-to-all-start = ((bf16[32,40,128]{2,1,0:T(8,128)(2,1)}), bf16[32,40,128]{2,1,0:T(8,128)(2,1)S(1)}, u32[]{:S(2)}, u32[]{:S(2)}) async-start(bf16[32,40,128]{2,1,0:T(8,128)(2,1)} %bitcast.23), calls=%async_computation | async-start | bytes 655360 | tf_op jit(solution)/shard_map/all_to_all | solution.py:722
  21.8 0.7 collective-permute-start.1
  22.5 0.7 collective-permute-start
  23.2 0.0 copy-done.4
  23.2 0.3 reshape.28
  23.5 0.3 slice_reduce_fusion
  23.8 0.1 squeeze.8
  23.9 0.1 squeeze.7
  24.0 0.7 reshape_reshape.3.even_row
  24.7 4.5 %basis.1.basis_hbm = bf16[4,640,1408]{2,1,0:T(8,128)(2,1)} custom-call(s32[16]{0:T(128)} %points.4), custom_call_target="tpu_custom_call" | custom-call | flops 18022400 | bytes 7208960 | tf_op jit(solution)/shard_map/basis/pallas_call | solution.py:732
  29.2 0.0 collective-permute-done.1.refs_1_
  29.2 0.0 copy-start.2
  29.3 0.0 collective-permute-done.refs_0_
  29.3 0.0 copy-start.3
  29.3 4.5 %all-to-all-done = bf16[32,40,128]{2,1,0:T(8,128)(2,1)S(1)} async-done(((bf16[32,40,128]{2,1,0:T(8,128)(2,1)}), bf16[32,40,128]{2,1,0:T(8,128)(2,1)S(1)}, u32[]{:S(2)}, u32[]{:S(2)}) %all-to-all-start) | async-done | bytes 327712 | tf_op jit(solution)/shard_map/all_to_all | solution.py:722
  33.8 0.0 copy-start.1
  33.8 0.7 copy-done.1
  34.5 8.6 %grid_products.1 = bf16[8,4,40,128]{3,2,1,0:T(8,128)(2,1)} custom-call(s32[16]{0:T(128)} %points.4, f32[16]{0:T(128)} %gauss.3, bf16[8,4,40,128]{3,2,1,0:T(8,128)(2,1)} %bitcast.21, s32[1,640]{1,0:T(1,128)} %reshape_reshape.3.even_row, bf16[4,640,1408]{2,1,0:T(8,128)(2,1)} %basis.1.basis_hbm), custom_call_target="tpu_custom_call" | custom-call | flops 1845493760 | bytes 7208960 | tf_op jit(solution)/shard_map/grid_products/pallas_call | solution.py:753
  43.1 3.5 %all-to-all-start.1 = ((bf16[32,40,128]{2,1,0:T(8,128)(2,1)}), bf16[32,40,128]{2,1,0:T(8,128)(2,1)S(1)}, u32[]{:S(2)}, u32[]{:S(2)}) async-start(bf16[32,40,128]{2,1,0:T(8,128)(2,1)} %bitcast.22), calls=%async_computation.1 | async-start | bytes 655360 | tf_op jit(solution)/shard_map/all_to_all | solution.py:773
  46.6 8.9 %dead_zeros.1.refs_4_ = f32[160,30,10,2,128]{4,3,2,1,0:T(2,128)} custom-call(s32[1280]{0:T(1024)} %wave.4), custom_call_target="tpu_custom_call" | custom-call | bytes 24576000 | tf_op jit(solution)/shard_map/dead_zeros/pallas_call | solution.py:776
  55.5 3.1 %all-to-all-done.1 = bf16[32,40,128]{2,1,0:T(8,128)(2,1)S(1)} async-done(((bf16[32,40,128]{2,1,0:T(8,128)(2,1)}), bf16[32,40,128]{2,1,0:T(8,128)(2,1)S(1)}, u32[]{:S(2)}, u32[]{:S(2)}) %all-to-all-start.1) | async-done | bytes 327712 | tf_op jit(solution)/shard_map/all_to_all | solution.py:773
  58.6 0.0 copy-start
  58.6 0.0 copy-done.2
  58.6 0.0 copy-done.3
  58.6 0.7 copy-done
  59.3 19.6 %forward_legendre.1 = f32[160,30,10,2,128]{4,3,2,1,0:T(2,128)} custom-call(s32[1280]{0:T(1024)} %wave.4, f32[30]{0:T(128)} %speed.1, bf16[8,4,40,128]{3,2,1,0:T(8,128)(2,1)} %bitcast.20, bf16[8,160,128]{2,1,0:T(8,128)(2,1)} %copy-done.3, bf16[8,160,128]{2,1,0:T(8,128)(2,1)} %copy-done.2, ...), custom_call_target="tpu_custom_call", output_to_operand_aliasing={{}: (7, {})} | custom-call | tf_op jit(solution)/shard_map/forward_legendre/pallas_call | solution.py:791
  (2 shorter events, 0.0 us)
Async XLA Ops:
  0.0 23.2 %copy-start.4 = (s32[1280]{0:T(1024)S(1)}, s32[1280]{0:T(1024)}, u32[]{:S(2)}) copy-start(s32[1280]{0:T(1024)} %wave.4) | copy-start | bytes 15364
  14.5 19.3 %all-to-all-start = ((bf16[32,40,128]{2,1,0:T(8,128)(2,1)}), bf16[32,40,128]{2,1,0:T(8,128)(2,1)S(1)}, u32[]{:S(2)}, u32[]{:S(2)}) async-start(bf16[32,40,128]{2,1,0:T(8,128)(2,1)} %bitcast.23), calls=%async_computation | async-start | bytes 655360 | tf_op jit(solution)/shard_map/all_to_all | solution.py:722
  21.8 7.4 %collective-permute-start.1 = (bf16[8,160,128]{2,1,0:T(8,128)(2,1)}, bf16[8,160,128]{2,1,0:T(8,128)(2,1)S(1)}, u32[]{:S(2)}, u32[]{:S(2)}) collective-permute-start(bf16[8,160,128]{2,1,0:T(8,128)(2,1)} %get-tuple-element.17), channel_id=1, source_target_pairs={{2,3},{6,7},{10,11},{14,15},{18,19},{22,23},{26,27},{30,31}} | collective-permute-start | bytes 983048 | tf_op jit(solution)/shard_map/ppermute | solution.py:751
  22.5 6.8 %collective-permute-start = (bf16[8,160,128]{2,1,0:T(8,128)(2,1)}, bf16[8,160,128]{2,1,0:T(8,128)(2,1)S(1)}, u32[]{:S(2)}, u32[]{:S(2)}) collective-permute-start(bf16[8,160,128]{2,1,0:T(8,128)(2,1)} %get-tuple-element.17), channel_id=1, source_target_pairs={{1,3},{5,7},{9,11},{13,15},{17,19},{21,23},{25,27},{29,31}} | collective-permute-start | bytes 983048 | tf_op jit(solution)/shard_map/ppermute | solution.py:751
  29.2 29.4 %copy-start.2 = (bf16[8,160,128]{2,1,0:T(8,128)(2,1)}, bf16[8,160,128]{2,1,0:T(8,128)(2,1)S(1)}, u32[]{:S(2)}) copy-start(bf16[8,160,128]{2,1,0:T(8,128)(2,1)S(1)} %collective-permute-done.1.refs_1_) | copy-start | bytes 983044
  29.3 29.3 %copy-start.3 = (bf16[8,160,128]{2,1,0:T(8,128)(2,1)}, bf16[8,160,128]{2,1,0:T(8,128)(2,1)S(1)}, u32[]{:S(2)}) copy-start(bf16[8,160,128]{2,1,0:T(8,128)(2,1)S(1)} %collective-permute-done.refs_0_) | copy-start | bytes 983044
  33.8 0.7 copy-start.1
  43.1 15.5 %all-to-all-start.1 = ((bf16[32,40,128]{2,1,0:T(8,128)(2,1)}), bf16[32,40,128]{2,1,0:T(8,128)(2,1)S(1)}, u32[]{:S(2)}, u32[]{:S(2)}) async-start(bf16[32,40,128]{2,1,0:T(8,128)(2,1)} %bitcast.22), calls=%async_computation.1 | async-start | bytes 655360 | tf_op jit(solution)/shard_map/all_to_all | solution.py:773
  58.6 0.7 copy-start

commit v13 on v12

--- a/solution.py
+++ b/solution.py
@@ -230,19 +230,26 @@
         lax.fori_loop(first, last, one, 0)
         self.ahead = (turn + 1) * AHEAD
 
-    def take(self, step):
+    def arrive(self, place):
+        await_tiles(self.x_hbm, self.x_sems.at[place])
+        here = self.leg_all.at[place]
+        pltpu.make_async_copy(here, here, self.leg_sems.at[place]).wait()
+
+    def run(self, body):
         each = self.sizes.block // 2
-
-        @pl.when(step + self.ahead < self.sizes.steps)
-        def _():
-            for k in range(each):
-                self.start((step + self.ahead) * each + k)
-
-        for k in range(each):
-            place = step * each + k
-            await_tiles(self.x_hbm, self.x_sems.at[place])
-            here = self.leg_all.at[place]
-            pltpu.make_async_copy(here, here, self.leg_sems.at[place]).wait()
+        steps = self.sizes.steps
+        middle = max(steps - self.ahead, 0)
+
+        def feeding(step, carry):
+            body(step, lambda k: self.start((step + self.ahead) * each + k))
+            return carry
+
+        def last(step, carry):
+            body(step, lambda k: None)
+            return carry
+
+        lax.fori_loop(0, middle, feeding, 0)
+        lax.fori_loop(middle, steps, last, 0)
 
 
 def inverse_kernel(sizes, rounds, wave, points, gauss, layer_depth, x_hbm, leg_hbm, send_ref, *refs):
@@ -259,13 +266,14 @@
     numbers[...] = jnp.full_like(numbers, -1)
     wide[...] = jnp.zeros_like(wide)
 
-    def block(step, carry):
-        stream.take(step)
+    def block(step, feed):
         found = []
         each = sz.block // 2
         empty = jnp.zeros((sz.rows, SLAB - pad), jnp.float32)
 
         def unpack(k):
+            stream.arrive(step * each + k)
+            feed(k)
             for f in range(sz.fields):
                 rows = x_all[step * each + k, f].astype(jnp.float32)
                 wide[k, pl.ds(f * sz.stride, sz.pitch), :] = rows[0:sz.pitch]
@@ -293,9 +301,8 @@
             spots[pair.rows(side), :] = total
             number = jnp.full((1, SLAB), pair.numbers[side], jnp.int32)
             numbers[pl.ds(pair.spot(side), 1), :] = number
-        return carry
-
-    lax.fori_loop(0, sz.steps, block, 0)
+
+    stream.run(block)
     spread = spread_matrix(sz, lev)
     shape = (2 * pad, SLAB)
     src, dst = iota(shape, 0), iota(shape, 1)
@@ -618,9 +625,7 @@
         for k in range(each):
             await_tiles(out_hbm, out_sems.at[at, k])
 
-    def block(step, carry):
-        stream.take(step)
-
+    def block(step, feed):
         @pl.when(step >= BEHIND)
         def _():
             left(step)
@@ -628,6 +633,8 @@
         at = lax.rem(step, BEHIND)
 
         def products(k):
+            stream.arrive(step * each + k)
+            feed(k)
             pair = pair_at(step * each + k)
             values = jnp.concatenate([spots[pair.rows(side), :] for side in range(2)], axis=0)
             values = values.T.astype(jnp.bfloat16)[0:pad]
@@ -662,9 +669,8 @@
                 products(k + 1)
             finish(k)
             leave(step * each + k, k)
-        return carry
-
-    lax.fori_loop(0, sz.steps, block, 0)
+
+    stream.run(block)
     for step in range(max(0, sz.steps - BEHIND), sz.steps):
         left(jnp.int32(step))
 

time: 79.4 us -> 93 us (1.17)
  Pallas kernels: 56.1 us -> 69.6 us
    pallas_call x1, Pallas kernels: 19.6 us -> 28.1 us  [shards(): pl.pallas_call(functools.partial(forward_kernel, sz), in_specs=[smem(), s...]
    pallas_call x1, Pallas kernels: 14.5 us -> 19.5 us  [shards(): pl.pallas_call(functools.partial(inverse_kernel, sz, sums), in_specs=[sme...]
  transfers between devices with their start and end apart: 4 -> 4, of which waited for: 2 -> 2; matrix products, arithmetic and copies ran while one was open for 2% -> 2% of each run, Pallas kernels for 17% -> 14%
where the time goes in v13:
time: 93 us; the launch traced here: 92.6 us
  Pallas kernels  69.6 us (75%)
  starting transfers between devices  12.4 us (13%)
  waiting for transfers between devices  7.45 us (8%)
  local copies, waits for them, and re-layouts  2.9 us (3%)
    pallas_call x1, Pallas kernels, shards(): pl.pallas_call(functools.partial(forward_kernel, sz), in_specs=[smem(), s...  28.1 us
    pallas_call x1, Pallas kernels, shards(): pl.pallas_call(functools.partial(inverse_kernel, sz, sums), in_specs=[sme...  19.5 us
    pallas_call x1, Pallas kernels, shards(): pl.pallas_call(functools.partial(zeros_kernel, sz), in_specs=[smem()], ou...  8.89 us
    pallas_call x1, Pallas kernels, shards(): pl.pallas_call(functools.partial(grid_kernel, sz), in_specs=[smem(), smem...  8.55 us
    all_to_all x1, starting transfers between devices, shards(): lax.all_to_all(sent.reshape(flat), both, split_axis=0, concat_axis=0, til...  7.28 us
    all_to_all x1, waiting for transfers between devices, shards(): lax.all_to_all(sent.reshape(flat), both, split_axis=0, concat_axis=0, til...  4.53 us
    pallas_call x1, Pallas kernels, shards(): pl.pallas_call(functools.partial(basis_kernel, sz), in_specs=[smem()], ou...  4.51 us
    all_to_all x1, starting transfers between devices, shards(): lax.all_to_all(returned.reshape(flat), both, split_axis=0, concat_axis=0,...  3.72 us
  transfers between devices with their start and end apart: 4, of which 2 were waited for; matrix products, arithmetic and copies ran while one was open for 2% of the time, Pallas kernels for 14%

profile of v13, /device:TPU:0, one launch (start us, length us, event | category | flops | bytes accessed | tf_op | source)
XLA Modules:
  0.0 92.6 jit_solution(13725547785084124089)
XLA Ops:
  0.0 0.0 copy-start.4
  0.0 19.5 %inverse_legendre.1 = (bf16[8,4,40,128]{3,2,1,0:T(8,128)(2,1)}, bf16[8,160,128]{2,1,0:T(8,128)(2,1)}) custom-call(s32[1280]{0:T(1024)} %wave.4, s32[16]{0:T(128)} %points.4, f32[16]{0:T(128)} %gauss.3, f32[24]{0:T(128)} %layer_depth.1, bf16[160,30,10,2,128]{4,3,2,1,0:T(2,128)(2,1)} %bitcast.16, bf16[160,16,1280]{2,1,0:T(8,128)(2,1)} %bitcast.18), custom_call_target="tpu_custom_call" | custom-call | tf_op jit(solution)/shard_map/inverse_legendre/pallas_call | solution.py:713
  19.5 7.3 %all-to-all-start = ((bf16[32,40,128]{2,1,0:T(8,128)(2,1)}), bf16[32,40,128]{2,1,0:T(8,128)(2,1)S(1)}, u32[]{:S(2)}, u32[]{:S(2)}) async-start(bf16[32,40,128]{2,1,0:T(8,128)(2,1)} %bitcast.23), calls=%async_computation | async-start | bytes 655360 | tf_op jit(solution)/shard_map/all_to_all | solution.py:728
  26.8 0.7 collective-permute-start.1
  27.5 0.7 collective-permute-start
  28.2 0.0 copy-done.4
  28.2 0.3 reshape.28
  28.5 0.3 slice_reduce_fusion
  28.8 0.1 squeeze.8
  28.9 0.1 squeeze.7
  29.0 0.7 reshape_reshape.3.even_row
  29.7 4.5 %basis.1.basis_hbm = bf16[4,640,1408]{2,1,0:T(8,128)(2,1)} custom-call(s32[16]{0:T(128)} %points.4), custom_call_target="tpu_custom_call" | custom-call | flops 18022400 | bytes 7208960 | tf_op jit(solution)/shard_map/basis/pallas_call | solution.py:738
  34.2 0.0 collective-permute-done.1.refs_1_
  34.2 0.0 copy-start.2
  34.3 0.0 collective-permute-done.refs_0_
  34.3 0.0 copy-start.3
  34.3 4.5 %all-to-all-done = bf16[32,40,128]{2,1,0:T(8,128)(2,1)S(1)} async-done(((bf16[32,40,128]{2,1,0:T(8,128)(2,1)}), bf16[32,40,128]{2,1,0:T(8,128)(2,1)S(1)}, u32[]{:S(2)}, u32[]{:S(2)}) %all-to-all-start) | async-done | bytes 327712 | tf_op jit(solution)/shard_map/all_to_all | solution.py:728
  38.8 0.0 copy-start.1
  38.8 0.7 copy-done.1
  39.5 8.6 %grid_products.1 = bf16[8,4,40,128]{3,2,1,0:T(8,128)(2,1)} custom-call(s32[16]{0:T(128)} %points.4, f32[16]{0:T(128)} %gauss.3, bf16[8,4,40,128]{3,2,1,0:T(8,128)(2,1)} %bitcast.21, s32[1,640]{1,0:T(1,128)} %reshape_reshape.3.even_row, bf16[4,640,1408]{2,1,0:T(8,128)(2,1)} %basis.1.basis_hbm), custom_call_target="tpu_custom_call" | custom-call | flops 1845493760 | bytes 7208960 | tf_op jit(solution)/shard_map/grid_products/pallas_call | solution.py:759
  48.1 3.7 %all-to-all-start.1 = ((bf16[32,40,128]{2,1,0:T(8,128)(2,1)}), bf16[32,40,128]{2,1,0:T(8,128)(2,1)S(1)}, u32[]{:S(2)}, u32[]{:S(2)}) async-start(bf16[32,40,128]{2,1,0:T(8,128)(2,1)} %bitcast.22), calls=%async_computation.1 | async-start | bytes 655360 | tf_op jit(solution)/shard_map/all_to_all | solution.py:779
  51.8 8.9 %dead_zeros.1.refs_4_ = f32[160,30,10,2,128]{4,3,2,1,0:T(2,128)} custom-call(s32[1280]{0:T(1024)} %wave.4), custom_call_target="tpu_custom_call" | custom-call | bytes 24576000 | tf_op jit(solution)/shard_map/dead_zeros/pallas_call | solution.py:782
  60.7 2.9 %all-to-all-done.1 = bf16[32,40,128]{2,1,0:T(8,128)(2,1)S(1)} async-done(((bf16[32,40,128]{2,1,0:T(8,128)(2,1)}), bf16[32,40,128]{2,1,0:T(8,128)(2,1)S(1)}, u32[]{:S(2)}, u32[]{:S(2)}) %all-to-all-start.1) | async-done | bytes 327712 | tf_op jit(solution)/shard_map/all_to_all | solution.py:779
  63.6 0.0 copy-start
  63.6 0.0 copy-done.2
  63.6 0.0 copy-done.3
  63.6 0.7 copy-done
  64.3 28.1 %forward_legendre.1 = f32[160,30,10,2,128]{4,3,2,1,0:T(2,128)} custom-call(s32[1280]{0:T(1024)} %wave.4, f32[30]{0:T(128)} %speed.1, bf16[8,4,40,128]{3,2,1,0:T(8,128)(2,1)} %bitcast.20, bf16[8,160,128]{2,1,0:T(8,128)(2,1)} %copy-done.3, bf16[8,160,128]{2,1,0:T(8,128)(2,1)} %copy-done.2, ...), custom_call_target="tpu_custom_call", output_to_operand_aliasing={{}: (7, {})} | custom-call | tf_op jit(solution)/shard_map/forward_legendre/pallas_call | solution.py:797
  (2 shorter events, 0.0 us)
Async XLA Ops:
  0.0 28.2 %copy-start.4 = (s32[1280]{0:T(1024)S(1)}, s32[1280]{0:T(1024)}, u32[]{:S(2)}) copy-start(s32[1280]{0:T(1024)} %wave.4) | copy-start | bytes 15364
  19.5 19.3 %all-to-all-start = ((bf16[32,40,128]{2,1,0:T(8,128)(2,1)}), bf16[32,40,128]{2,1,0:T(8,128)(2,1)S(1)}, u32[]{:S(2)}, u32[]{:S(2)}) async-start(bf16[32,40,128]{2,1,0:T(8,128)(2,1)} %bitcast.23), calls=%async_computation | async-start | bytes 655360 | tf_op jit(solution)/shard_map/all_to_all | solution.py:728
  26.8 7.4 %collective-permute-start.1 = (bf16[8,160,128]{2,1,0:T(8,128)(2,1)}, bf16[8,160,128]{2,1,0:T(8,128)(2,1)S(1)}, u32[]{:S(2)}, u32[]{:S(2)}) collective-permute-start(bf16[8,160,128]{2,1,0:T(8,128)(2,1)} %get-tuple-element.17), channel_id=1, source_target_pairs={{2,3},{6,7},{10,11},{14,15},{18,19},{22,23},{26,27},{30,31}} | collective-permute-start | bytes 983048 | tf_op jit(solution)/shard_map/ppermute | solution.py:757
  27.5 6.8 %collective-permute-start = (bf16[8,160,128]{2,1,0:T(8,128)(2,1)}, bf16[8,160,128]{2,1,0:T(8,128)(2,1)S(1)}, u32[]{:S(2)}, u32[]{:S(2)}) collective-permute-start(bf16[8,160,128]{2,1,0:T(8,128)(2,1)} %get-tuple-element.17), channel_id=1, source_target_pairs={{1,3},{5,7},{9,11},{13,15},{17,19},{21,23},{25,27},{29,31}} | collective-permute-start | bytes 983048 | tf_op jit(solution)/shard_map/ppermute | solution.py:757
  34.2 29.4 %copy-start.2 = (bf16[8,160,128]{2,1,0:T(8,128)(2,1)}, bf16[8,160,128]{2,1,0:T(8,128)(2,1)S(1)}, u32[]{:S(2)}) copy-start(bf16[8,160,128]{2,1,0:T(8,128)(2,1)S(1)} %collective-permute-done.1.refs_1_) | copy-start | bytes 983044
  34.3 29.4 %copy-start.3 = (bf16[8,160,128]{2,1,0:T(8,128)(2,1)}, bf16[8,160,128]{2,1,0:T(8,128)(2,1)S(1)}, u32[]{:S(2)}) copy-start(bf16[8,160,128]{2,1,0:T(8,128)(2,1)S(1)} %collective-permute-done.refs_0_) | copy-start | bytes 983044
  38.8 0.7 copy-start.1
  48.1 15.5 %all-to-all-start.1 = ((bf16[32,40,128]{2,1,0:T(8,128)(2,1)}), bf16[32,40,128]{2,1,0:T(8,128)(2,1)S(1)}, u32[]{:S(2)}, u32[]{:S(2)}) async-start(bf16[32,40,128]{2,1,0:T(8,128)(2,1)} %bitcast.22), calls=%async_computation.1 | async-start | bytes 655360 | tf_op jit(solution)/shard_map/all_to_all | solution.py:779
  63.6 0.7 copy-start
